TPU v7x, 32 devices: a whole 2x2x4 slice. The times are simulated.
32 devices in a mesh: batch: 2 (over y), hidden: 8 (over z, core), width: 2 (over x).
Axes of the slice: x: 2, y: 2, z: 4, core: 2. Of those that a mesh axis runs over, the one named last changes fastest.
Arguments:
- tokens: bfloat16 [8192, 512], P(('batch', 'hidden'), 'width'), may hold values from -6 to 6
- ln1_gain: float32 [512], P('width'), may hold values from 0.5 to 1.5
- ln1_bias: float32 [512], P('width'), may hold values from -1.5 to 1.5
- w_query: bfloat16 [512, 512], P(None, 'width'), may hold values from -0.25 to 0.25
- w_key: bfloat16 [512, 512], P(None, 'width'), may hold values from -0.25 to 0.25
- w_value: bfloat16 [512, 512], P(None, 'width'), may hold values from -0.25 to 0.25
- w_out: bfloat16 [512, 512], P('width'), may hold values from -2 to 2
- gate1_weight: bfloat16 [512, 512], P(None, 'width'), may hold values from -0.25 to 0.25
- gate1_bias: float32 [512], P('width'), may hold values from -2 to 2
- ln2_gain: float32 [512], P('width'), may hold values from 0.5 to 1.5
- ln2_bias: float32 [512], P('width'), may hold values from -1.5 to 1.5
- gate2_weight: bfloat16 [512, 512], P(None, 'width'), may hold values from -0.25 to 0.25
- gate2_bias: float32 [512], P('width'), may hold values from -2 to 2
- w_up: bfloat16 [512, 2048], P('width', 'hidden'), may hold values from -0.25 to 0.25
- w_down: bfloat16 [2048, 512], P('hidden', 'width'), may hold values from -0.25 to 0.25
- lengths: int32 [2, 3], P('batch'), may hold values from 1 to 4094, as said below
- cotangent: bfloat16 [8192, 512], P(('batch', 'hidden'), 'width'), may hold values from -6 to 6
Outputs:
- output: bfloat16 [8192, 512], P(('batch', 'hidden'), 'width')
- grad_tokens: float32 [8192, 512], P(('batch', 'hidden'), 'width')
- grad_ln1_gain: float32 [512], P('width')
- grad_ln1_bias: float32 [512], P('width')
- grad_w_query: float32 [512, 512], P(None, 'width')
- grad_w_key: float32 [512, 512], P(None, 'width')
- grad_w_value: float32 [512, 512], P(None, 'width')
- grad_w_out: float32 [512, 512], P('width')
- grad_gate1_weight: float32 [512, 512], P(None, 'width')
- grad_gate1_bias: float32 [512], P('width')
- grad_ln2_gain: float32 [512], P('width')
- grad_ln2_bias: float32 [512], P('width')
- grad_gate2_weight: float32 [512, 512], P(None, 'width')
- grad_gate2_bias: float32 [512], P('width')
- grad_w_up: float32 [512, 2048], P('width', 'hidden')
- grad_w_down: float32 [2048, 512], P('hidden', 'width')
Inputs may be any that keep to these rules, and one draw needn't show every extreme that they name: `lengths`: in every group, slot 1 starts at or before position 256 and ends within the last 256 positions; slot 0 holds 1 to 256 tokens, slot 2 holds 1 to 128, and at most 128 padding positions follow. In one group, drawn from the seed, slots 0 and 2 hold one token each and no padding follows.
All inputs are finite; a program needn't handle non-finite values.
Results may differ from a plain program's by a relative error of at most 0.014.
Values may be sent and summed in bfloat16 or wider, within the bound.
A program may use at most 192 MiB of HBM per device.

v0:
```python
import jax
import jax.numpy as jnp
from jax import lax
from jax.sharding import PartitionSpec as P

HEAD_DIM = 64


EPSILON = 1e-05


def layer_norm(values, gain, shift):
    centre = values - jnp.mean(values, -1, keepdims=True)
    spread = jnp.mean(centre * centre, -1, keepdims=True)
    return centre * lax.rsqrt(spread + EPSILON) * gain + shift


def matmul(left, right):
    return jnp.dot(left, right, preferred_element_type=jnp.float32)


def inner_rows(left, right):
    return lax.dot_general(
        left, right, (((0,), (0,)), ((), ())), preferred_element_type=jnp.float32
    )


def outer_cols(left, right):
    return lax.dot_general(
        left, right, (((1,), (1,)), ((), ())), preferred_element_type=jnp.float32
    )


def columns(values, gain, shift):
    return (
        lax.all_gather(values, "width", axis=1, tiled=True),
        lax.all_gather(gain[None, :], "width", axis=1, tiled=True),
        lax.all_gather(shift[None, :], "width", axis=1, tiled=True),
    )


def spread_rows(values):
    return lax.all_gather(values, "hidden", axis=0, tiled=True)


def width_total(partial_sum):
    return lax.psum(partial_sum, "width")


def unit_total(partial_sum):
    return lax.psum(partial_sum, "width")


def gelu_grad(pre_act, grad_hidden):
    _, gelu_back = jax.vjp(jax.nn.gelu, pre_act)
    return gelu_back(grad_hidden)[0].astype(jnp.bfloat16)


def local(
    tokens,
    ln1_gain,
    ln1_bias,
    w_query,
    w_key,
    w_value,
    w_out,
    gate1_weight,
    gate1_bias,
    ln2_gain,
    ln2_bias,
    gate2_weight,
    gate2_bias,
    w_up,
    w_down,
    lengths,
    cotangent,
):
    tok_rows, col_width = tokens.shape
    hidden_size = lax.axis_size("hidden")
    group_len = tok_rows * hidden_size
    hidden_pos = lax.axis_index("hidden")
    width_pos = lax.axis_index("width")
    head_count = col_width // HEAD_DIM
    scale = HEAD_DIM ** (-0.5)
    seq_ends = jnp.cumsum(lengths[0])
    key_pos = jnp.arange(group_len, dtype=jnp.int32)
    key_seg = jnp.sum((key_pos[:, None] >= seq_ends[None, :]).astype(jnp.int32), 1)
    query_pos = hidden_pos * tok_rows + jnp.arange(tok_rows, dtype=jnp.int32)
    query_seg = lax.dynamic_slice_in_dim(key_seg, hidden_pos * tok_rows, tok_rows, 0)
    allowed = (query_seg[:, None] == key_seg[None, :]) & (key_pos[None, :] <= query_pos[:, None])

    def own_cols(full):
        return lax.dynamic_slice_in_dim(full, width_pos * col_width, col_width, 1)

    def own_part(vector):
        return lax.dynamic_slice_in_dim(vector, width_pos * col_width, col_width, 0)

    def head_slice(matrix, index):
        return lax.dynamic_slice_in_dim(matrix, index * HEAD_DIM, HEAD_DIM, 1)

    resid_in = tokens.astype(jnp.float32)
    wide_in, gain_one, shift_one = columns(resid_in, ln1_gain, ln1_bias)
    normed_one = layer_norm(wide_in, gain_one[0], shift_one[0]).astype(jnp.bfloat16)
    queries = matmul(normed_one, w_query).astype(jnp.bfloat16)
    keys_own = matmul(normed_one, w_key).astype(jnp.bfloat16)
    values_own = matmul(normed_one, w_value).astype(jnp.bfloat16)
    keys_all, values_all = (
        lax.all_gather(keys_own, "hidden", axis=0, tiled=True),
        lax.all_gather(values_own, "hidden", axis=0, tiled=True),
    )

    def head_scores(index):
        scores = outer_cols(head_slice(queries, index), head_slice(keys_all, index)) * scale
        return jnp.where(allowed, scores, -1e30)

    def head_forward(index):
        scores = head_scores(index)
        top = jnp.max(scores, 1, keepdims=True)
        weights = jnp.exp(scores - top)
        total = jnp.sum(weights, 1, keepdims=True)
        probs = weights / total
        mixed = matmul(probs.astype(jnp.bfloat16), head_slice(values_all, index))
        return (mixed, top[:, 0] + jnp.log(total[:, 0]))

    head_out, log_total = lax.map(head_forward, jnp.arange(head_count, dtype=jnp.int32))
    attended = head_out.transpose(1, 0, 2).reshape(tok_rows, col_width).astype(jnp.bfloat16)
    branch_one = lax.psum_scatter(matmul(attended, w_out), "width", scatter_dimension=1, tiled=True)
    gate_one = jax.nn.sigmoid(matmul(normed_one, gate1_weight) + gate1_bias)
    middle = resid_in + gate_one * (branch_one - resid_in)
    wide_mid, gain_two, shift_two = columns(middle, ln2_gain, ln2_bias)
    normed_two = layer_norm(wide_mid, gain_two[0], shift_two[0]).astype(jnp.bfloat16)
    gate_two = jax.nn.sigmoid(matmul(normed_two, gate2_weight) + gate2_bias)
    up_full = lax.all_gather(w_up, "width", axis=0, tiled=True)
    rows_all = spread_rows(normed_two)
    pre_act = matmul(rows_all, up_full)
    hidden_act = jax.nn.gelu(pre_act).astype(jnp.bfloat16)
    branch_two = lax.psum_scatter(
        matmul(hidden_act, w_down), "hidden", scatter_dimension=0, tiled=True
    )
    result = middle + gate_two * (branch_two - middle)
    grad_out = cotangent.astype(jnp.float32)
    grad_branch_two = (grad_out * gate_two).astype(jnp.bfloat16)
    grad_logit_two = (grad_out * (branch_two - middle) * gate_two * (1.0 - gate_two)).astype(
        jnp.bfloat16
    )
    grad_middle = grad_out * (1.0 - gate_two)
    grad_rows = spread_rows(grad_branch_two)
    grad_down = inner_rows(hidden_act, grad_rows)
    grad_hidden = unit_total(outer_cols(grad_rows, w_down))
    grad_pre = gelu_grad(pre_act, grad_hidden)
    grad_up = inner_rows(own_cols(rows_all), grad_pre)
    grad_norm_ffn = lax.psum_scatter(
        outer_cols(grad_pre, up_full), "hidden", scatter_dimension=0, tiled=True
    )
    grad_norm_two = grad_norm_ffn + width_total(outer_cols(grad_logit_two, gate2_weight))
    _, norm_back_two = jax.vjp(layer_norm, wide_mid, gain_two[0], shift_two[0])
    grad_wide_mid, grad_gain_two, grad_shift_two = norm_back_two(grad_norm_two)
    grad_middle = grad_middle + own_cols(grad_wide_mid)
    grad_branch_one = (grad_middle * gate_one).astype(jnp.bfloat16)
    grad_logit_one = (grad_middle * (branch_one - resid_in) * gate_one * (1.0 - gate_one)).astype(
        jnp.bfloat16
    )
    grad_input = grad_middle * (1.0 - gate_one)
    grad_heads_all = lax.all_gather(grad_branch_one, "width", axis=1, tiled=True)
    grad_w_out = inner_rows(attended, grad_heads_all)
    grad_attended = outer_cols(grad_heads_all, w_out).astype(jnp.bfloat16)

    def query_side(index, log_sum):
        probs = jnp.exp(head_scores(index) - log_sum[:, None])
        grad_head = head_slice(grad_attended, index)
        grad_probs = outer_cols(grad_head, head_slice(values_all, index))
        centre = jnp.sum(probs * grad_probs, 1, keepdims=True)
        grad_scores = (probs * (grad_probs - centre)).astype(jnp.bfloat16)
        grad_query = matmul(grad_scores, head_slice(keys_all, index)) * scale
        return (probs, grad_head, centre[:, 0], grad_scores, grad_query)

    head_ids = jnp.arange(head_count, dtype=jnp.int32)

    def head_backward(inputs):
        index, log_sum = inputs
        probs, grad_head, _, grad_scores, grad_query = query_side(index, log_sum)
        grad_key = inner_rows(grad_scores, head_slice(queries, index)) * scale
        grad_value = inner_rows(probs.astype(jnp.bfloat16), grad_head)
        return (grad_query, grad_key, grad_value)

    query_parts, key_parts, value_parts = lax.map(head_backward, (head_ids, log_total))
    key_term = key_parts.transpose(1, 0, 2).reshape(group_len, col_width)
    value_term = value_parts.transpose(1, 0, 2).reshape(group_len, col_width)
    key_sums, value_sums = (
        lax.psum_scatter(
            key_term.astype(jnp.bfloat16), "hidden", scatter_dimension=0, tiled=True
        ).astype(jnp.float32),
        lax.psum_scatter(
            value_term.astype(jnp.bfloat16), "hidden", scatter_dimension=0, tiled=True
        ).astype(jnp.float32),
    )
    grad_keys = key_sums.astype(jnp.bfloat16)
    grad_values = value_sums.astype(jnp.bfloat16)
    grad_queries = query_parts.transpose(1, 0, 2).reshape(tok_rows, col_width).astype(jnp.bfloat16)
    grad_norm_one = width_total(
        outer_cols(grad_queries, w_query)
        + outer_cols(grad_keys, w_key)
        + outer_cols(grad_values, w_value)
        + outer_cols(grad_logit_one, gate1_weight)
    )
    _, norm_back_one = jax.vjp(layer_norm, wide_in, gain_one[0], shift_one[0])
    grad_wide_in, grad_gain_one, grad_shift_one = norm_back_one(grad_norm_one)
    grad_input = grad_input + own_cols(grad_wide_in)
    summed = lax.psum(
        (
            inner_rows(normed_one, grad_queries),
            inner_rows(normed_one, grad_keys),
            inner_rows(normed_one, grad_values),
            grad_w_out,
            inner_rows(normed_one, grad_logit_one),
            inner_rows(normed_two, grad_logit_two),
            jnp.sum(grad_logit_one.astype(jnp.float32), 0),
            jnp.sum(grad_logit_two.astype(jnp.float32), 0),
            own_part(grad_gain_one),
            own_part(grad_shift_one),
            own_part(grad_gain_two),
            own_part(grad_shift_two),
        ),
        ("batch", "hidden"),
    )
    ffn_summed = (
        lax.psum(grad_up.astype(jnp.bfloat16), "batch").astype(jnp.float32),
        lax.psum(grad_down.astype(jnp.bfloat16), "batch").astype(jnp.float32),
    )
    return (
        result.astype(jnp.bfloat16),
        grad_input,
        summed[8],
        summed[9],
        summed[0],
        summed[1],
        summed[2],
        summed[3],
        summed[4],
        summed[6],
        summed[10],
        summed[11],
        summed[5],
        summed[7],
        ffn_summed[0],
        ffn_summed[1],
    )


def solution(mesh):
    in_specs = (
        P(("batch", "hidden"), "width"),
        P("width"),
        P("width"),
        P(None, "width"),
        P(None, "width"),
        P(None, "width"),
        P("width", None),
        P(None, "width"),
        P("width"),
        P("width"),
        P("width"),
        P(None, "width"),
        P("width"),
        P("width", "hidden"),
        P("hidden", "width"),
        P("batch", None),
        P(("batch", "hidden"), "width"),
    )
    out_specs = (
        P(("batch", "hidden"), "width"),
        P(("batch", "hidden"), "width"),
        P("width"),
        P("width"),
        P(None, "width"),
        P(None, "width"),
        P(None, "width"),
        P("width", None),
        P(None, "width"),
        P("width"),
        P("width"),
        P("width"),
        P(None, "width"),
        P("width"),
        P("width", "hidden"),
        P("hidden", "width"),
    )
    return jax.shard_map(local, mesh=mesh, in_specs=in_specs, out_specs=out_specs, check_vma=False)
```

profile of v0, /device:TPU:0, one launch (start us, length us, event | category | flops | bytes accessed | tf_op | source)
XLA Modules:
  0.0 950.8 jit_solution(14766623988569431293)
XLA Ops:
  9.2 5.4 all-gather.4
  14.6 4.4 all-gather.5
  19.1 15.2 %all-gather.15.cloned.1.call-done = f32[512,512]{1,0:T(8,128)} async-done(((f32[512,256]{1,0:T(8,128)}), f32[512,512]{1,0:T(8,128)}) %all-gather.15.cloned.1.call-update) | async-done | bytes 1048592 | tf_op jit(solution)/shard_map/all_gather | solution.py:36
  42.8 26.7 %all-gather.19.cloned.1.call-done = bf16[4096,256]{1,0:T(8,128)(2,1)} async-done(((bf16[512,256]{1,0:T(8,128)(2,1)}), bf16[4096,256]{1,0:T(8,128)(2,1)}) %all-gather.19.cloned.1.call-update) | async-done | bytes 2097168 | tf_op jit(solution)/shard_map/all_gather | solution.py:109
  69.5 30.8 %all-gather.17.cloned.1.call-done = bf16[4096,256]{1,0:T(8,128)(2,1)} async-done(((bf16[512,256]{1,0:T(8,128)(2,1)}), bf16[4096,256]{1,0:T(8,128)(2,1)}) %all-gather.17.cloned.1.call-update) | async-done | bytes 2097168 | tf_op jit(solution)/shard_map/all_gather | solution.py:108
  100.3 35.8 %while.28 = (s32[]{:T(128)}, bf16[4,512,64]{1,2,0:T(8,128)(2,1)S(1)}, f32[4,512]{1,0:T(4,128)S(1)}, s32[4]{0:T(128)S(1)}, bf16[512,256]{1,0:T(8,128)(2,1)}, /*in...) while((s32[]{:T(128)}, ...), condition=%wide.region_7.8_spmd.clone, body=%wide.region_4.7_spmd.clone.sunk | while | flops 559939072 | bytes 35955948 | solution.py:125
  101.6 3.9 fusion.145
  107.1 2.1 fusion.147
  110.5 3.9 fusion.145
  116.0 2.1 fusion.147
  119.5 3.9 fusion.145
  125.0 2.1 fusion.147
  128.4 3.9 fusion.145
  133.9 2.1 fusion.147
  136.2 2.4 fusion.69
  138.6 19.9 %reduce-scatter.6.cloned.1.call-done = f32[512,256]{1,0:T(8,128)} async-done(((f32[512,512]{1,0:T(8,128)}), f32[512,256]{1,0:T(8,128)}) %reduce-scatter.6.cloned.1.call-update) | async-done | bytes 524304 | tf_op jit(solution)/shard_map/reduce_scatter | solution.py:127
  158.5 2.4 multiply_add_fusion
  161.0 4.2 all-gather.6
  165.3 4.2 all-gather.7
  169.5 12.9 %all-gather.21.cloned.1.call-done = f32[512,512]{1,0:T(8,128)} async-done(((f32[512,256]{1,0:T(8,128)}), f32[512,512]{1,0:T(8,128)}) %all-gather.21.cloned.1.call-update) | async-done | bytes 1048592 | tf_op jit(solution)/shard_map/all_gather | solution.py:36
  185.3 2.2 add_convert_fusion
  187.6 5.9 all_gather.45
  193.6 41.3 %all-gather.23.cloned.1.call-done = bf16[4096,512]{1,0:T(8,128)(2,1)} async-done(((bf16[512,512]{1,0:T(8,128)(2,1)}), bf16[4096,512]{1,0:T(8,128)(2,1)}) %all-gather.23.cloned.1.call-update) | async-done | bytes 4194320 | tf_op jit(solution)/shard_map/all_gather | solution.py:43
  234.9 3.4 fusion.70
  238.4 2.0 copy-done.7
  240.4 3.4 fusion.63
  244.1 48.6 %reduce-scatter.8.cloned.1.call-done = f32[512,256]{1,0:T(8,128)} async-done(((f32[4096,256]{1,0:T(8,128)}), f32[512,256]{1,0:T(8,128)}) %reduce-scatter.8.cloned.1.call-update) | async-done | bytes 524304 | tf_op jit(solution)/shard_map/reduce_scatter | solution.py:137
  292.7 2.5 convert_reduce_fusion
  296.6 26.1 %all-gather.25.cloned.1.call-done = bf16[4096,256]{1,0:T(8,128)(2,1)} async-done(((bf16[512,256]{1,0:T(8,128)(2,1)}), bf16[4096,256]{1,0:T(8,128)(2,1)}) %all-gather.25.cloned.1.call-update) | async-done | bytes 2097168 | tf_op jit(solution)/shard_map/all_gather | solution.py:43
  322.6 4.4 fusion.71
  327.1 130.5 %all-reduce.13.cloned.1.call-done = (f32[4096,256]{1,0:T(8,128)}, f32[512,512]{1,0:T(8,128)}) async-done(((f32[4096,256]{1,0:T(8,128)}, f32[512,512]{1,0:T(8,128)}), (f32[4096,256]{1,0:T(8,128)}, f32[512,512]{1,0:T(8,128)})) %all-reduce.13.cloned.1.call-update) | async-done | bytes 5242896 | tf_op jit(solution)/shard_map/psum | solution.py:51
  457.5 5.0 fusion.40
  463.9 4.6 fusion.72
  468.6 89.7 %reduce-scatter.10.cloned.1.call-done = f32[512,512]{1,0:T(8,128)} async-done(((f32[4096,512]{1,0:T(8,128)}), f32[512,512]{1,0:T(8,128)}) %reduce-scatter.10.cloned.1.call-update) | async-done | bytes 1048592 | tf_op jit(solution)/shard_map/reduce_scatter | solution.py:152
  560.5 2.5 convert_reduce_fusion.1
  563.1 7.0 all_gather.47
  572.0 113.1 %while.29 = (s32[]{:T(128)}, bf16[4,512,64]{1,2,0:T(8,128)(2,1)}, bf16[4,4096,64]{1,2,0:T(8,128)(2,1)}, bf16[4,4096,64]{1,2,0:T(8,128)(2,1)}, s32[4]{0:T(128)S(1...) while((s32[]{:T(128)}, bf16[4,512,64]{1,2,0:T(8,128)(2,1)}, ...), condition=%wide.region_19.20_spmd.clone, body=%wide.region_17.19_spmd.clone.sunk | while | flops 1367637504 | bytes 138052016 | solution.py:186
  574.9 7.1 multiply_reduce_fusion.8
  581.9 7.9 multiply_convert_fusion.8
  589.9 5.3 fusion.159
  597.0 2.0 fusion.158
  603.2 7.1 multiply_reduce_fusion.8
  610.2 7.9 multiply_convert_fusion.8
  618.2 5.3 fusion.159
  625.3 2.0 fusion.158
  631.4 7.1 multiply_reduce_fusion.8
  638.5 7.9 multiply_convert_fusion.8
  646.5 5.3 fusion.159
  653.5 2.0 fusion.158
  659.7 7.1 multiply_reduce_fusion.8
  666.7 7.9 multiply_convert_fusion.8
  674.7 5.3 fusion.159
  681.8 2.0 fusion.158
  687.4 4.8 convolution_convert_fusion.4
  694.3 26.8 %reduce-scatter.12.cloned.1.call-done = bf16[512,256]{0,1:T(8,128)(2,1)} async-done(((bf16[4096,256]{0,1:T(8,128)(2,1)}), bf16[512,256]{0,1:T(8,128)(2,1)}) %reduce-scatter.12.cloned.1.call-update) | async-done | bytes 262160 | tf_op jit(solution)/shard_map/reduce_scatter | solution.py:190
  722.4 35.1 %reduce-scatter.14.cloned.1.call-done = bf16[512,256]{0,1:T(8,128)(2,1)} async-done(((bf16[4096,256]{0,1:T(8,128)(2,1)}), bf16[512,256]{0,1:T(8,128)(2,1)}) %reduce-scatter.14.cloned.1.call-update) | async-done | bytes 262160 | tf_op jit(solution)/shard_map/reduce_scatter | solution.py:193
  759.0 2.3 convolution_add_fusion
  761.4 2.0 fusion.78
  768.0 14.5 %all-reduce.15.cloned.1.call-done = (bf16[256,256]{1,0:T(8,128)(2,1)}, bf16[256,256]{1,0:T(8,128)(2,1)}) async-done(((bf16[256,256]{1,0:T(8,128)(2,1)}, bf16[256,256]{1,0:T(8,128)(2,1)}), (bf16[256,256]{1,0:T(8,128)(2,1)}, bf16[256,256]{1,0:T(8,128)(2,1)})) %all-reduce.15.cloned.1.call-update) | async-done | bytes 262160 | tf_op jit(solution)/shard_map/psum | solution.py:227
  785.9 38.9 %all-reduce.9.cloned.1.call-done = f32[512,512]{1,0:T(8,128)} async-done(((f32[512,512]{1,0:T(8,128)}), f32[512,512]{1,0:T(8,128)}) %all-reduce.9.cloned.1.call-update) | async-done | bytes 1048592 | tf_op jit(solution)/shard_map/psum | solution.py:47
  826.7 35.0 %all-reduce = (f32[256]{0:T(256)}, f32[256]{0:T(256)}, f32[256]{0:T(256)}, f32[256]{0:T(256)}, f32[256]{0:T(256)}, /*index=5*/f32[256]{0:T(256)}) all-reduce(f32[256]{0:T(256)S(1)} %dynamic_slice.61, f32[256]{0:T(256)S(1)} %dynamic_slice.62, ...), channel_id=1, replica_groups=mesh['batch'=2,'hidden'=8,'width'=2] {'batch','hidden'}, use_global_device_ids=true, to_apply=%region_26.27 | all-reduce | flops 1536 | bytes 12288 | tf_op jit(solution)/shard_map/psum | solution.py:209
  864.4 70.8 %all-reduce.11.cloned.1.call-done = (f32[512,256]{1,0:T(8,128)}, f32[512,256]{1,0:T(8,128)}, f32[512,256]{1,0:T(8,128)}, f32[256,512]{1,0:T(8,128)}, f32[512,256]{1,0:T(8,128)}, /*index=5*/f32[512,256]{1,0:T(8,128)}) async-done(((f32[512,256]{1,0:T(8,128)}, f32[512,256]{1,0:T(8,128)}, f32[512,256]{1,0:T(8,128)}, f32[256,512]{1,0:T(8,128)}, f32[512,256]{1,0:T(8,128)}, /*index=5*/f32[512,256]{1,0:T(8,128)}), ...) | async-done | bytes 3145744 | tf_op jit(solution)/shard_map/psum | solution.py:209
  935.1 2.0 copy.72
  937.1 1.9 copy.73
  (292 shorter events, 75.4 us)
Async XLA Ops:
  7.2 285.5 %copy-start = (bf16[512,256]{1,0:T(8,128)(2,1)S(1)}, bf16[512,256]{1,0:T(8,128)(2,1)}, u32[]{:S(2)}) copy-start(bf16[512,256]{1,0:T(8,128)(2,1)} %param.32) | copy-start | bytes 786436
  7.2 32.0 %copy-start.39 = (bf16[512,256]{1,0:T(8,128)(2,1)S(1)}, bf16[512,256]{1,0:T(8,128)(2,1)}, u32[]{:S(2)}) copy-start(bf16[512,256]{1,0:T(8,128)(2,1)} %param.26) | copy-start | bytes 786436
  7.2 33.0 %copy-start.37 = (bf16[512,256]{1,0:T(8,128)(2,1)S(1)}, bf16[512,256]{1,0:T(8,128)(2,1)}, u32[]{:S(2)}) copy-start(bf16[512,256]{1,0:T(8,128)(2,1)} %param.25) | copy-start | bytes 786436
  7.2 34.1 %copy-start.63 = (s32[1,3]{1,0:T(1,128)S(1)}, s32[1,3]{1,0:T(1,128)}, u32[]{:S(2)}) copy-start(s32[1,3]{1,0:T(1,128)} %param.36) | copy-start | bytes 40
  7.2 34.5 %copy-start.43 = (bf16[512,256]{1,0:T(8,128)(2,1)S(1)}, bf16[512,256]{1,0:T(8,128)(2,1)}, u32[]{:S(2)}) copy-start(bf16[512,256]{1,0:T(8,128)(2,1)} %param.24) | copy-start | bytes 786436
  7.2 27.0 %all-gather.15.cloned.1.call-start = ((), (), s32[]{:S(2)}) async-start(), calls=%async_computation.5 | async-start | bytes 1572864 | tf_op jit(solution)/shard_map/all_gather | solution.py:36
  9.2 60.3 %all-gather.19.cloned.1.call-start = ((), (), s32[]{:S(2)}) async-start(), calls=%async_computation.7 | async-start | bytes 2359296 | tf_op jit(solution)/shard_map/all_gather | solution.py:109
  14.6 85.7 %copy-start.53 = (f32[2,1,256]{2,1,0:T(1,128)}, f32[2,1,256]{2,1,0:T(1,128)S(1)}, u32[]{:S(2)}) copy-start(f32[2,1,256]{2,1,0:T(1,128)S(1)} %all-gather.4) | copy-start | bytes 6148
  39.2 119.3 %copy-start.3 = (bf16[512,512]{1,0:T(8,128)(2,1)}, bf16[512,512]{1,0:T(8,128)(2,1)S(1)}, u32[]{:S(2)}) copy-start(bf16[512,512]{1,0:T(8,128)(2,1)S(1)} %add_convert_fusion.1) | copy-start | bytes 1572868
  40.2 60.1 %all-gather.17.cloned.1.call-start = ((), (), s32[]{:S(2)}) async-start(), calls=%async_computation.6 | async-start | bytes 2359296 | tf_op jit(solution)/shard_map/all_gather | solution.py:108
  41.3 117.2 %reduce-scatter.6.cloned.1.call-start = ((), (), s32[]{:S(2)}) async-start(), calls=%async_computation.8 | async-start | bytes 1572864 | tf_op jit(solution)/shard_map/reduce_scatter | solution.py:127
  100.3 58.2 %copy-start.33 = (bf16[512,256]{1,0:T(8,128)(2,1)S(1)}, bf16[512,256]{1,0:T(8,128)(2,1)}, u32[]{:S(2)}) copy-start(bf16[512,256]{1,0:T(8,128)(2,1)} %param.21) | copy-start | bytes 786436
  100.3 58.2 %copy-start.61 = (f32[256]{0:T(256)S(1)}, f32[256]{0:T(256)}, u32[]{:S(2)}) copy-start(f32[256]{0:T(256)} %param.29) | copy-start | bytes 3076
  136.1 49.2 %copy-start.29 = (bf16[4,512,64]{1,2,0:T(8,128)(2,1)}, bf16[4,512,64]{1,2,0:T(8,128)(2,1)S(1)}, u32[]{:S(2)}) copy-start(bf16[4,512,64]{1,2,0:T(8,128)(2,1)S(1)} %get-tuple-element.118) | copy-start | bytes 786436
  136.1 24.9 %copy-start.59 = (f32[256]{0:T(256)S(1)}, f32[256]{0:T(256)}, u32[]{:S(2)}) copy-start(f32[256]{0:T(256)} %param.30) | copy-start | bytes 3076
  136.2 29.1 %copy-start.60 = (f32[256]{0:T(256)S(1)}, f32[256]{0:T(256)}, u32[]{:S(2)}) copy-start(f32[256]{0:T(256)} %param.31) | copy-start | bytes 3076
  138.5 49.1 %copy-start.50 = (bf16[256,256]{1,0:T(8,128)(2,1)S(1)}, bf16[256,256]{1,0:T(8,128)(2,1)}, u32[]{:S(2)}) copy-start(bf16[256,256]{1,0:T(8,128)(2,1)} %param.34) | copy-start | bytes 393220
  138.6 43.9 %all-gather.21.cloned.1.call-start = ((), (), s32[]{:S(2)}) async-start(), calls=%async_computation.9 | async-start | bytes 1572864 | tf_op jit(solution)/shard_map/all_gather | solution.py:36
  161.0 73.9 %all-gather.23.cloned.1.call-start = ((), (), s32[]{:S(2)}) async-start(), calls=%async_computation.10 | async-start | bytes 4718592 | tf_op jit(solution)/shard_map/all_gather | solution.py:43
  187.6 105.1 %reduce-scatter.8.cloned.1.call-start = ((), (), s32[]{:S(2)}) async-start(), calls=%async_computation.11 | async-start | bytes 4718592 | tf_op jit(solution)/shard_map/reduce_scatter | solution.py:137
  193.6 46.8 %copy-start.49 = (bf16[256,256]{1,0:T(8,128)(2,1)S(1)}, bf16[256,256]{1,0:T(8,128)(2,1)}, u32[]{:S(2)}) copy-start(bf16[256,256]{1,0:T(8,128)(2,1)} %param.35) | copy-start | bytes 393220
  243.8 48.9 %copy-start.16 = (bf16[512,512]{1,0:T(8,128)(2,1)S(1)}, bf16[512,512]{1,0:T(8,128)(2,1)}, u32[]{:S(2)}) copy-start(bf16[512,512]{1,0:T(8,128)(2,1)} %add_convert_fusion) | copy-start | bytes 1572868
  243.8 48.9 %copy-start.47 = (f32[512,256]{1,0:T(8,128)S(1)}, f32[512,256]{1,0:T(8,128)}, u32[]{:S(2)}) copy-start(f32[512,256]{1,0:T(8,128)} %get-tuple-element.263) | copy-start | bytes 1572868
  243.8 48.9 %copy-start.48 = (bf16[512,256]{1,0:T(8,128)(2,1)S(1)}, bf16[512,256]{1,0:T(8,128)(2,1)}, u32[]{:S(2)}) copy-start(bf16[512,256]{1,0:T(8,128)(2,1)} %param.37) | copy-start | bytes 786436
  243.8 48.9 %copy-start.62 = (f32[256]{0:T(256)S(1)}, f32[256]{0:T(256)}, u32[]{:S(2)}) copy-start(f32[256]{0:T(256)} %param.33) | copy-start | bytes 3076
  243.8 78.8 %all-gather.25.cloned.1.call-start = ((), (), s32[]{:S(2)}) async-start(), calls=%async_computation.12 | async-start | bytes 2359296 | tf_op jit(solution)/shard_map/all_gather | solution.py:43
  295.2 31.8 %copy-start.40 = (bf16[512,256]{1,0:T(8,128)(2,1)}, bf16[512,256]{1,0:T(8,128)(2,1)S(1)}, u32[]{:S(2)}) copy-start(bf16[512,256]{1,0:T(8,128)(2,1)S(1)} %get-tuple-element.248) | copy-start | bytes 786436
  295.2 162.3 %all-reduce.13.cloned.1.call-start = ((), (), s32[]{:S(2)}) async-start(), calls=%async_computation.18 | async-start | bytes 10485760 | tf_op jit(solution)/shard_map/psum | solution.py:51
  327.0 231.2 %reduce-scatter.10.cloned.1.call-start = ((), (), s32[]{:S(2)}) async-start(), calls=%async_computation.13 | async-start | bytes 9437184 | tf_op jit(solution)/shard_map/reduce_scatter | solution.py:152
  468.5 89.8 %copy-start.5 = (f32[512,512]{1,0:T(8,128)S(1)}, f32[512,512]{1,0:T(8,128)}, u32[]{:S(2)}) copy-start(f32[512,512]{1,0:T(8,128)} %all-gather.21.cloned.1.call-done) | copy-start | bytes 3145732
  468.5 89.8 %copy-start.32 = (f32[512,512]{1,0:T(8,128)S(1)}, f32[512,512]{1,0:T(8,128)}, u32[]{:S(2)}) copy-start(f32[512,512]{1,0:T(8,128)} %get-tuple-element.244) | copy-start | bytes 3145732
  468.5 92.0 %copy-start.34 = (bf16[512,256]{1,0:T(8,128)(2,1)S(1)}, bf16[512,256]{1,0:T(8,128)(2,1)}, u32[]{:S(2)}) copy-start(bf16[512,256]{1,0:T(8,128)(2,1)} %param.21) | copy-start | bytes 786436
  468.5 252.6 %reduce-scatter.12.cloned.1.call-start = ((), (), s32[]{:S(2)}) async-start(), calls=%async_computation.14 | async-start | bytes 2359296 | tf_op jit(solution)/shard_map/reduce_scatter | solution.py:190
  560.0 11.0 %copy-start.42 = (bf16[256,512]{1,0:T(8,128)(2,1)S(1)}, bf16[256,512]{1,0:T(8,128)(2,1)}, u32[]{:S(2)}) copy-start(bf16[256,512]{1,0:T(8,128)(2,1)} %param.27) | copy-start | bytes 786436
  560.5 11.6 %copy-start.9 = (bf16[4096,256]{1,0:T(8,128)(2,1)S(1)}, bf16[4096,256]{1,0:T(8,128)(2,1)}, u32[]{:S(2)}) copy-start(bf16[4096,256]{1,0:T(8,128)(2,1)} %get-tuple-element.562) | copy-start | bytes 6291460
  563.0 8.3 copy-start.22
  574.9 7.1 copy-start.2
  589.9 5.4 copy-start.11
  589.9 5.4 copy-start.25
  603.2 7.1 copy-start.2
  618.2 5.3 copy-start.11
  631.4 7.1 copy-start.2
  659.7 7.1 copy-start.2
  685.1 72.5 %reduce-scatter.14.cloned.1.call-start = ((), (), s32[]{:S(2)}) async-start(), calls=%async_computation.15 | async-start | bytes 2359296 | tf_op jit(solution)/shard_map/reduce_scatter | solution.py:193
  685.7 96.8 %all-reduce.15.cloned.1.call-start = ((), (), s32[]{:S(2)}) async-start(), calls=%async_computation.19 | async-start | bytes 524288 | tf_op jit(solution)/shard_map/psum | solution.py:227
  692.2 28.9 %copy-start.38 = (bf16[512,256]{1,0:T(8,128)(2,1)S(1)}, bf16[512,256]{1,0:T(8,128)(2,1)}, u32[]{:S(2)}) copy-start(bf16[512,256]{1,0:T(8,128)(2,1)} %param.25) | copy-start | bytes 786436
  693.6 65.4 %copy-start.24 = (bf16[512,256]{1,0:T(8,128)(2,1)S(1)}, bf16[512,256]{1,0:T(8,128)(2,1)}, u32[]{:S(2)}) copy-start(bf16[512,256]{1,0:T(8,128)(2,1)} %get-tuple-element.250) | copy-start | bytes 786436
  693.6 131.2 %all-reduce.9.cloned.1.call-start = ((), (), s32[]{:S(2)}) async-start(), calls=%async_computation.16 | async-start | bytes 2097152 | tf_op jit(solution)/shard_map/psum | solution.py:47
  694.3 67.1 %copy-start.19 = (bf16[512,512]{1,0:T(8,128)(2,1)S(1)}, bf16[512,512]{1,0:T(8,128)(2,1)}, u32[]{:S(2)}) copy-start(bf16[512,512]{1,0:T(8,128)(2,1)} %copy-done.18) | copy-start | bytes 1572868
  722.4 41.0 %copy-start.4 = (bf16[512,512]{1,0:T(8,128)(2,1)S(1)}, bf16[512,512]{1,0:T(8,128)(2,1)}, u32[]{:S(2)}) copy-start(bf16[512,512]{1,0:T(8,128)(2,1)} %copy-done.3) | copy-start | bytes 1572868
  722.4 41.0 %copy-start.28 = (bf16[4,512,64]{1,2,0:T(8,128)(2,1)S(1)}, bf16[4,512,64]{1,2,0:T(8,128)(2,1)}, u32[]{:S(2)}) copy-start(bf16[4,512,64]{1,2,0:T(8,128)(2,1)} %get-tuple-element.120) | copy-start | bytes 786436
  759.0 6.8 copy-start.35
  759.0 7.9 copy-start.36
  761.3 173.8 %all-reduce.11.cloned.1.call-start = ((), (), s32[]{:S(2)}) async-start(), calls=%async_computation.17 | async-start | bytes 6291456 | tf_op jit(solution)/shard_map/psum | solution.py:209
  764.6 60.3 %copy-start.6 = (f32[512,512]{1,0:T(8,128)S(1)}, f32[512,512]{1,0:T(8,128)}, u32[]{:S(2)}) copy-start(f32[512,512]{1,0:T(8,128)} %all-gather.15.cloned.1.call-done) | copy-start | bytes 3145732
  764.6 60.3 %copy-start.52 = (f32[512]{0:T(512)S(1)}, f32[512]{0:T(512)}, u32[]{:S(2)}) copy-start(f32[512]{0:T(512)} %copy-done.51) | copy-start | bytes 6148
  764.6 60.3 %copy-start.54 = (f32[2,1,256]{2,1,0:T(1,128)S(1)}, f32[2,1,256]{2,1,0:T(1,128)}, u32[]{:S(2)}) copy-start(f32[2,1,256]{2,1,0:T(1,128)} %copy-done.53) | copy-start | bytes 6148
  764.6 60.3 %copy-start.56 = (f32[512]{0:T(512)S(1)}, f32[512]{0:T(512)}, u32[]{:S(2)}) copy-start(f32[512]{0:T(512)} %copy-done.55) | copy-start | bytes 6148
  765.7 96.0 %copy-start.58 = (f32[512]{0:T(512)S(1)}, f32[512]{0:T(512)}, u32[]{:S(2)}) copy-start(f32[512]{0:T(512)} %copy-done.57) | copy-start | bytes 6148
  768.0 95.4 %copy-start.21 = (f32[512,256]{1,0:T(8,128)S(1)}, f32[512,256]{1,0:T(8,128)}, u32[]{:S(2)}) copy-start(f32[512,256]{1,0:T(8,128)} %get-tuple-element.264) | copy-start | bytes 1572868
  768.0 95.4 %copy-start.23 = (f32[512,256]{1,0:T(8,128)S(1)}, f32[512,256]{1,0:T(8,128)}, u32[]{:S(2)}) copy-start(f32[512,256]{1,0:T(8,128)} %copy-done.22) | copy-start | bytes 1572868
  863.4 80.9 %copy-start.1 = (bf16[512,256]{1,0:T(8,128)(2,1)S(1)}, bf16[512,256]{1,0:T(8,128)(2,1)}, u32[]{:S(2)}) copy-start(bf16[512,256]{1,0:T(8,128)(2,1)} %param.32) | copy-start | bytes 786436
  935.1 7.6 copy-start.46
  935.1 8.4 copy-start.45
  (39 other events, 89.0 us)
Sparse Core Ops, SparseCore 0:
  10.2 23.9 all-gather.14
  40.3 29.1 all-gather.18
  71.7 28.5 all-gather.16
  138.7 19.7 reduce-scatter.5
  161.1 21.3 all-gather.20
  187.7 47.1 all-gather.22
  243.9 48.7 reduce-scatter.7
  295.3 27.2 all-gather.24
  327.1 130.3 all-reduce.12
  468.6 89.5 reduce-scatter.9
  685.2 35.8 reduce-scatter.11
  723.3 34.2 reduce-scatter.13
  760.5 21.9 all-reduce.14
  784.8 40.0 all-reduce.8
  829.5 105.5 all-reduce.10
where the time goes:
time: 953 us; the launch traced here: 951 us
  waiting for transfers between devices  629 us (66%)
  matrix products  141 us (15%)
  blocking collectives  66.3 us (7%)
  other arithmetic  65.8 us (7%)
  local copies, waits for them, and re-layouts  28.1 us (3%)
  between operations  14.6 us (2%)
    psum x1, waiting for transfers between devices, unit_total(): return lax.psum(partial_sum, 'width')  130 us
    reduce_scatter x1, waiting for transfers between devices, local(): lax.psum_scatter(outer_cols(grad_pre, up_full), 'hidden', scatter_dimensi...  89.7 us
    psum x1, waiting for transfers between devices, local(): lax.psum((inner_rows(normed_one, grad_queries), inner_rows(normed_one, gr...  70.8 us
    all_gather x2, waiting for transfers between devices, spread_rows(): return lax.all_gather(values, 'hidden', axis=0, tiled=True)  67.4 us
    dot_general x20, matrix products, outer_cols(): lax.dot_general(left, right, (((1,), (1,)), ((), ())), preferred_element_...  65 us
    reduce_scatter x1, waiting for transfers between devices, local(): lax.psum_scatter(matmul(hidden_act, w_down), 'hidden', scatter_dimension=...  48.6 us
    dot_general x16, matrix products, inner_rows(): lax.dot_general(left, right, (((0,), (0,)), ((), ())), preferred_element_...  43.1 us
    psum x1, waiting for transfers between devices, width_total(): return lax.psum(partial_sum, 'width')  38.9 us
  transfers between devices with their start and end apart: 15, of which 15 were waited for; matrix products, arithmetic and copies ran while one was open for 3% of the time, Pallas kernels for 0%

commit v1 on v0

v1 whole, which is shorter than its diff:
```python
import functools

import jax
import jax.numpy as jnp
from jax import lax
from jax.experimental import pallas as pl
from jax.experimental.pallas import tpu as pltpu
from jax.sharding import PartitionSpec as P

HD = 64
EPSILON = 1e-05
MESH = pl.DeviceIdType.MESH
F32 = jnp.float32
BF16 = jnp.bfloat16
NEG = -1e30
VMEM_LIMIT = 60 * 1024 * 1024


def nn(a, b):
    return lax.dot_general(a, b, (((1,), (0,)), ((), ())), preferred_element_type=F32)


def nt(a, b):
    return lax.dot_general(a, b, (((1,), (1,)), ((), ())), preferred_element_type=F32)


def place():
    return lax.axis_index("batch"), lax.axis_index("hidden"), lax.axis_index("width")


def remote(src, dst, send, recv, dev):
    return pltpu.make_async_remote_copy(
        src_ref=src, dst_ref=dst, send_sem=send, recv_sem=recv, device_id=dev, device_id_type=MESH
    )


def at(index, size):
    return pl.ds(pl.multiple_of(index * size, size), size)


def greet_group(nh, b, h, w):
    barrier = pltpu.get_barrier_semaphore()
    for dw in range(2):
        for dh in range(nh):
            if dh or dw:
                dev = (b, lax.rem(h + dh, nh), lax.rem(w + dw, 2))
                pl.semaphore_signal(barrier, inc=1, device_id=dev, device_id_type=MESH)
    pl.semaphore_wait(barrier, 2 * nh - 1)


def sub_row(index, sub, dph):
    return jnp.where(lax.rem(index, 2) == 0, sub, dph - 1 - sub)


def segments(pos, ends):
    total = jnp.zeros(pos.shape, jnp.int32)
    for end in ends:
        total = total + (pos >= end).astype(jnp.int32)
    return total


def allowed_mask(key_base, query_base, keys, queries, ends):
    key_pos = key_base + lax.broadcasted_iota(jnp.int32, (keys, 1), 0)
    query_pos = query_base + lax.broadcasted_iota(jnp.int32, (1, queries), 1)
    same = segments(key_pos, ends) == segments(query_pos, ends)
    return same & (key_pos <= query_pos)


def for_key_blocks(h, nh, block, carry):
    plain_end = jnp.where(h == nh - 1, 1, jnp.maximum(h, 1))
    carry = lax.fori_loop(1, plain_end, lambda j, c: block(j, c, False), carry)
    masked = 1 + jnp.where(h > 0, h + 1 - plain_end, 0)

    def some(t, c):
        return block(jnp.where(t == 0, 0, plain_end + t - 1), c, True)

    return lax.fori_loop(0, masked, some, carry)


def front_kernel(nh, rows, dims, *refs):
    (
        lens, tok, cot, vecs, wq, wk, wv,
        tok_rows, cot_rows, vecf, normed, att_t, kvt, kvn, qt, ot, lse, wqt_out, wkvt_out,
        tokf, wqt, wkvt, qsrc, kvsrc, osend,
        xs, xr, qs, qr, ks, kr, fs, fr, osnd, orcv, lsem,
    ) = refs
    heads, dph, tq, half = dims
    b, h, w = place()
    group, sub = lax.div(h, dph), lax.rem(h, dph)
    partner = (b, h, 1 - w)
    cw = 256
    chunks = rows // half
    own = at(w, cw)
    other = at(1 - w, cw)
    ends = [lens[0, 0], lens[0, 0] + lens[0, 1], lens[0, 0] + lens[0, 1] + lens[0, 2]]

    greet_group(nh, b, h, w)

    vecf[:, own] = vecs[...]
    copies = [remote(vecs, vecf.at[:, own], xs.at[0], xr.at[0], partner)]
    for c in range(chunks):
        part = pl.ds(c * half, half)
        copies.append(
            remote(tok.at[part], tokf.at[part, own], xs.at[1 + c], xr.at[1 + c], partner)
        )
    copies.append(
        remote(cot.at[at(1 - w, half)], cot_rows.at[:, own], xs.at[1 + chunks], xr.at[1 + chunks], partner)
    )
    for copy in copies:
        copy.start()
    tokf[:, own] = tok[...]
    cot_rows[:, own] = cot[at(w, half), :]

    wqt[...] = wq[...].astype(F32).T.astype(BF16)
    wkt = wk[...].astype(F32).T.astype(BF16)
    wvt = wv[...].astype(F32).T.astype(BF16)
    for t in range(heads):
        wkvt[t, :HD, :] = wkt[t * HD : (t + 1) * HD]
        wkvt[t, HD:, :] = wvt[t * HD : (t + 1) * HD]
    wqt_out[...] = wqt[...]
    wkvt_out[...] = wkvt[...]

    copies[0].wait()
    gain = vecf[0:1, :]
    shift = vecf[1:2, :]
    sends = []
    per_chunk = half // tq
    for c in range(chunks):
        part = slice(c * half, (c + 1) * half)
        copies[1 + c].wait()
        x = tokf[part, :].astype(F32)
        centre = x - jnp.mean(x, -1, keepdims=True)
        spread = jnp.mean(centre * centre, -1, keepdims=True)
        n = (centre * lax.rsqrt(spread + EPSILON) * gain + shift).astype(BF16)
        normed[part, :] = n
        q = (nt(wqt[...], n)).astype(BF16)
        for t in range(heads):
            qsrc[t, :, part] = q[t * HD : (t + 1) * HD]
            kvsrc[t, :, part] = nt(wkvt[t], n).astype(BF16)
        for k in range(heads - 1, -1, -1):
            t = lax.rem(group + k, heads)
            dev = (b, t * dph + sub, w)
            src, dst = kvsrc.at[t, :, pl.ds(c * half, half)], kvt.at[h, :, pl.ds(c * half, half)]
            if k:
                copy = remote(src, dst, ks.at[k, c], kr.at[h, c], dev)
                copy.start()
                sends.append((None, copy))
            else:
                pltpu.make_async_copy(src, dst, kr.at[h, c]).start()
            for i in range(per_chunk):
                r = c * per_chunk + i
                target = sub_row(h, r, dph)
                src, dst = qsrc.at[t, :, pl.ds(r * tq, tq)], qt.at[h]
                copy = remote(src, dst, qs.at[k, r], qr.at[h], (b, t * dph + target, w))
                if k:
                    copy.start()
                    sends.append((None, copy))
                else:
                    away = target != sub

                    @pl.when(away)
                    def _(copy=copy):
                        copy.start()

                    @pl.when(jnp.logical_not(away))
                    def _(src=src, dst=dst):
                        pltpu.make_async_copy(src, dst, qr.at[h]).start()

                    sends.append((away, copy))

    tok_rows[...] = tokf[at(w, half), :]

    def pass_on(s, _):
        direct = lax.rem(s, dph) == sub

        @pl.when(direct)
        def _():
            for c in range(chunks):
                part = kvt.at[s, :, pl.ds(c * half, half)]
                pltpu.make_async_copy(part, part, kr.at[s, c]).wait()
            for k in range(1, dph):
                dev = (b, group * dph + lax.rem(sub + k, dph), w)
                remote(kvt.at[s], kvt.at[s], fs.at[s, k], fr.at[s], dev).start()

        return 0

    lax.fori_loop(0, nh, pass_on, 0)

    def arrive(s):
        @pl.when(lax.rem(s, dph) != sub)
        def _():
            pltpu.make_async_copy(kvt.at[s], kvt.at[s], fr.at[s]).wait()

        kvn[s] = kvt[s].astype(F32).T.astype(BF16)
        pltpu.make_async_copy(qt.at[s], qt.at[s], qr.at[s]).wait()

    def one_query_block(s, _):
        arrive(s)
        r = sub_row(s, sub, dph)
        query_base = s * rows + r * tq
        q = qt[s].astype(F32) * (HD**-0.5)
        q = jnp.concatenate([q, jnp.zeros_like(q)], 0).astype(BF16)

        def block(j, carry, masked):
            top, total, mixed = carry
            scores = nn(kvn[j], q)
            if masked:
                keep = allowed_mask(j * rows, query_base, rows, tq, ends)
                scores = jnp.where(keep, scores, NEG)
            new_top = jnp.maximum(top, jnp.max(scores, 0, keepdims=True))
            fade = jnp.exp(top - new_top)
            weights = jnp.exp(scores - new_top)
            total = total * fade + jnp.sum(weights, 0, keepdims=True)
            mixed = mixed * fade + nn(kvt[j, HD:, :], weights.astype(BF16))
            return new_top, total, mixed

        init = (jnp.full((1, tq), NEG, F32), jnp.zeros((1, tq), F32), jnp.zeros((HD, tq), F32))
        top, total, mixed = for_key_blocks(s, nh, block, init)
        mixed = mixed / total
        ot[s] = mixed
        lse[s] = top + jnp.log(total)
        osend[s] = mixed.astype(BF16)
        row_w = lax.div(r * tq, half)
        lane = lax.rem(r * tq, half)
        place_in = lax.div(lane, tq)
        dst = att_t.at[at(w * heads + group, HD), pl.ds(pl.multiple_of(lane, tq), tq)]
        slot = orcv.at[w * heads + group, place_in]
        here = (s == h) & (row_w == w)

        @pl.when(here)
        def _():
            pltpu.make_async_copy(osend.at[s], dst, slot).start()

        @pl.when(jnp.logical_not(here))
        def _():
            remote(osend.at[s], dst, osnd.at[s], slot, (b, s, row_w)).start()

        return 0

    lax.fori_loop(0, nh, one_query_block, 0)

    for g in range(2 * heads):
        for i in range(half // tq):
            dst = att_t.at[pl.ds(g * HD, HD), pl.ds(i * tq, tq)]
            pltpu.make_async_copy(dst, dst, orcv.at[g, i]).wait()

    def sent(s, _):
        r = sub_row(s, sub, dph)
        here = (s == h) & (lax.div(r * tq, half) == w)

        @pl.when(jnp.logical_not(here))
        def _():
            pltpu.make_async_copy(osend.at[s], osend.at[s], osnd.at[s]).wait()

        @pl.when(lax.rem(s, dph) == sub)
        def _():
            for k in range(1, dph):
                pltpu.make_async_copy(kvt.at[s], kvt.at[s], fs.at[s, k]).wait()

        return 0

    lax.fori_loop(0, nh, sent, 0)
    copies[-1].wait()
    for away, copy in sends:
        if away is None:
            copy.wait_send()
        else:

            @pl.when(away)
            def _(copy=copy):
                copy.wait_send()


def sigmoid(x):
    return 1.0 / (1.0 + jnp.exp(-x))


def middle_kernel(nh, *refs):
    (
        tok_rows, cot_rows, vecf, normed, att_t, wg1, wg2, wout, wup, wdn,
        out_rows, gatt_t, gup, gdn_t, gwo, gg1, gg2, vecp, ginp, gterm,
        pre_s, act_s,
    ) = refs
    half = tok_rows.shape[0]
    w = lax.axis_index("width")
    cw = 256
    tok = tok_rows[...].astype(F32)
    n1 = normed[at(w, half), :]

    def two(a, wt):
        return jnp.concatenate([nn(a, wt[0]), nn(a, wt[1])], 1)

    def two_back(g, wt):
        return nt(g[:, :cw], wt[0]) + nt(g[:, cw:], wt[1])

    attended = att_t[...].astype(F32).T.astype(BF16)
    branch_one = nn(attended, wout[...])
    gate_one = sigmoid(two(n1, wg1) + vecf[2:3, :])
    middle = tok + gate_one * (branch_one - tok)
    centre = middle - jnp.mean(middle, -1, keepdims=True)
    rstd = lax.rsqrt(jnp.mean(centre * centre, -1, keepdims=True) + EPSILON)
    n2 = centre * rstd
    gain_two = vecf[3:4, :]
    normed_two = (n2 * gain_two + vecf[4:5, :]).astype(BF16)
    gate_two = sigmoid(two(normed_two, wg2) + vecf[5:6, :])

    def up(i, branch):
        pre = nn(normed_two, wup[i])
        pre_s[i] = pre
        act = jax.nn.gelu(pre).astype(BF16)
        act_s[i] = act
        return branch + jnp.concatenate([nn(act, wdn[i, 0]), nn(act, wdn[i, 1])], 1)

    branch_two = lax.fori_loop(0, nh, up, jnp.zeros(middle.shape, F32))
    delta = branch_two - middle
    out_rows[...] = (middle + gate_two * delta).astype(BF16)
    grad = cot_rows[...].astype(F32)
    gb2 = (grad * gate_two).astype(BF16)
    gl2 = (grad * delta * gate_two * (1.0 - gate_two)).astype(BF16)
    gmid = grad * (1.0 - gate_two)
    normed_two_t = normed_two.astype(F32).T.astype(BF16)
    gb2_t = gb2.astype(F32).T.astype(BF16)

    def down(i, total):
        ghid = nt(gb2[:, :cw], wdn[i, 0]) + nt(gb2[:, cw:], wdn[i, 1])
        pre = pre_s[i]
        c = 0.7978845608028654
        t = jnp.tanh(c * (pre + 0.044715 * pre * pre * pre))
        slope = 0.5 * (1.0 + t) + 0.5 * pre * (1.0 - t * t) * (c * (1.0 + 3 * 0.044715 * pre * pre))
        gpre = (ghid * slope).astype(BF16)
        gdn_t[i] = nn(gb2_t, act_s[i]).astype(BF16)
        gup[i] = nn(normed_two_t, gpre).astype(BF16)
        return total + nt(gpre, wup[i])

    gnorm = lax.fori_loop(0, nh, down, two_back(gl2, wg2))
    gg2[...] = nn(normed_two_t, gl2).astype(BF16)
    e = gnorm * gain_two
    gmid = gmid + rstd * (
        e - jnp.mean(e, -1, keepdims=True) - n2 * jnp.mean(e * n2, -1, keepdims=True)
    )
    gb1 = (gmid * gate_one).astype(BF16)
    gl1 = (gmid * (branch_one - tok) * gate_one * (1.0 - gate_one)).astype(BF16)
    ginp[...] = gmid * (1.0 - gate_one)
    gatt_t[...] = nt(wout[...], gb1).astype(BF16)
    gwo[...] = nn(att_t[...], gb1).astype(BF16)
    gg1[...] = nn(n1.astype(F32).T.astype(BF16), gl1).astype(BF16)
    gterm[...] = two_back(gl1, wg1)
    vecp[...] = jnp.zeros_like(vecp)
    vecp[2:3, :] = jnp.sum(gl1.astype(F32), 0, keepdims=True)
    vecp[3:4, :] = jnp.sum(gnorm * n2, 0, keepdims=True)
    vecp[4:5, :] = jnp.sum(gnorm, 0, keepdims=True)
    vecp[5:6, :] = jnp.sum(gl2.astype(F32), 0, keepdims=True)


def back_kernel(nh, rows, dims, *refs):
    (
        lens, gatt_t, kvt, kvn, qt, ot, lse, normed, wqt, wkvt, tok_rows, ginp, gterm, out_rows, vecf,
        out_c, gtok, gq_t, gkv_t, vecp,
        dot_all, acc, part_in, dqsend, dkvsend, dq_t, dkv_t, psend, precv, tsend, trecv,
        ds, dr, xs, xr, qs, qr, ps, pr, ks, kr,
    ) = refs
    heads, dph, tq, half = dims
    b, h, w = place()
    group, sub = lax.div(h, dph), lax.rem(h, dph)
    partner = (b, h, 1 - w)
    cw = 256
    own, other = at(w, cw), at(1 - w, cw)
    per = half // tq
    ends = [lens[0, 0], lens[0, 0] + lens[0, 1], lens[0, 0] + lens[0, 1] + lens[0, 2]]

    greet_group(nh, b, h, w)

    sends = []
    for dw in (1, 0):
        wt = lax.rem(w + dw, 2)
        for k in range(heads - 1, -1, -1):
            t = lax.rem(group + k, heads)
            for i in range(per):
                r = w * per + i
                target = sub_row(h, r, dph)
                src = gatt_t.at[at(wt * heads + t, HD), pl.ds(i * tq, tq)]
                dst = dot_all.at[h]
                copy = remote(src, dst, ds.at[dw, k, i], dr.at[h], (b, t * dph + target, wt))
                if k or dw:
                    copy.start()
                    sends.append((None, copy))
                else:
                    away = target != sub

                    @pl.when(away)
                    def _(copy=copy):
                        copy.start()

                    @pl.when(jnp.logical_not(away))
                    def _(src=src, dst=dst):
                        pltpu.make_async_copy(src, dst, dr.at[h]).start()

                    sends.append((away, copy))
    mine = at(w, half)
    out_copy = remote(out_rows.at[:, other], out_c.at[mine, :], xs.at[0], xr.at[0], partner)
    out_copy.start()
    out_c[mine, :] = out_rows[:, own]
    acc[...] = jnp.zeros_like(acc)

    def send_kv(s, total):
        dkvsend[s] = total.astype(BF16)
        dst = dkv_t.at[group]

        @pl.when(s == h)
        def _():
            pltpu.make_async_copy(dkvsend.at[s], dst, kr.at[group]).start()

        @pl.when(s != h)
        def _():
            remote(dkvsend.at[s], dst, ks.at[s], kr.at[group], (b, s, w)).start()

    def finish(s):
        @pl.when(lax.rem(s, dph) == sub)
        def _():
            total = acc[s]
            for k in range(1, dph):
                slot = part_in.at[lax.div(s, dph), k - 1]
                pltpu.make_async_copy(slot, slot, pr.at[lax.div(s, dph), k - 1]).wait()
                total = total + part_in[lax.div(s, dph), k - 1]
            send_kv(s, total)

    def one_query_block(step, _):
        s = nh - 1 - step
        r = sub_row(s, sub, dph)
        query_base = s * rows + r * tq
        pltpu.make_async_copy(dot_all.at[s], dot_all.at[s], dr.at[s]).wait()
        q = qt[s]
        dout = dot_all[s]
        q_low = jnp.concatenate([q.astype(F32) * (HD**-0.5), jnp.zeros((HD, tq), F32)], 0).astype(BF16)
        d_high = jnp.concatenate([jnp.zeros((HD, tq), BF16), dout], 0)
        log_sum = lse[s]
        centre = jnp.sum(ot[s] * dout.astype(F32), 0, keepdims=True)

        def block(j, dq, masked):
            scores = nn(kvn[j], q_low)
            if masked:
                keep = allowed_mask(j * rows, query_base, rows, tq, ends)
                scores = jnp.where(keep, scores, NEG)
            probs = jnp.exp(scores - log_sum)
            gprobs = nn(kvn[j], d_high)
            gscores = (probs * (gprobs - centre)).astype(BF16)
            acc[j, HD:, :] += nt(dout, probs.astype(BF16))
            acc[j, :HD, :] += nt(q, gscores) * (HD**-0.5)
            return dq + nn(kvt[j, :HD, :], gscores)

        dq = for_key_blocks(s, nh, block, jnp.zeros((HD, tq), F32))
        dqsend[s] = (dq * (HD**-0.5)).astype(BF16)
        dst = dq_t.at[pl.ds(pl.multiple_of(group * HD, HD), HD), pl.ds(pl.multiple_of(r * tq, tq), tq)]

        @pl.when(s == h)
        def _():
            pltpu.make_async_copy(dqsend.at[s], dst, qr.at[group, r]).start()

        @pl.when(s != h)
        def _():
            remote(dqsend.at[s], dst, qs.at[s], qr.at[group, r], (b, s, w)).start()

        owner = lax.rem(s, dph)

        @pl.when(owner != sub)
        def _():
            k = lax.rem(sub - owner + dph, dph)
            dev = (b, group * dph + owner, w)
            remote(acc.at[s], part_in.at[lax.div(s, dph), k - 1], ps.at[s], pr.at[lax.div(s, dph), k - 1], dev).start()

        @pl.when(step > 0)
        def _():
            finish(s + 1)

        return 0

    lax.fori_loop(0, nh, one_query_block, 0)
    finish(0)

    for g in range(heads):
        pltpu.make_async_copy(dkv_t.at[g], dkv_t.at[g], kr.at[g]).wait()
        for r in range(dph):
            dst = dq_t.at[pl.ds(g * HD, HD), pl.ds(r * tq, tq)]
            pltpu.make_async_copy(dst, dst, qr.at[g, r]).wait()

    kv = dkv_t[...].reshape(heads * 2 * HD, rows)
    wkv = wkvt[...].reshape(heads * 2 * HD, wkvt.shape[2])

    def wide(lanes):
        a = dq_t[:, lanes].astype(F32).T.astype(BF16)
        c = dkv_t[:, :, lanes].reshape(heads * 2 * HD, half).astype(F32).T.astype(BF16)
        return nn(a, wqt[...]) + nn(c, wkv)

    psend[...] = wide(at(1 - w, half)).astype(BF16)
    pcopy = remote(psend, precv, xs.at[1], xr.at[1], partner)
    pcopy.start()
    gnorm = wide(at(w, half)) + gterm[...]
    gq_t[...] = nn(dq_t[...], normed[...])
    gkv_t[...] = nn(kv, normed[...])
    x = tok_rows[...].astype(F32)
    centre = x - jnp.mean(x, -1, keepdims=True)
    rstd = lax.rsqrt(jnp.mean(centre * centre, -1, keepdims=True) + EPSILON)
    n = centre * rstd
    pcopy.wait()
    gnorm = gnorm + precv[...].astype(F32)
    e = gnorm * vecf[0:1, :]
    result = ginp[...] + rstd * (
        e - jnp.mean(e, -1, keepdims=True) - n * jnp.mean(e * n, -1, keepdims=True)
    )
    tsend[...] = result.astype(BF16)
    tcopy = remote(tsend.at[:, other], trecv, xs.at[2], xr.at[2], partner)
    tcopy.start()
    vecp[...] = jnp.zeros_like(vecp)
    vecp[0:1, :] = jnp.sum(gnorm * n, 0, keepdims=True)
    vecp[1:2, :] = jnp.sum(gnorm, 0, keepdims=True)
    gtok[mine, :] = jnp.where(w == 0, result[:, :cw], result[:, cw:])
    tcopy.wait()
    gtok[at(1 - w, half), :] = trecv[...].astype(F32)
    out_copy.wait()

    def sent(s, _):
        @pl.when(s != h)
        def _():
            pltpu.make_async_copy(dqsend.at[s], dqsend.at[s], qs.at[s]).wait()

        @pl.when((s != h) & (lax.rem(s, dph) == sub))
        def _():
            pltpu.make_async_copy(dkvsend.at[s], dkvsend.at[s], ks.at[s]).wait()

        @pl.when(lax.rem(s, dph) != sub)
        def _():
            pltpu.make_async_copy(acc.at[s], acc.at[s], ps.at[s]).wait()

        return 0

    lax.fori_loop(0, nh, sent, 0)
    for away, copy in sends:
        if away is None:
            copy.wait_send()
        else:

            @pl.when(away)
            def _(copy=copy):
                copy.wait_send()


def call(kernel, ins, smem, outs, scratch, collective_id=None, flops=0, nbytes=0):
    specs = [pl.BlockSpec(memory_space=pltpu.SMEM if i < smem else pltpu.VMEM) for i in range(len(ins))]
    params = dict(vmem_limit_bytes=VMEM_LIMIT)
    if collective_id is not None:
        params.update(collective_id=collective_id, has_side_effects=True)
    return pl.pallas_call(
        kernel,
        out_shape=[jax.ShapeDtypeStruct(shape, kind) for shape, kind in outs],
        in_specs=specs,
        out_specs=[pl.BlockSpec(memory_space=pltpu.VMEM)] * len(outs),
        scratch_shapes=scratch,
        compiler_params=pltpu.CompilerParams(**params),
        cost_estimate=pl.CostEstimate(flops=flops, bytes_accessed=nbytes, transcendentals=0),
    )(*ins)


def local(
    tokens, ln1_gain, ln1_bias, w_query, w_key, w_value, w_out, gate1_weight, gate1_bias,
    ln2_gain, ln2_bias, gate2_weight, gate2_bias, w_up, w_down, lengths, cotangent,
):
    nh = lax.axis_size("hidden")
    rows, cw = tokens.shape
    wide = 2 * cw
    heads = cw // HD
    dph = nh // heads
    tq = rows // dph
    half = rows // 2
    units = w_up.shape[1]
    dims = (heads, dph, tq, half)
    dma, vmem = pltpu.SemaphoreType.DMA, pltpu.VMEM

    vecs = jnp.stack([ln1_gain, ln1_bias, gate1_bias, ln2_gain, ln2_bias, gate2_bias, ln1_gain, ln1_gain])
    wup = lax.all_gather(w_up, ("hidden", "width"), axis=0, tiled=True).reshape(nh, wide, units)
    wdn = lax.all_gather(w_down, ("hidden", "width"), axis=0).reshape(nh, 2, units, cw)
    wg1 = lax.all_gather(gate1_weight, "width", axis=0)
    wg2 = lax.all_gather(gate2_weight, "width", axis=0)
    wout = lax.all_gather(w_out, "width", axis=0, tiled=True)

    front = call(
        functools.partial(front_kernel, nh, rows, dims),
        [lengths, tokens, cotangent, vecs, w_query, w_key, w_value],
        1,
        [
            ((half, wide), BF16), ((half, wide), BF16), ((8, wide), F32), ((rows, wide), BF16),
            ((2 * heads * HD, half), BF16), ((nh, 2 * HD, rows), BF16), ((nh, rows, 2 * HD), BF16),
            ((nh, HD, tq), BF16), ((nh, HD, tq), F32), ((nh, 1, tq), F32),
            ((cw, wide), BF16), ((heads, 2 * HD, wide), BF16),
        ],
        [
            vmem((rows, wide), BF16), vmem((cw, wide), BF16), vmem((heads, 2 * HD, wide), BF16),
            vmem((heads, HD, rows), BF16), vmem((heads, 2 * HD, rows), BF16), vmem((nh, HD, tq), BF16),
            dma((4,)), dma((4,)), dma((heads, dph)), dma((nh,)), dma((heads, 2)), dma((nh, 2)),
            dma((nh, dph)), dma((nh,)), dma((nh,)), dma((2 * heads, half // tq)), dma((1,)),
        ],
        collective_id=1,
        flops=30 * 10**9,
        nbytes=20 * 10**6,
    )
    tok_rows, cot_rows, vecf, normed, att_t, kvt, kvn, qt, ot, lse, wqt, wkvt = front

    mid = call(
        functools.partial(middle_kernel, nh),
        [tok_rows, cot_rows, vecf, normed, att_t, wg1, wg2, wout, wup, wdn],
        0,
        [
            ((half, wide), BF16), ((wide, half), BF16), ((nh, wide, units), BF16), ((nh, wide, units), BF16),
            ((wide, wide), BF16), ((wide, wide), BF16), ((wide, wide), BF16), ((8, wide), F32),
            ((half, wide), F32), ((half, wide), F32),
        ],
        [vmem((nh, half, units), F32), vmem((nh, half, units), BF16)],
        flops=10 * 10**9,
        nbytes=20 * 10**6,
    )
    out_rows, gatt_t, gup, gdn_t, gwo, gg1, gg2, vecp_two, ginp, gterm = mid

    back = call(
        functools.partial(back_kernel, nh, rows, dims),
        [lengths, gatt_t, kvt, kvn, qt, ot, lse, normed, wqt, wkvt, tok_rows, ginp, gterm, out_rows, vecf],
        1,
        [
            ((rows, cw), BF16), ((rows, cw), F32), ((cw, wide), F32), ((2 * cw, wide), F32), ((8, wide), F32),
        ],
        [
            vmem((nh, HD, tq), BF16), vmem((nh, 2 * HD, rows), F32),
            vmem((nh // dph, max(dph - 1, 1), 2 * HD, rows), F32), vmem((nh, HD, tq), BF16),
            vmem((nh, 2 * HD, rows), BF16), vmem((cw, rows), BF16), vmem((heads, 2 * HD, rows), BF16),
            vmem((half, wide), BF16), vmem((half, wide), BF16), vmem((half, wide), BF16), vmem((half, cw), BF16),
            dma((2, heads, half // tq)), dma((nh,)), dma((3,)), dma((3,)), dma((nh,)), dma((heads, dph)),
            dma((nh,)), dma((nh // dph, max(dph - 1, 1))), dma((nh,)), dma((heads,)),
        ],
        collective_id=2,
        flops=40 * 10**9,
        nbytes=20 * 10**6,
    )
    out_c, gtok, gq_t, gkv_t, vecp_one = back

    ffn = jnp.concatenate([gup.reshape(2 * nh, cw, units), gdn_t.reshape(2 * nh, cw, units)], 2)
    ffn = lax.psum(lax.psum_scatter(ffn, ("hidden", "width"), scatter_dimension=0, tiled=True), "batch")[0]
    grad_up = ffn[:, :units].astype(F32)
    grad_down = ffn[:, units:].astype(F32).T
    width_pos = lax.axis_index("width")
    every = ("batch", "hidden")
    gwo, gg1, gg2 = lax.psum(
        (
            lax.psum_scatter(gwo, "width", scatter_dimension=0, tiled=True),
            lax.psum_scatter(gg1, "width", scatter_dimension=1, tiled=True),
            lax.psum_scatter(gg2, "width", scatter_dimension=1, tiled=True),
        ),
        every,
    )
    gq_t, gkv_t = lax.psum((gq_t, gkv_t), every)
    vec = lax.psum(vecp_one + vecp_two, ("batch", "hidden", "width"))
    vec = lax.dynamic_slice_in_dim(vec, width_pos * cw, cw, 1)
    gkv_t = gkv_t.reshape(heads, 2, HD, wide)
    return (
        out_c,
        gtok,
        vec[0],
        vec[1],
        gq_t.T,
        gkv_t[:, 0].reshape(cw, wide).T,
        gkv_t[:, 1].reshape(cw, wide).T,
        gwo.astype(F32),
        gg1.astype(F32),
        vec[2],
        vec[3],
        vec[4],
        gg2.astype(F32),
        vec[5],
        grad_up,
        grad_down,
    )


def solution(mesh):
    cols = P(None, "width")
    vec = P("width")
    in_specs = (
        P(("batch", "hidden"), "width"), vec, vec, cols, cols, cols, P("width", None), cols, vec, vec, vec,
        cols, vec, P("width", "hidden"), P("hidden", "width"), P("batch", None),
        P(("batch", "hidden"), "width"),
    )
    out_specs = (
        P(("batch", "hidden"), "width"), P(("batch", "hidden"), "width"), vec, vec, cols, cols, cols,
        P("width", None), cols, vec, vec, vec, cols, vec, P("width", "hidden"), P("hidden", "width"),
    )
    return jax.shard_map(local, mesh=mesh, in_specs=in_specs, out_specs=out_specs, check_vma=False)
```

time: 953 us -> 478 us (0.50)
  waiting for transfers between devices: 629 us -> 228 us
  matrix products: 141 us -> 0 us
  Pallas kernels: 0 us -> 137 us
  other arithmetic: 65.8 us -> 11 us
  local copies, waits for them, and re-layouts: 28.1 us -> 18 us
    reduce_scatter x5 -> x4, waiting for transfers between devices: 220 us -> 13.4 us  [the longest x1 13.4 us: local(): lax.psum_scatter(ffn, ('hidden', 'width'), scatter_dimension=0, tiled=True)]
    all_gather x6 -> x2, waiting for transfers between devices: 153 us -> 3.34 us  [the longest x1 3.32 us: local(): lax.all_gather(w_down, ('hidden', 'width'), axis=0)]
    dot_general x52 -> x0, matrix products: 141 us -> none  [the longest x20 65 us: outer_cols(): lax.dot_general(left, right, (((1,), (1,)), ((), ())), preferred_element_...]
    pallas_call x0 -> x3, Pallas kernels: none -> 137 us  [call(): pl.pallas_call(kernel, out_shape=[jax.ShapeDtypeStruct(shape, kind) for s...]
    psum x4 -> x3, waiting for transfers between devices: 255 us -> 208 us  [the longest x1 98.3 us: local(): gq_t, gkv_t = lax.psum((gq_t, gkv_t), every)]
    convert_element_type x11 -> x3, other arithmetic: 45.6 us -> 5.42 us  [the longest x1 1.86 us: local(): gwo.astype(F32)]
    reduce_sum x14 -> x0, other arithmetic: 18.9 us -> none  [the longest x4 5.11 us: head_forward(): total = jnp.sum(weights, 1, keepdims=True)]
    all_gather x6 -> x3, blocking collectives: 31.3 us -> 30.1 us  [the longest x1 11.9 us: local(): wout = lax.all_gather(w_out, 'width', axis=0, tiled=True)]
  transfers between devices with their start and end apart: 15 -> 9, of which waited for: 15 -> 5; matrix products, arithmetic and copies ran while one was open for 3% -> 5% of each run, Pallas kernels for 0% -> 25%
where the time goes in v1:
time: 478 us; the launch traced here: 477 us
  waiting for transfers between devices  228 us (48%)
  Pallas kernels  137 us (29%)
  blocking collectives  68.7 us (14%)
  local copies, waits for them, and re-layouts  18 us (4%)
  between operations  14 us (3%)
  other arithmetic  11 us (2%)
    pallas_call x3, Pallas kernels, call(): pl.pallas_call(kernel, out_shape=[jax.ShapeDtypeStruct(shape, kind) for s...  137 us
    psum x1, waiting for transfers between devices, local(): gq_t, gkv_t = lax.psum((gq_t, gkv_t), every)  98.3 us
    psum x1, waiting for transfers between devices, local(): lax.psum((lax.psum_scatter(gwo, 'width', scatter_dimension=0, tiled=True)...  90.9 us
    psum x1, blocking collectives, local(): vec = lax.psum(vecp_one + vecp_two, ('batch', 'hidden', 'width'))  38.6 us
    psum x1, waiting for transfers between devices, local(): lax.psum(lax.psum_scatter(ffn, ('hidden', 'width'), scatter_dimension=0,...  19.1 us
    reduce_scatter x1, waiting for transfers between devices, local(): lax.psum_scatter(ffn, ('hidden', 'width'), scatter_dimension=0, tiled=True)  13.4 us
    all_gather x1, blocking collectives, local(): wout = lax.all_gather(w_out, 'width', axis=0, tiled=True)  11.9 us
    all_gather x1, blocking collectives, local(): wg2 = lax.all_gather(gate2_weight, 'width', axis=0)  9.56 us
  transfers between devices with their start and end apart: 9, of which 5 were waited for; matrix products, arithmetic and copies ran while one was open for 5% of the time, Pallas kernels for 25%

profile of v1, /device:TPU:0, one launch (start us, length us, event | category | flops | bytes accessed | tf_op | source)
XLA Modules:
  0.0 477.5 jit_solution(14486563912882514075)
XLA Ops:
  7.2 0.0 all-gather.6.cloned.1.call-start
  7.2 0.7 all-gather.6.cloned.1.call-update
  7.9 0.0 all-gather.8.cloned.1.call-start
  8.0 0.7 all-gather.8.cloned.1.call-update
  8.7 0.0 reduce-scatter.5.cloned.1.call-start
  8.7 1.4 stack.29.refs_3_
  10.1 11.9 %all_gather.28.refs_7_ = bf16[512,512]{1,0:T(8,128)(2,1)} all-gather(bf16[256,512]{1,0:T(8,128)(2,1)} %param.23), channel_id=1, replica_groups=mesh['batch'=2,'hidden'=8,'width'=2] {'width'}, dimensions={0}, use_global_device_ids=true | all-gather | bytes 786432 | tf_op jit(solution)/shard_map/all_gather | solution.py:583
  22.0 8.7 %all-gather = bf16[1024,256]{1,0:T(8,128)(2,1)} all-gather(bf16[512,256]{1,0:T(8,128)(2,1)} %param.24), channel_id=2, replica_groups=mesh['batch'=2,'hidden'=8,'width'=2] {'width'}, dimensions={0}, use_global_device_ids=true | all-gather | bytes 786432 | tf_op jit(solution)/shard_map/all_gather | solution.py:581
  30.7 9.6 %all-gather.1 = bf16[1024,256]{1,0:T(8,128)(2,1)} all-gather(bf16[512,256]{1,0:T(8,128)(2,1)} %param.28), channel_id=3, replica_groups=mesh['batch'=2,'hidden'=8,'width'=2] {'width'}, dimensions={0}, use_global_device_ids=true | all-gather | bytes 786432 | tf_op jit(solution)/shard_map/all_gather | solution.py:582
  40.2 59.2 %shard_map.288 = (bf16[256,512]{1,0:T(8,128)(2,1)}, bf16[256,512]{1,0:T(8,128)(2,1)}, f32[8,512]{1,0:T(8,128)}, bf16[512,512]{1,0:T(8,128)(2,1)}, bf16[512,256]{...) custom-call(s32[1,3]{1,0:T(1,128)} %refs_0_.3, ...), custom_call_target="tpu_custom_call" | custom-call | flops 30000001024 | bytes 20000000 | tf_op jit(solution)/shard_map/pallas_call | solution.py:552
  99.4 0.0 all-gather.6.cloned.1.call-done
  99.5 3.3 all-gather.8.cloned.1.call-done
  102.8 17.4 %shard_map.289 = (bf16[256,512]{1,0:T(8,128)(2,1)}, bf16[512,256]{1,0:T(8,128)(2,1)}, bf16[8,512,256]{2,1,0:T(8,128)(2,1)}, bf16[8,512,256]{2,1,0:T(8,128)(2,1)}...) custom-call(bf16[256,512]{1,0:T(8,128)(2,1)} %get-tuple-element.43.r, ...), custom_call_target="tpu_custom_call" | custom-call | flops 10000000000 | bytes 20000000 | tf_op jit(solution)/shard_map/pallas_call | solution.py:552
  120.1 0.0 reduce-scatter.5.cloned.1.call-update
  120.2 0.0 reduce-scatter.7.cloned.1.call-start
  120.2 0.5 reduce-scatter.7.cloned.1.call-update
  120.7 0.0 reduce-scatter.9.cloned.1.call-start
  120.8 0.5 reduce-scatter.9.cloned.1.call-update
  121.3 0.0 reduce-scatter.11.cloned.1.call-start
  121.4 2.9 copy.40
  124.2 4.1 copy.41
  128.3 3.9 pad_maximum_fusion
  132.2 0.0 reduce-scatter.11.cloned.1.call-update
  132.2 0.0 all-reduce.8.cloned.1.call-start
  132.3 60.7 %shard_map.290 = (bf16[512,256]{1,0:T(8,128)(2,1)}, f32[512,256]{1,0:T(8,128)}, f32[256,512]{1,0:T(8,128)}, f32[512,512]{1,0:T(8,128)}, f32[8,512]{1,0:T(8,128)}) custom-call(s32[1,3]{1,0:T(1,128)} %refs_0_.3, bf16[512,256]{1,0:T(8,128)(2,1)} %get-tuple-element.48.refs_1_, bf16[8,128,512]{2,1,0:T(8,128)(2,1)} %get-tuple-element.49.refs_2_, ...), custom_call_target="tpu_custom_call" | custom-call | flops 40000000000 | bytes 20000000 | tf_op jit(solution)/shard_map/pallas_call | solution.py:552
  192.9 0.0 copy-start.3
  192.9 0.0 copy-start.4
  192.9 2.4 copy.39
  195.3 0.0 all-reduce.8.cloned.1.call-update
  195.3 0.0 all-reduce.10.cloned.1.call-start
  195.4 0.0 reduce-scatter.5.cloned.1.call-done
  195.4 0.0 reduce-scatter.7.cloned.1.call-done
  195.4 0.0 reduce-scatter.9.cloned.1.call-done
  195.5 0.6 all-reduce.10.cloned.1.call-update
  196.1 0.0 all-reduce.6.cloned.1.call-start
  196.1 0.0 copy-done.3
  196.2 0.0 copy-done.4
  196.2 38.6 %psum.49 = f32[8,512]{1,0:T(8,128)S(1)} all-reduce(f32[8,512]{1,0:T(8,128)S(1)} %add.28), channel_id=1, replica_groups=mesh['batch'=2,'hidden'=8,'width'=2] {'batch','hidden','width'}, use_global_device_ids=true, to_apply=%region_0.0 | all-reduce | flops 4096 | bytes 32768 | tf_op jit(solution)/shard_map/psum | solution.py:658
  234.8 0.7 fusion.1
  235.4 13.4 %reduce-scatter.11.cloned.1.call-done = bf16[1,256,512]{1,2,0:T(8,128)(2,1)} async-done(((bf16[16,256,512]{1,2,0:T(8,128)(2,1)}), bf16[1,256,512]{1,2,0:T(8,128)(2,1)}) %reduce-scatter.11.cloned.1.call-update) | async-done | bytes 262160 | tf_op jit(solution)/shard_map/reduce_scatter | solution.py:644
  248.8 0.0 all-reduce.6.cloned.1.call-update
  248.8 98.3 %all-reduce.8.cloned.1.call-done = (f32[512,256]{0,1:T(8,128)}, f32[4,2,64,512]{3,2,0,1:T(8,128)}) async-done(((f32[512,256]{0,1:T(8,128)}, f32[4,2,64,512]{3,2,0,1:T(8,128)}), (f32[512,256]{0,1:T(8,128)}, f32[4,2,64,512]{3,2,0,1:T(8,128)})) %all-reduce.8.cloned.1.call-update) | async-done | bytes 1572880 | tf_op jit(solution)/shard_map/psum | solution.py:657
  347.1 0.0 copy-start.1
  347.1 1.4 fusion
  348.5 1.0 copy.43
  349.5 1.0 copy.44
  350.5 0.0 copy-done.1
  350.5 1.0 copy.42
  351.5 0.0 copy-start.2
  351.5 90.9 %all-reduce.10.cloned.1.call-done = (bf16[256,512]{1,0:T(8,128)(2,1)}, bf16[512,256]{1,0:T(8,128)(2,1)}, bf16[512,256]{1,0:T(8,128)(2,1)}) async-done(((bf16[256,512]{1,0:T(8,128)(2,1)}, bf16[512,256]{1,0:T(8,128)(2,1)}, bf16[512,256]{1,0:T(8,128)(2,1)}), (bf16[256,512]{1,0:T(8,128)(2,1)}, bf16[512,256]{1,0:T(8,128)(2,1)}, bf16[512,256]{1,0:T(8,128)(2,1)})) %all-reduce.10.cloned.1.call-update) | async-done | bytes 786448 | tf_op jit(solution)/shard_map/psum | solution.py:649
  442.4 0.0 copy-start
  442.4 1.9 convert_element_type.13
  444.3 1.8 convert_element_type.14
  446.0 1.8 convert_element_type.15
  447.8 19.1 %all-reduce.6.cloned.1.call-done = bf16[256,512]{0,1:T(8,128)(2,1)} async-done(((bf16[256,512]{0,1:T(8,128)(2,1)}), bf16[256,512]{0,1:T(8,128)(2,1)}) %all-reduce.6.cloned.1.call-update) | async-done | bytes 262160 | tf_op jit(solution)/shard_map/psum | solution.py:644
  466.9 1.7 convert_bitcast_fusion
  468.6 0.8 copy.45
  469.4 0.0 copy-done.2
  469.4 0.7 copy.54
  470.2 0.0 copy-done
  470.2 0.8 copy.55
  (1 shorter events, 0.0 us)
Async XLA Ops:
  7.2 92.3 %all-gather.6.cloned.1.call-start = ((), (), s32[]{:S(2)}) async-start(), calls=%async_computation.4 | async-start | bytes 2228224 | tf_op jit(solution)/shard_map/all_gather | solution.py:579
  7.9 94.9 %all-gather.8.cloned.1.call-start = ((), (), s32[]{:S(2)}) async-start(), calls=%async_computation.10 | async-start | bytes 2228224 | tf_op jit(solution)/shard_map/all_gather | solution.py:580
  8.7 186.7 %reduce-scatter.5.cloned.1.call-start = ((), (), s32[]{:S(2)}) async-start(), calls=%async_computation.5 | async-start | bytes 786432 | tf_op jit(solution)/shard_map/reduce_scatter | solution.py:651
  120.2 75.3 %reduce-scatter.7.cloned.1.call-start = ((), (), s32[]{:S(2)}) async-start(), calls=%async_computation.6 | async-start | bytes 786432 | tf_op jit(solution)/shard_map/reduce_scatter | solution.py:652
  120.7 74.7 %reduce-scatter.9.cloned.1.call-start = ((), (), s32[]{:S(2)}) async-start(), calls=%async_computation.7 | async-start | bytes 786432 | tf_op jit(solution)/shard_map/reduce_scatter | solution.py:653
  121.3 127.5 %reduce-scatter.11.cloned.1.call-start = ((), (), s32[]{:S(2)}) async-start(), calls=%async_computation.8 | async-start | bytes 4456448 | tf_op jit(solution)/shard_map/reduce_scatter | solution.py:644
  132.2 214.9 %all-reduce.8.cloned.1.call-start = ((), (), s32[]{:S(2)}) async-start(), calls=%async_computation.11 | async-start | bytes 3145728 | tf_op jit(solution)/shard_map/psum | solution.py:657
  192.9 3.2 copy-start.3
  192.9 3.2 copy-start.4
  195.3 247.0 %all-reduce.10.cloned.1.call-start = ((), (), s32[]{:S(2)}) async-start(), calls=%async_computation.12 | async-start | bytes 1572864 | tf_op jit(solution)/shard_map/psum | solution.py:649
  196.1 270.8 %all-reduce.6.cloned.1.call-start = ((), (), s32[]{:S(2)}) async-start(), calls=%async_computation.9 | async-start | bytes 524288 | tf_op jit(solution)/shard_map/psum | solution.py:644
  347.1 3.4 copy-start.1
  351.5 118.0 %copy-start.2 = (bf16[512,256]{1,0:T(8,128)(2,1)S(1)}, bf16[512,256]{1,0:T(8,128)(2,1)}, u32[]{:S(2)}) copy-start(bf16[512,256]{1,0:T(8,128)(2,1)} %get-tuple-element.133) | copy-start | bytes 786436
  442.4 27.8 %copy-start = (f32[512,256]{1,0:T(8,128)S(1)}, f32[512,256]{1,0:T(8,128)}, u32[]{:S(2)}) copy-start(f32[512,256]{1,0:T(8,128)} %get-tuple-element.134) | copy-start | bytes 1572868
Sparse Core Ops, SparseCore 0:
  10.2 44.4 all-gather.5
  56.9 45.8 all-gather.7
  120.3 13.4 reduce-scatter.4
  136.5 15.0 reduce-scatter.6
  154.3 14.0 reduce-scatter.8
  172.6 76.1 reduce-scatter.10
  252.4 94.6 all-reduce.7
  350.8 91.5 all-reduce.9
  444.8 22.0 all-reduce.5

commit v2 on v0

v2 whole, which is shorter than its diff:
```python
import functools
import types

import jax
import jax.numpy as jnp
from jax import lax
from jax.experimental import pallas as pl
from jax.experimental.pallas import tpu as pltpu
from jax.sharding import PartitionSpec as P

HD = 64
EPSILON = 1e-05
MESH = pl.DeviceIdType.MESH
F32 = jnp.float32
BF16 = jnp.bfloat16
NEG = -1e30
VMEM_LIMIT = 62 * 1024 * 1024
SCALE = HD**-0.5


def nn(a, b):
    return lax.dot_general(a, b, (((1,), (0,)), ((), ())), preferred_element_type=F32)


def nt(a, b):
    return lax.dot_general(a, b, (((1,), (1,)), ((), ())), preferred_element_type=F32)


def flip(a):
    return a.astype(F32).T.astype(BF16)


def remote(src, dst, send, recv, dev):
    return pltpu.make_async_remote_copy(
        src_ref=src, dst_ref=dst, send_sem=send, recv_sem=recv, device_id=dev, device_id_type=MESH
    )


def await_copy(ref, sem):
    pltpu.make_async_copy(ref, ref, sem).wait()


def at(index, size):
    return pl.ds(pl.multiple_of(index * size, size), size)


def sub_row(index, sub, dph):
    return jnp.where(lax.rem(index, 2) == 0, sub, dph - 1 - sub)


def segments(pos, ends):
    total = jnp.zeros(pos.shape, jnp.int32)
    for end in ends:
        total = total + (pos >= end).astype(jnp.int32)
    return total


def allowed_mask(key_base, query_base, keys, queries, ends):
    key_pos = key_base + lax.broadcasted_iota(jnp.int32, (keys, 1), 0)
    query_pos = query_base + lax.broadcasted_iota(jnp.int32, (1, queries), 1)
    same = segments(key_pos, ends) == segments(query_pos, ends)
    return same & (key_pos <= query_pos)


def sigmoid(x):
    return 1.0 / (1.0 + jnp.exp(-x))


class Sends:
    def __init__(self):
        self.items = []

    def start(self, copy):
        copy.start()
        self.items.append((None, copy))

    def start_if(self, cond, copy):
        @pl.when(cond)
        def _():
            copy.start()

        self.items.append((cond, copy))

    def finish(self):
        for cond, copy in self.items:
            if cond is None:
                copy.wait_send()
            else:

                @pl.when(cond)
                def _(copy=copy):
                    copy.wait_send()


def layer_kernel(names, sizes, *refs):
    r = types.SimpleNamespace(**dict(zip(names, refs)))
    nb, nh, rows, cw, units, heads, dph, tq = sizes
    half, wide, nz = rows // 2, 2 * cw, nh // 2
    per = half // tq
    pairs = nb // 2
    b, h, w = lax.axis_index("batch"), lax.axis_index("hidden"), lax.axis_index("width")
    group, sub = lax.div(h, dph), lax.rem(h, dph)
    z, c, bp = lax.div(h, 2), lax.rem(h, 2), lax.rem(b, 2)
    x_dev = (b, h, 1 - w)
    c_dev = (b, h + 1 - 2 * c, w)
    y_dev = (b + 1 - 2 * bp, h, w)

    def z_dev(k):
        zz = lax.rem(z + k, nz)
        return zz, (b, 2 * zz + c, w)

    own, other = at(w, cw), at(1 - w, cw)
    mine, theirs = at(w, half), at(1 - w, half)
    lanes = at(c, half)
    ends = [
        r.lens[0, 0],
        r.lens[0, 0] + r.lens[0, 1],
        r.lens[0, 0] + r.lens[0, 1] + r.lens[0, 2],
    ]
    sends = Sends()

    barrier = pltpu.get_barrier_semaphore()
    count = 0
    for dw in range(2):
        for dh in range(nh):
            if dh or dw:
                dev = (b, lax.rem(h + dh, nh), lax.rem(w + dw, 2))
                pl.semaphore_signal(barrier, inc=1, device_id=dev, device_id_type=MESH)
                count += 1
    for db in range(1, nb):
        dev = (lax.rem(b + db, nb), h, w)
        pl.semaphore_signal(barrier, inc=1, device_id=dev, device_id_type=MESH)
        count += 1
    pl.semaphore_wait(barrier, count)

    for i, vec in enumerate((r.v0, r.v1, r.v2, r.v3, r.v4, r.v5)):
        r.vsrc[i : i + 1, :] = vec[...]
    vcopy = remote(r.vsrc, r.vecf.at[:, own], r.xs.at[0], r.xr.at[0], x_dev)
    sends.start(vcopy)
    tcopies = []
    for k in range(2):
        part = pl.ds(k * half, half)
        copy = remote(r.tok.at[part], r.tokf.at[part, own], r.xs.at[1 + k], r.xr.at[1 + k], x_dev)
        sends.start(copy)
        tcopies.append(copy)
    for kind, (src, dst) in enumerate(((r.wu, r.wup), (r.wd, r.wdn))):
        for k in range(nz - 1, 0, -1):
            _, dev = z_dev(k)
            copy = remote(src, dst.at[z, c, w], r.wzs.at[k], r.wzr.at[z], dev)
            sends.start_if(bp == kind, copy)
    ccopy = remote(r.cot.at[theirs], r.cotr.at[:, own], r.xs.at[3], r.xr.at[3], x_dev)
    sends.start(ccopy)
    gates = ((r.wg1, r.g1f), (r.wg2, r.g2f), (r.wo, r.wof))
    for i, (src, dst) in enumerate(gates):
        piece = at(c, src.shape[0] // 2)
        sends.start(remote(src.at[piece], dst.at[w, piece], r.gxs.at[i], r.gxr.at[i], x_dev))
        dst[w] = src[...]
    r.wup[z, c, w] = r.wu[...]
    r.wdn[z, c, w] = r.wd[...]
    r.vecf[:, own] = r.vsrc[...]
    r.tokf[:, own] = r.tok[...]
    r.cotr[:, own] = r.cot[mine, :]

    for i, weight in enumerate((r.wq, r.wk, r.wv)):
        turned = flip(weight[...])
        for t in range(heads):
            r.wt[t, i * HD : (i + 1) * HD, :] = turned[t * HD : (t + 1) * HD]

    vcopy.wait_recv()
    gain, shift = r.vecf[0:1, :], r.vecf[1:2, :]
    for k in range(2):
        part = slice(k * half, (k + 1) * half)
        tcopies[k].wait_recv()
        x = r.tokf[part, :].astype(F32)
        centre = x - jnp.mean(x, -1, keepdims=True)
        spread = jnp.mean(centre * centre, -1, keepdims=True)
        n = (centre * lax.rsqrt(spread + EPSILON) * gain + shift).astype(BF16)
        r.npair[c, part, :] = n
        for t in range(heads):
            qkv = nt(r.wt[t], n).astype(BF16)
            r.qsrc[t, :, part] = qkv[:HD]
            r.kvsrc[t, :, part] = qkv[HD:]
        for step in range(heads - 1, -1, -1):
            t = lax.rem(group + step, heads)
            span = pl.ds(k * half, half)
            src, dst = r.kvsrc.at[t, :, span], r.kvt.at[h, :, span]
            if step:
                dev = (b, t * dph + sub, w)
                sends.start(remote(src, dst, r.ks.at[step, k], r.kr.at[h, k], dev))
            else:
                pltpu.make_async_copy(src, dst, r.kr.at[h, k]).start()
            for i in range(per):
                row = k * per + i
                target = sub_row(h, row, dph)
                src, dst = r.qsrc.at[t, :, pl.ds(row * tq, tq)], r.qt.at[h]
                copy = remote(src, dst, r.qs.at[step, row], r.qr.at[h], (b, t * dph + target, w))
                if step:
                    sends.start(copy)
                else:
                    sends.start_if(target != sub, copy)

                    @pl.when(target == sub)
                    def _(src=src, dst=dst):
                        pltpu.make_async_copy(src, dst, r.qr.at[h]).start()

    sends.start(remote(r.npair.at[c], r.npair.at[c], r.cs.at[0], r.cr.at[0], c_dev))

    def weights_over_x():
        for kind, buf in enumerate((r.wup, r.wdn)):

            @pl.when(bp == kind)
            def _(buf=buf):
                for k in range(nz):
                    zz, _ = z_dev(k)
                    if k:
                        await_copy(buf.at[zz, c, w], r.wzr.at[zz])
                    block = buf.at[zz, c, w]
                    remote(block, block, r.wxs.at[zz], r.wxr.at[zz], x_dev).start()

    def weights_over_y():
        for kind, buf in enumerate((r.wup, r.wdn)):

            @pl.when(bp == kind)
            def _(buf=buf):
                for k in range(nz):
                    zz, _ = z_dev(k)
                    if k:
                        block = buf.at[zz, c, w]
                        remote(block, block, r.wys.at[zz, w], r.wyr.at[zz, w], y_dev).start()
                for k in range(nz):
                    zz, _ = z_dev(k)
                    block = buf.at[zz, c, 1 - w]
                    await_copy(block, r.wxr.at[zz])
                    remote(block, block, r.wys.at[zz, 1 - w], r.wyr.at[zz, 1 - w], y_dev).start()

    def weights_over_core():
        for kind, buf in enumerate((r.wup, r.wdn)):

            @pl.when(bp != kind)
            def _(buf=buf):
                for k in range(nz):
                    zz, _ = z_dev(k)
                    if k:
                        await_copy(buf.at[zz, c, w], r.wyr.at[zz, w])
                    await_copy(buf.at[zz, c, 1 - w], r.wyr.at[zz, 1 - w])

            block = buf.at[:, c]
            sends.start(remote(block, block, r.wcs.at[kind], r.wcr.at[kind], c_dev))
        for i, (src, dst) in enumerate(gates):
            piece = dst.at[1 - w, at(c, src.shape[0] // 2)]
            await_copy(piece, r.gxr.at[i])
            sends.start(remote(piece, piece, r.gcs.at[i], r.gcr.at[i], c_dev))

    def weights_sent():
        for kind, buf in enumerate((r.wup, r.wdn)):

            @pl.when(bp == kind)
            def _(buf=buf):
                for k in range(nz):
                    zz, _ = z_dev(k)
                    if k:
                        await_copy(buf.at[zz, c, w], r.wys.at[zz, w])
                    await_copy(buf.at[zz, c, w], r.wxs.at[zz])
                    await_copy(buf.at[zz, c, w], r.wys.at[zz, 1 - w])

    def pass_on(s):
        @pl.when(lax.rem(s, dph) == sub)
        def _():
            for k in range(2):
                await_copy(r.kvt.at[s, :, pl.ds(k * half, half)], r.kr.at[s, k])
            for k in range(1, dph):
                dev = (b, group * dph + lax.rem(sub + k, dph), w)
                remote(r.kvt.at[s], r.kvt.at[s], r.fs.at[s, k], r.fr.at[s], dev).start()

    def query_forward(s, _):
        @pl.when(s + 1 < nh)
        def _():
            pass_on(s + 1)

        @pl.when(lax.rem(s, dph) != sub)
        def _():
            await_copy(r.kvt.at[s], r.fr.at[s])

        r.kvn[s] = flip(r.kvt[s])
        await_copy(r.qt.at[s], r.qr.at[s])
        row = sub_row(s, sub, dph)
        query_base = s * rows + row * tq
        q = r.qt[s].astype(F32) * SCALE
        q = jnp.concatenate([q, jnp.zeros_like(q)], 0).astype(BF16)

        def masked(j, scores):
            return jnp.where(allowed_mask(j * rows, query_base, rows, tq, ends), scores, NEG)

        def absorb(j, scores, carry):
            top, total, mixed = carry
            new_top = jnp.maximum(top, jnp.max(scores, 0, keepdims=True))
            fade = jnp.exp(top - new_top)
            weights = jnp.exp(scores - new_top)
            total = total * fade + jnp.sum(weights, 0, keepdims=True)
            mixed = mixed * fade + nn(r.kvt[j, HD:, :], weights.astype(BF16))
            return new_top, total, mixed

        def plain_step(j, carry):
            scores = r.sbuf[lax.rem(j, 2)]
            r.sbuf[lax.rem(j + 1, 2)] = nn(r.kvn[j + 1], q)
            return absorb(j, scores, carry)

        def masked_step(j, carry):
            scores = masked(j, r.sbuf[lax.rem(j, 2)])
            r.sbuf[lax.rem(j + 1, 2)] = nn(r.kvn[j + 1], q)
            return absorb(j, scores, carry)

        r.sbuf[0] = masked(0, nn(r.kvn[0], q))
        plain = jnp.where(s == nh - 1, 0, s)
        carry = (jnp.full((1, tq), NEG, F32), jnp.zeros((1, tq), F32), jnp.zeros((HD, tq), F32))
        carry = lax.fori_loop(0, plain, plain_step, carry)
        carry = lax.fori_loop(plain, s, masked_step, carry)
        top, total, mixed = absorb(s, masked(s, r.sbuf[lax.rem(s, 2)]), carry)
        mixed = mixed / total
        r.ot[s] = mixed
        r.lse[s] = top + jnp.log(total)
        r.osend[s] = mixed.astype(BF16)
        row_w = lax.div(row * tq, half)
        lane = lax.rem(row * tq, half)
        dst = r.att.at[at(w * heads + group, HD), pl.ds(pl.multiple_of(lane, tq), tq)]
        slot = r.orc.at[w * heads + group, lax.div(lane, tq)]
        here = (s == h) & (row_w == w)

        @pl.when(here)
        def _():
            pltpu.make_async_copy(r.osend.at[s], dst, slot).start()

        @pl.when(jnp.logical_not(here))
        def _():
            remote(r.osend.at[s], dst, r.osd.at[s], slot, (b, s, row_w)).start()

        @pl.when(s == nh // 4)
        def _():
            weights_over_x()

        @pl.when(s == nh // 2)
        def _():
            weights_over_y()

        return 0

    pass_on(0)
    lax.fori_loop(0, nh, query_forward, 0)
    weights_over_core()

    for i, (src, dst) in enumerate(gates):
        await_copy(dst.at[1 - w, at(1 - c, src.shape[0] // 2)], r.gcr.at[i])

    def two(a, weight):
        return jnp.concatenate([nn(a, weight[0]), nn(a, weight[1])], 1)

    def two_back(g, weight):
        return nt(g[:, :cw], weight[0]) + nt(g[:, cw:], weight[1])

    tok = r.tokf[mine, :].astype(F32)
    n1 = r.npair[c, mine, :]
    gate_one = sigmoid(two(n1, r.g1f) + r.vecf[2:3, :])
    for g in range(2 * heads):
        for i in range(per):
            await_copy(r.att.at[pl.ds(g * HD, HD), pl.ds(i * tq, tq)], r.orc.at[g, i])
    wof = r.wof[...].reshape(wide, wide)
    branch_one = nn(flip(r.att[...]), wof)
    middle = tok + gate_one * (branch_one - tok)
    centre = middle - jnp.mean(middle, -1, keepdims=True)
    rstd = lax.rsqrt(jnp.mean(centre * centre, -1, keepdims=True) + EPSILON)
    n2 = centre * rstd
    gain_two = r.vecf[3:4, :]
    normed_two = (n2 * gain_two + r.vecf[4:5, :]).astype(BF16)
    gate_two = sigmoid(two(normed_two, r.g2f) + r.vecf[5:6, :])
    for kind, buf in enumerate((r.wup, r.wdn)):
        await_copy(buf.at[:, 1 - c], r.wcr.at[kind])

    def units_of(i2, p):
        return i2, lax.rem(c + p, 2)

    def up(i2, branch):
        for p in range(2):
            i, q = units_of(i2, p)
            pre = nn(normed_two, r.wup[i, q].reshape(wide, units))
            r.pre[i2, p] = pre
            act = jax.nn.gelu(pre).astype(BF16)
            branch = branch + jnp.concatenate([nn(act, r.wdn[i, q, 0]), nn(act, r.wdn[i, q, 1])], 1)
            if p:
                r.acts[i2] = act
                dst = r.actp.at[i2, lanes, :]
                remote(r.acts.at[i2], dst, r.as_.at[i2], r.ar.at[i2], c_dev).start()
            else:
                r.actp[i2, lanes, :] = act
        return branch

    branch_two = lax.fori_loop(0, nz, up, jnp.zeros(middle.shape, F32))
    delta = branch_two - middle
    r.outr[...] = (middle + gate_two * delta).astype(BF16)
    ocopy = remote(r.outr.at[:, other], r.out_c.at[mine, :], r.xs.at[4], r.xr.at[4], x_dev)
    sends.start(ocopy)
    ccopy.wait_recv()
    grad = r.cotr[...].astype(F32)
    gb2 = (grad * gate_two).astype(BF16)
    gl2 = (grad * delta * gate_two * (1.0 - gate_two)).astype(BF16)
    gmid = grad * (1.0 - gate_two)

    def down(i2, total):
        for p in range(2):
            i, q = units_of(i2, p)
            ghid = nt(gb2[:, :cw], r.wdn[i, q, 0]) + nt(gb2[:, cw:], r.wdn[i, q, 1])
            pre = r.pre[i2, p]
            k = 0.7978845608028654
            t = jnp.tanh(k * (pre + 0.044715 * pre * pre * pre))
            slope = 0.5 * (1.0 + t) + 0.5 * pre * (1.0 - t * t) * (k * (1.0 + 3 * 0.044715 * pre * pre))
            gpre = (ghid * slope).astype(BF16)
            total = total + nt(gpre, r.wup[i, q].reshape(wide, units))
            if p:
                r.gpres[i2] = gpre
                dst = r.gprep.at[i2, lanes, :]
                remote(r.gpres.at[i2], dst, r.ps_.at[i2], r.pr.at[i2], c_dev).start()
            else:
                r.gprep[i2, lanes, :] = gpre
        return total

    gnorm = lax.fori_loop(0, nz, down, two_back(gl2, r.g2f))
    e = gnorm * gain_two
    gmid = gmid + rstd * (
        e - jnp.mean(e, -1, keepdims=True) - n2 * jnp.mean(e * n2, -1, keepdims=True)
    )
    gb1 = (gmid * gate_one).astype(BF16)
    r.gatt[...] = nt(wof, gb1).astype(BF16)
    for dw in (1, 0):
        wt = lax.rem(w + dw, 2)
        for step in range(heads - 1, -1, -1):
            t = lax.rem(group + step, heads)
            for i in range(per):
                target = sub_row(h, w * per + i, dph)
                src = r.gatt.at[at(wt * heads + t, HD), pl.ds(i * tq, tq)]
                dst = r.dot.at[h]
                dev = (b, t * dph + target, wt)
                copy = remote(src, dst, r.ds.at[dw, step, i], r.dr.at[h], dev)
                if step or dw:
                    sends.start(copy)
                else:
                    sends.start_if(target != sub, copy)

                    @pl.when(target == sub)
                    def _(src=src, dst=dst):
                        pltpu.make_async_copy(src, dst, r.dr.at[h]).start()

    gl1 = (gmid * (branch_one - tok) * gate_one * (1.0 - gate_one)).astype(BF16)
    r.ginp[...] = gmid * (1.0 - gate_one)
    r.npt[:, lanes] = flip(normed_two)
    sends.start(remote(r.npt.at[:, lanes], r.npt.at[:, lanes], r.cs.at[1], r.cr.at[1], c_dev))
    r.gbt[:, lanes] = flip(gb2)
    sends.start(remote(r.gbt.at[:, lanes], r.gbt.at[:, lanes], r.cs.at[2], r.cr.at[2], c_dev))
    quarter = half // 2
    r.lsrc[0] = r.att[...]
    r.lsrc[1] = flip(gl1)
    r.lsrc[2] = flip(gl2)
    for m, right in enumerate((gb1, n1, normed_two)):
        r.bpair[m, lanes, :] = right
        block = r.bpair.at[m, lanes, :]
        sends.start(remote(block, block, r.cs.at[3 + m], r.cr.at[3 + m], c_dev))
        for v in range(2):
            src = r.lsrc.at[m, at(2 * v + 1 - c, quarter), :]
            dst = r.apair.at[m, v, :, lanes]
            sends.start(remote(src, dst, r.cs.at[6 + 2 * m + v], r.cr.at[6 + 2 * m + v], c_dev))
            r.apair[m, v, :, lanes] = r.lsrc[m, at(2 * v + c, quarter), :]
    r.gterm[...] = two_back(gl1, r.g1f)
    r.vsum[...] = jnp.zeros_like(r.vsum)
    r.vsum[2:3, :] = jnp.sum(gl1.astype(F32), 0, keepdims=True)
    r.vsum[3:4, :] = jnp.sum(gnorm * n2, 0, keepdims=True)
    r.vsum[4:5, :] = jnp.sum(gnorm, 0, keepdims=True)
    r.vsum[5:6, :] = jnp.sum(gl2.astype(F32), 0, keepdims=True)
    r.out_c[mine, :] = r.outr[:, own]

    eighth = quarter // 2
    for m in range(3):
        await_copy(r.bpair.at[m, lanes, :], r.cr.at[3 + m])
        for v in range(2):
            await_copy(r.apair.at[m, v, :, lanes], r.cr.at[6 + 2 * m + v])
            block = nn(r.apair[m, v], r.bpair[m]).astype(BF16)
            for y in range(2):
                r.gb[v, y, m * eighth : (m + 1) * eighth, :] = block[y * eighth : (y + 1) * eighth]
    sends.start(remote(r.gb.at[:, 1 - bp], r.ybin, r.ys.at[0], r.yr.at[0], y_dev))
    await_copy(r.npt.at[:, lanes], r.cr.at[1])
    await_copy(r.gbt.at[:, lanes], r.cr.at[2])

    def weight_grads(i2, _):
        await_copy(r.gprep.at[i2, lanes, :], r.pr.at[i2])
        await_copy(r.actp.at[i2, lanes, :], r.ar.at[i2])
        r.ga[0, i2] = nn(r.npt[...], r.gprep[i2]).astype(BF16).reshape(2, 2, quarter, units)
        r.ga[1, i2] = nn(r.gbt[...], r.actp[i2]).astype(BF16).reshape(2, 2, quarter, units)
        return 0

    lax.fori_loop(0, nz, weight_grads, 0)
    sends.start(remote(r.ga.at[0, :, 1 - w], r.xin0, r.xs.at[5], r.xr.at[5], x_dev))
    sends.start(remote(r.ga.at[1, :, :, 1 - bp], r.yin1, r.ys.at[1], r.yr.at[1], y_dev))

    def ffn_second():
        await_copy(r.xin0, r.xr.at[5])
        r.ga[0, :, w] = (r.ga[0, :, w].astype(F32) + r.xin0[...].astype(F32)).astype(BF16)
        remote(r.ga.at[0, :, w, 1 - bp], r.yin0, r.ys.at[2], r.yr.at[2], y_dev).start()
        await_copy(r.yin1, r.yr.at[1])
        r.ga[1, :, :, bp] = (r.ga[1, :, :, bp].astype(F32) + r.yin1[...].astype(F32)).astype(BF16)
        remote(r.ga.at[1, :, 1 - w, bp], r.xin1, r.xs.at[6], r.xr.at[6], x_dev).start()

    def ffn_third():
        await_copy(r.yin0, r.yr.at[2])
        await_copy(r.xin1, r.xr.at[6])
        r.zs[:, 0] = (r.ga[0, :, w, bp].astype(F32) + r.yin0[...].astype(F32)).astype(BF16)
        r.zs[:, 1] = (r.ga[1, :, w, bp].astype(F32) + r.xin1[...].astype(F32)).astype(BF16)
        for k in range(nz - 1, 0, -1):
            zz, dev = z_dev(k)
            remote(r.zs.at[zz], r.zin.at[z], r.zss.at[k], r.zsr.at[z], dev).start()
        r.zin[z] = r.zs[z]

    def ffn_fourth():
        for k in range(1, nz):
            zz, _ = z_dev(k)
            await_copy(r.zin.at[zz], r.zsr.at[zz])
        total = r.zin[0].astype(F32)
        for k in range(1, nz):
            total = total + r.zin[k].astype(F32)
        if pairs > 1:
            mypair = lax.div(b, 2)
            r.pin[mypair] = total.astype(BF16)
            for k in range(1, pairs):
                dev = (lax.rem(b + 2 * k, nb), h, w)
                block = r.pin.at[mypair]
                sends.start(remote(block, block, r.pas.at[k], r.par.at[mypair], dev))
            for k in range(1, pairs):
                pp = lax.rem(mypair + k, pairs)
                await_copy(r.pin.at[pp], r.par.at[pp])
            total = r.pin[0].astype(F32)
            for k in range(1, pairs):
                total = total + r.pin[k].astype(F32)
        r.red_a[bp] = total.astype(BF16)
        block = r.red_a.at[bp]
        sends.start(remote(block, block, r.ys.at[3], r.yr.at[3], y_dev))

    def ffn_sent():
        await_copy(r.yin0, r.ys.at[2])
        await_copy(r.xin1, r.xs.at[6])
        for k in range(1, nz):
            await_copy(r.zin.at[z], r.zss.at[k])

    deep = (heads // 2) * 3 * HD // 2
    zr = deep * 4 // nz

    def z_part(zz):
        return pl.ds(pl.multiple_of(lax.div(zz, 4) * zr, zr), zr), at(lax.rem(zz, 4), 128)

    def square_x():
        await_copy(r.ybin, r.yr.at[0])
        r.gb[:, bp] = (r.gb[:, bp].astype(F32) + r.ybin[...].astype(F32)).astype(BF16)
        remote(r.gb.at[1 - w, bp], r.xbin, r.xs.at[7], r.xr.at[7], x_dev).start()

    def square_z(which):
        if which == 0:
            await_copy(r.xbin, r.xr.at[7])
            total = r.gb[w, bp].astype(F32) + r.xbin[...].astype(F32)
        else:
            await_copy(r.ycin, r.yr.at[4])
            total = r.gc[bp].astype(F32) + r.ycin[...].astype(F32)
        r.sq[which] = total.astype(BF16)
        for k in range(nz - 1, 0, -1):
            zz, dev = z_dev(k)
            src = r.sq.at[(which,) + z_part(zz)]
            remote(src, r.sqin.at[which, z], r.sqs.at[which, k], r.sqr.at[which, z], dev).start()

    def square_spread(which):
        total = r.sq[(which,) + z_part(z)].astype(F32)
        r.sqin[which, z] = total.astype(BF16)
        for k in range(1, nz):
            zz, _ = z_dev(k)
            await_copy(r.sqin.at[which, zz], r.sqr.at[which, zz])
        total = r.sqin[which, 0].astype(F32)
        for k in range(1, nz):
            total = total + r.sqin[which, k].astype(F32)
        if pairs > 1:
            mypair = lax.div(b, 2)
            r.sqpair[which, mypair] = total.astype(BF16)
            for k in range(1, pairs):
                dev = (lax.rem(b + 2 * k, nb), h, w)
                block = r.sqpair.at[which, mypair]
                remote(block, block, r.sqps.at[which, k], r.sqpr.at[which, mypair], dev).start()
            for k in range(1, pairs):
                pp = lax.rem(mypair + k, pairs)
                await_copy(r.sqpair.at[which, pp], r.sqpr.at[which, pp])
            total = r.sqpair[which, 0].astype(F32)
            for k in range(1, pairs):
                total = total + r.sqpair[which, k].astype(F32)
        r.red_s[(which, c, bp) + z_part(z)] = total.astype(BF16)
        for k in range(nz - 1, 0, -1):
            _, dev = z_dev(k)
            block = r.red_s.at[(which, c, bp) + z_part(z)]
            remote(block, block, r.sgs.at[which, k], r.sgr.at[which, z], dev).start()

    def square_y(which):
        for k in range(1, nz):
            zz, _ = z_dev(k)
            await_copy(r.red_s.at[(which, c, bp) + z_part(zz)], r.sgr.at[which, zz])
        block = r.red_s.at[which, c, bp]
        remote(block, block, r.sys.at[which], r.syr.at[which], y_dev).start()

    def square_core(which):
        await_copy(r.red_s.at[which, c, 1 - bp], r.syr.at[which])
        block = r.red_s.at[which, c]
        remote(block, block, r.scs.at[which], r.scr.at[which], c_dev).start()

    def square_end(which):
        await_copy(r.red_s.at[which, 1 - c], r.scr.at[which])
        await_copy(r.red_s.at[which, c], r.scs.at[which])
        await_copy(r.red_s.at[which, c, bp], r.sys.at[which])
        for k in range(1, nz):
            await_copy(r.sqin.at[which, z], r.sqs.at[which, k])
            await_copy(r.sqin.at[which, z], r.sgs.at[which, k])
            if k < pairs:
                await_copy(r.sqpair.at[which, 0], r.sqps.at[which, k])

    r.acc[...] = jnp.zeros_like(r.acc)

    def finish(s):
        @pl.when(lax.rem(s, dph) == sub)
        def _():
            total = r.acc[s]
            for k in range(1, dph):
                slot = r.pin_kv.at[lax.div(s, dph), k - 1]
                await_copy(slot, r.pkr.at[lax.div(s, dph), k - 1])
                total = total + r.pin_kv[lax.div(s, dph), k - 1]
            r.dkvsend[s] = total.astype(BF16)
            dst = r.dqkv.at[group, pl.ds(HD, 2 * HD), :]

            @pl.when(s == h)
            def _():
                pltpu.make_async_copy(r.dkvsend.at[s], dst, r.dkr.at[group]).start()

            @pl.when(s != h)
            def _():
                remote(r.dkvsend.at[s], dst, r.dks.at[s], r.dkr.at[group], (b, s, w)).start()

    def query_backward(step, _):
        s = nh - 1 - step
        row = sub_row(s, sub, dph)
        query_base = s * rows + row * tq
        await_copy(r.dot.at[s], r.dr.at[s])
        q = r.qt[s]
        dout = r.dot[s]
        q_low = jnp.concatenate([q.astype(F32) * SCALE, jnp.zeros((HD, tq), F32)], 0).astype(BF16)
        d_high = jnp.concatenate([jnp.zeros((HD, tq), BF16), dout], 0)
        log_sum = r.lse[s]
        centre = jnp.sum(r.ot[s] * dout.astype(F32), 0, keepdims=True)

        def block(j, dq, masked):
            scores = nn(r.kvn[j], q_low)
            if masked:
                scores = jnp.where(allowed_mask(j * rows, query_base, rows, tq, ends), scores, NEG)
            probs = jnp.exp(scores - log_sum)
            gprobs = nn(r.kvn[j], d_high)
            gscores = (probs * (gprobs - centre)).astype(BF16)
            r.acc[j, HD:, :] += nt(dout, probs.astype(BF16))
            r.acc[j, :HD, :] += nt(q, gscores) * SCALE
            return dq + nn(r.kvt[j, :HD, :], gscores)

        plain_end = jnp.where(s == nh - 1, 1, jnp.maximum(s, 1))
        dq = jnp.zeros((HD, tq), F32)
        dq = lax.fori_loop(1, plain_end, lambda j, d: block(j, d, False), dq)
        count = 1 + jnp.where(s > 0, s + 1 - plain_end, 0)

        def with_mask(t, d):
            return block(jnp.where(t == 0, 0, plain_end + t - 1), d, True)

        dq = lax.fori_loop(0, count, with_mask, dq)
        r.dqsend[s] = (dq * SCALE).astype(BF16)
        dst = r.dqkv.at[group, pl.ds(0, HD), pl.ds(pl.multiple_of(row * tq, tq), tq)]

        @pl.when(s == h)
        def _():
            pltpu.make_async_copy(r.dqsend.at[s], dst, r.dqr.at[group, row]).start()

        @pl.when(s != h)
        def _():
            remote(r.dqsend.at[s], dst, r.dqs.at[s], r.dqr.at[group, row], (b, s, w)).start()

        owner = lax.rem(s, dph)

        @pl.when(owner != sub)
        def _():
            k = lax.rem(sub - owner + dph, dph)
            dev = (b, group * dph + owner, w)
            slot = lax.div(s, dph)
            remote(r.acc.at[s], r.pin_kv.at[slot, k - 1], r.pks.at[s], r.pkr.at[slot, k - 1], dev).start()

        @pl.when(step > 0)
        def _():
            finish(s + 1)

        unit = nh // 8

        @pl.when(step == 2 * unit)
        def _():
            square_x()
            ffn_second()

        @pl.when(step == 4 * unit)
        def _():
            square_z(0)
            ffn_third()

        @pl.when(step == 6 * unit)
        def _():
            square_spread(0)

        return 0

    lax.fori_loop(0, nh, query_backward, 0)
    finish(0)

    for t in range(heads):
        await_copy(r.dqkv.at[t, pl.ds(HD, 2 * HD), :], r.dkr.at[t])
        for i in range(dph):
            await_copy(r.dqkv.at[t, pl.ds(0, HD), pl.ds(i * tq, tq)], r.dqr.at[t, i])
        sends.start_if(
            t % 2 != c, remote(r.dqkv.at[t], r.dsib.at[t // 2], r.ts.at[t], r.tr.at[t // 2], c_dev)
        )
    wts = r.wt[...].reshape(heads * 3 * HD, wide)

    def grad_normed(span):
        return nn(flip(r.dqkv[:, :, span].reshape(heads * 3 * HD, half)), wts)

    r.psend[...] = grad_normed(theirs).astype(BF16)
    pcopy = remote(r.psend, r.precv, r.xs.at[8], r.xr.at[8], x_dev)
    sends.start(pcopy)
    await_copy(r.npair.at[1 - c], r.cr.at[0])
    for j in range(heads // 2):
        await_copy(r.dsib.at[j], r.tr.at[j])
        part = nn(r.dqkv[2 * j + c], r.npair[c]) + nn(r.dsib[j], r.npair[1 - c])
        span = slice((j % (heads // 4)) * 3 * HD, (j % (heads // 4) + 1) * 3 * HD)
        r.gc[j // (heads // 4), span, :] = part.astype(BF16)
    sends.start(remote(r.gc.at[1 - bp], r.ycin, r.ys.at[4], r.yr.at[4], y_dev))
    gnorm = grad_normed(mine) + r.gterm[...]
    x = r.tokf[mine, :].astype(F32)
    centre = x - jnp.mean(x, -1, keepdims=True)
    rstd = lax.rsqrt(jnp.mean(centre * centre, -1, keepdims=True) + EPSILON)
    n = centre * rstd
    square_y(0)
    ffn_fourth()
    square_z(1)
    pcopy.wait_recv()
    gnorm = gnorm + r.precv[...].astype(F32)
    e = gnorm * r.vecf[0:1, :]
    result = r.ginp[...] + rstd * (
        e - jnp.mean(e, -1, keepdims=True) - n * jnp.mean(e * n, -1, keepdims=True)
    )
    r.tsend[...] = result.astype(BF16)
    tcopy = remote(r.tsend.at[:, other], r.trecv, r.xs.at[9], r.xr.at[9], x_dev)
    sends.start(tcopy)
    r.vsum[0:1, :] = jnp.sum(gnorm * n, 0, keepdims=True)
    r.vsum[1:2, :] = jnp.sum(gnorm, 0, keepdims=True)
    me4 = 2 * c + w
    r.vin4[me4] = r.vsum[...]
    k = 0
    for dc in range(2):
        for dw in range(2):
            if dc or dw:
                cc, ww = lax.rem(c + dc, 2), lax.rem(w + dw, 2)
                dev = (b, 2 * z + cc, ww)
                sends.start(remote(r.vin4.at[me4], r.vin4.at[me4], r.v4s.at[k], r.v4r.at[me4], dev))
                k += 1
    r.gtok[mine, :] = jnp.where(w == 0, result[:, :cw], result[:, cw:])
    square_core(0)
    square_spread(1)
    for dc in range(2):
        for dw in range(2):
            if dc or dw:
                peer = 2 * lax.rem(c + dc, 2) + lax.rem(w + dw, 2)
                await_copy(r.vin4.at[peer], r.v4r.at[peer])
    r.vinz[z] = r.vin4[0] + r.vin4[1] + r.vin4[2] + r.vin4[3]
    for k in range(1, nz):
        _, dev = z_dev(k)
        sends.start(remote(r.vinz.at[z], r.vinz.at[z], r.vzs.at[k], r.vzr.at[z], dev))
    tcopy.wait_recv()
    r.gtok[theirs, :] = r.trecv[...].astype(F32)
    ocopy.wait_recv()
    for k in range(1, nz):
        zz, _ = z_dev(k)
        await_copy(r.vinz.at[zz], r.vzr.at[zz])
    total = r.vinz[0]
    for k in range(1, nz):
        total = total + r.vinz[k]
    r.vinb[b] = total
    for k in range(1, nb):
        dev = (lax.rem(b + k, nb), h, w)
        sends.start(remote(r.vinb.at[b], r.vinb.at[b], r.vbs.at[k], r.vbr.at[b], dev))
    square_y(1)
    for k in range(1, nb):
        bb = lax.rem(b + k, nb)
        await_copy(r.vinb.at[bb], r.vbr.at[bb])
    total = r.vinb[0]
    for k in range(1, nb):
        total = total + r.vinb[k]
    r.red_v[...] = jnp.where(w == 0, total[:, :cw], total[:, cw:])
    await_copy(r.red_a.at[1 - bp], r.yr.at[3])
    square_core(1)

    def sent(s, _):
        row = sub_row(s, sub, dph)
        here = (s == h) & (lax.div(row * tq, half) == w)

        @pl.when(jnp.logical_not(here))
        def _():
            await_copy(r.osend.at[s], r.osd.at[s])

        @pl.when(lax.rem(s, dph) == sub)
        def _():
            for k in range(1, dph):
                await_copy(r.kvt.at[s], r.fs.at[s, k])

        @pl.when(s != h)
        def _():
            await_copy(r.dqsend.at[s], r.dqs.at[s])

        @pl.when((s != h) & (lax.rem(s, dph) == sub))
        def _():
            await_copy(r.dkvsend.at[s], r.dks.at[s])

        @pl.when(lax.rem(s, dph) != sub)
        def _():
            await_copy(r.acc.at[s], r.pks.at[s])

        return 0

    lax.fori_loop(0, nh, sent, 0)
    weights_sent()
    for i2 in range(nz):
        await_copy(r.acts.at[i2], r.as_.at[i2])
        await_copy(r.gpres.at[i2], r.ps_.at[i2])
    ffn_sent()
    await_copy(r.xbin, r.xs.at[7])
    sends.finish()
    square_end(0)
    square_end(1)


def final_kernel(heads, *refs):
    (
        out_c, gtok, red_a, red_s, red_v,
        o_out, o_tok, o_g1, o_b1, o_wq, o_wk, o_wv, o_wo, o_gw1, o_gb1, o_g2, o_b2, o_gw2, o_gb2, o_up, o_dn,
    ) = refs
    o_out[...] = out_c[...]
    o_tok[...] = gtok[...]
    for i, ref in enumerate((o_g1, o_b1, o_gb1, o_g2, o_b2, o_gb2)):
        ref[...] = red_v[i : i + 1, :]
    _, quarter, units = red_a.shape[1:]
    o_up[:quarter, :] = red_a[0, 0].astype(F32)
    o_up[quarter:, :] = red_a[1, 0].astype(F32)
    o_dn[:, :quarter] = red_a[0, 1].astype(F32).T
    o_dn[:, quarter:] = red_a[1, 1].astype(F32).T
    eighth = quarter // 2
    for core in range(2):
        for y in range(2):
            base = (2 * core + y) * eighth
            o_wo[base : base + eighth, :] = red_s[0, core, y, :eighth, :].astype(F32)
    for m, ref in ((1, o_gw1), (2, o_gw2)):
        full = [red_s[0, core, y, m * eighth : (m + 1) * eighth, :] for core in range(2) for y in range(2)]
        ref[...] = jnp.concatenate(full, 0).astype(F32).T
    for i, ref in enumerate((o_wq, o_wk, o_wv)):
        full = []
        for t in range(heads):
            j, core = t // 2, t % 2
            base = (j % (heads // 4)) * 3 * HD + i * HD
            full.append(red_s[1, core, j // (heads // 4), base : base + HD, :])
        ref[...] = jnp.concatenate(full, 0).astype(F32).T


def local(
    tokens, ln1_gain, ln1_bias, w_query, w_key, w_value, w_out, gate1_weight, gate1_bias,
    ln2_gain, ln2_bias, gate2_weight, gate2_bias, w_up, w_down, lengths, cotangent,
):
    nb, nh = lax.axis_size("batch"), lax.axis_size("hidden")
    rows, cw = tokens.shape
    units = w_up.shape[1]
    heads = cw // HD
    dph = nh // heads
    tq, half, wide, nz, pairs = rows // dph, rows // 2, 2 * cw, nh // 2, nb // 2
    quarter = half // 2
    deep = (heads // 2) * 3 * HD // 2
    zr = deep * 4 // nz
    per = half // tq
    sizes = (nb, nh, rows, cw, units, heads, dph, tq)

    ins = dict(
        lens=lengths, tok=tokens, cot=cotangent, v0=ln1_gain[None], v1=ln1_bias[None], v2=gate1_bias[None],
        v3=ln2_gain[None], v4=ln2_bias[None], v5=gate2_bias[None], wq=w_query, wk=w_key, wv=w_value,
        wo=w_out, wg1=gate1_weight, wg2=gate2_weight, wu=w_up, wd=w_down,
    )
    outs = dict(
        out_c=((rows, cw), BF16),
        gtok=((rows, cw), F32),
        red_a=((2, 2, quarter, units), BF16),
        red_s=((2, 2, 2, deep, wide), BF16),
        red_v=((8, cw), F32),
    )
    bufs = dict(
        vsrc=((8, cw), F32), vecf=((8, wide), F32), tokf=((rows, wide), BF16), cotr=((half, wide), BF16),
        g1f=((2, wide, cw), BF16), g2f=((2, wide, cw), BF16), wof=((2, cw, wide), BF16),
        wup=((nz, 2, 2, cw, units), BF16), wdn=((nz, 2, 2, units, cw), BF16),
        wt=((heads, 3 * HD, wide), BF16), npair=((2, rows, wide), BF16),
        qsrc=((heads, HD, rows), BF16), kvsrc=((heads, 2 * HD, rows), BF16),
        kvt=((nh, 2 * HD, rows), BF16), kvn=((nh, rows, 2 * HD), BF16), qt=((nh, HD, tq), BF16),
        sbuf=((2, rows, tq), F32), ot=((nh, HD, tq), F32), lse=((nh, 1, tq), F32), osend=((nh, HD, tq), BF16),
        att=((2 * heads * HD, half), BF16),
        pre=((nz, 2, half, units), F32), acts=((nz, half, units), BF16), actp=((nz, rows, units), BF16),
        gpres=((nz, half, units), BF16), gprep=((nz, rows, units), BF16),
        outr=((half, wide), BF16), gatt=((wide, half), BF16), dot=((nh, HD, tq), BF16),
        ginp=((half, wide), F32), gterm=((half, wide), F32), npt=((wide, rows), BF16), gbt=((wide, rows), BF16),
        lsrc=((3, wide, half), BF16), bpair=((3, rows, wide), BF16), apair=((3, 2, quarter, rows), BF16),
        vsum=((8, wide), F32),
        gb=((2, 2, deep, wide), BF16), ybin=((2, deep, wide), BF16), xbin=((deep, wide), BF16),
        ga=((2, nz, 2, 2, quarter, units), BF16), xin0=((nz, 2, quarter, units), BF16),
        yin1=((nz, 2, quarter, units), BF16), yin0=((nz, quarter, units), BF16), xin1=((nz, quarter, units), BF16),
        zs=((nz, 2, quarter, units), BF16), zin=((nz, 2, quarter, units), BF16),
        pin=((pairs, 2, quarter, units), BF16),
        gc=((2, deep, wide), BF16), ycin=((deep, wide), BF16), sq=((2, deep, wide), BF16),
        sqin=((2, nz, zr, 128), BF16), sqpair=((2, pairs, zr, 128), BF16),
        acc=((nh, 2 * HD, rows), F32), pin_kv=((nh // dph, max(dph - 1, 1), 2 * HD, rows), F32),
        dkvsend=((nh, 2 * HD, rows), BF16), dqsend=((nh, HD, tq), BF16),
        dqkv=((heads, 3 * HD, rows), BF16), dsib=((heads // 2, 3 * HD, rows), BF16),
        psend=((half, wide), BF16), precv=((half, wide), BF16),
        tsend=((half, wide), BF16), trecv=((half, cw), BF16),
        vin4=((4, 8, wide), F32), vinz=((nz, 8, wide), F32), vinb=((nb, 8, wide), F32),
    )
    sems = dict(
        xs=(10,), xr=(10,), wzs=(nz,), wzr=(nz,), gxs=(3,), gxr=(3,), gcs=(3,), gcr=(3,),
        ks=(heads, 2), kr=(nh, 2), qs=(heads, dph), qr=(nh,), cs=(12,), cr=(12,),
        wxs=(nz,), wxr=(nz,), wys=(nz, 2), wyr=(nz, 2), wcs=(2,), wcr=(2,),
        fs=(nh, dph), fr=(nh,), osd=(nh,), orc=(2 * heads, per),
        as_=(nz,), ar=(nz,), ps_=(nz,), pr=(nz,), ds=(2, heads, per), dr=(nh,),
        ys=(5,), yr=(5,), zss=(nz,), zsr=(nz,), pas=(pairs,), par=(pairs,),
        sqs=(2, nz), sqr=(2, nz), sqps=(2, pairs), sqpr=(2, pairs), sgs=(2, nz), sgr=(2, nz),
        sys=(2,), syr=(2,), scs=(2,), scr=(2,),
        pks=(nh,), pkr=(nh // dph, max(dph - 1, 1)), dqs=(nh,), dqr=(heads, dph), dks=(nh,), dkr=(heads,),
        ts=(heads,), tr=(heads // 2,), v4s=(3,), v4r=(4,), vzs=(nz,), vzr=(nz,), vbs=(nb,), vbr=(nb,),
    )
    names = list(ins) + list(outs) + list(bufs) + list(sems)
    vmem = pl.BlockSpec(memory_space=pltpu.VMEM)
    results = pl.pallas_call(
        functools.partial(layer_kernel, names, sizes),
        out_shape=[jax.ShapeDtypeStruct(shape, kind) for shape, kind in outs.values()],
        in_specs=[pl.BlockSpec(memory_space=pltpu.SMEM)] + [vmem] * (len(ins) - 1),
        out_specs=[vmem] * len(outs),
        scratch_shapes=[pltpu.VMEM(shape, kind) for shape, kind in bufs.values()]
        + [pltpu.SemaphoreType.DMA(shape) for shape in sems.values()],
        compiler_params=pltpu.CompilerParams(
            collective_id=1, has_side_effects=True, vmem_limit_bytes=VMEM_LIMIT
        ),
        cost_estimate=pl.CostEstimate(flops=10**10, bytes_accessed=10**7, transcendentals=10**7),
    )(*ins.values())
    grads = [
        ((rows, cw), BF16), ((rows, cw), F32), ((1, cw), F32), ((1, cw), F32),
        ((wide, cw), F32), ((wide, cw), F32), ((wide, cw), F32), ((cw, wide), F32),
        ((wide, cw), F32), ((1, cw), F32), ((1, cw), F32), ((1, cw), F32), ((wide, cw), F32), ((1, cw), F32),
        ((cw, units), F32), ((units, cw), F32),
    ]
    done = pl.pallas_call(
        functools.partial(final_kernel, heads),
        out_shape=[jax.ShapeDtypeStruct(shape, kind) for shape, kind in grads],
        in_specs=[vmem] * len(outs),
        out_specs=[vmem] * len(grads),
        compiler_params=pltpu.CompilerParams(vmem_limit_bytes=32 * 1024 * 1024),
    )(*results)
    return tuple(a[0] if a.shape[0] == 1 else a for a in done)


def solution(mesh):
    cols = P(None, "width")
    vec = P("width")
    in_specs = (
        P(("batch", "hidden"), "width"), vec, vec, cols, cols, cols, P("width", None), cols, vec, vec, vec,
        cols, vec, P("width", "hidden"), P("hidden", "width"), P("batch", None),
        P(("batch", "hidden"), "width"),
    )
    out_specs = (
        P(("batch", "hidden"), "width"), P(("batch", "hidden"), "width"), vec, vec, cols, cols, cols,
        P("width", None), cols, vec, vec, vec, cols, vec, P("width", "hidden"), P("hidden", "width"),
    )
    return jax.shard_map(local, mesh=mesh, in_specs=in_specs, out_specs=out_specs, check_vma=False)
```

time: 953 us -> 188 us (0.20)
  waiting for transfers between devices: 629 us -> 0 us
  Pallas kernels: 0 us -> 182 us
  matrix products: 141 us -> 0 us
  blocking collectives: 66.3 us -> 0 us
  other arithmetic: 65.8 us -> 0 us
  local copies, waits for them, and re-layouts: 28.1 us -> 5.04 us
  between operations: 14.6 us -> 0.75 us
    psum x4 -> x0, waiting for transfers between devices: 255 us -> none  [the longest x1 130 us: unit_total(): return lax.psum(partial_sum, 'width')]
    reduce_scatter x5 -> x0, waiting for transfers between devices: 220 us -> none  [the longest x1 89.7 us: local(): lax.psum_scatter(outer_cols(grad_pre, up_full), 'hidden', scatter_dimensi...]
    pallas_call x0 -> x2, Pallas kernels: none -> 182 us  [the longest x1 179 us: local(): pl.pallas_call(functools.partial(layer_kernel, names, sizes), out_shape=[...]
    all_gather x6 -> x0, waiting for transfers between devices: 153 us -> none  [the longest x2 67.4 us: spread_rows(): return lax.all_gather(values, 'hidden', axis=0, tiled=True)]
    dot_general x52 -> x0, matrix products: 141 us -> none  [the longest x20 65 us: outer_cols(): lax.dot_general(left, right, (((1,), (1,)), ((), ())), preferred_element_...]
    convert_element_type x11 -> x0, other arithmetic: 45.6 us -> none  [the longest x4 31.7 us: query_side(): grad_scores = (probs * (grad_probs - centre)).astype(jnp.bfloat16)]
    psum x1 -> x0, blocking collectives: 35 us -> none  [local(): lax.psum((inner_rows(normed_one, grad_queries), inner_rows(normed_one, gr...]
    all_gather x6 -> x0, blocking collectives: 31.3 us -> none  [the longest x2 9.66 us: columns(): lax.all_gather(gain[None, :], 'width', axis=1, tiled=True)]
  transfers between devices with their start and end apart: 15 -> 0, of which waited for: 15 -> 0; matrix products, arithmetic and copies ran while one was open for 3% -> 0% of each run, Pallas kernels for 0% -> 0%
where the time goes in v2:
time: 188 us
  Pallas kernels  182 us (97%)
  local copies, waits for them, and re-layouts  5.04 us (3%)
    pallas_call x1, Pallas kernels, local(): pl.pallas_call(functools.partial(layer_kernel, names, sizes), out_shape=[...  179 us
    unnamed x10, local copies, waits for them, and re-layouts  5.04 us

profile of v2, /device:TPU:0, one launch (start us, length us, event | category | flops | bytes accessed | tf_op | source)
XLA Modules:
  0.0 187.8 jit_solution(17705670704994209694)
XLA Ops:
  0.7 179.5 %shard_map.288 = (bf16[512,256]{1,0:T(8,128)(2,1)}, f32[512,256]{1,0:T(8,128)}, bf16[2,2,128,256]{3,2,1,0:T(8,128)(2,1)}, bf16[2,2,2,192,512]{4,3,2,1,0:T(8,128)(2,1)}, f32[8,256]{1,0:T(8,128)}) custom-call(s32[1,3]{1,0:T(1,128)} %refs_0_.1, bf16[512,256]{1,0:T(8,128)(2,1)} %refs_1_.1, bf16[512,256]{1,0:T(8,128)(2,1)} %refs_2_.1, f32[1,256]{1,0:T(1,128)} %bitcast.12, ...), custom_call_target="tpu_custom_call" | custom-call | flops 10000000000 | bytes 10000000 | tf_op jit(solution)/shard_map/pallas_call | solution.py:949
  180.2 0.0 copy-start
  180.2 1.4 copy-done
  181.6 0.0 copy-start.1
  181.6 1.0 copy-done.1
  182.6 0.0 copy-start.2
  182.6 0.9 copy-done.2
  183.6 0.0 copy-start.3
  183.6 0.9 copy-done.3
  184.5 0.0 copy-start.4
  184.5 0.7 copy-done.4
  185.2 2.5 %shard_map.289 = (bf16[512,256]{1,0:T(8,128)(2,1)}, f32[512,256]{1,0:T(8,128)}, f32[1,256]{1,0:T(1,128)}, f32[1,256]{1,0:T(1,128)}, f32[512,256]{1,0:T(8,128)}, ...) custom-call(bf16[512,256]{1,0:T(8,128)(2,1)S(1)} %copy-done.2, ...), custom_call_target="tpu_custom_call" | custom-call | tf_op jit(solution)/shard_map/pallas_call | solution.py:967
Async XLA Ops:
  180.2 1.4 copy-start
  181.6 1.0 copy-start.1
  182.6 0.9 copy-start.2
  183.6 0.9 copy-start.3
  184.5 0.7 copy-start.4

commit v3 on v2

--- a/solution.py
+++ b/solution.py
@@ -143,20 +143,41 @@
         copy = remote(r.tok.at[part], r.tokf.at[part, own], r.xs.at[1 + k], r.xr.at[1 + k], x_dev)
         sends.start(copy)
         tcopies.append(copy)
-    for kind, (src, dst) in enumerate(((r.wu, r.wup), (r.wd, r.wdn))):
-        for k in range(nz - 1, 0, -1):
-            _, dev = z_dev(k)
-            copy = remote(src, dst.at[z, c, w], r.wzs.at[k], r.wzr.at[z], dev)
-            sends.start_if(bp == kind, copy)
-    ccopy = remote(r.cot.at[theirs], r.cotr.at[:, own], r.xs.at[3], r.xr.at[3], x_dev)
-    sends.start(ccopy)
+    r.wup[z, c, w] = r.wu[...]
+    r.wdn[z, c, w] = r.wd[...]
+
+    def weight_hop(k):
+        for kind, buf in enumerate((r.wup, r.wdn)):
+            for way, step in enumerate((1, -1)):
+                zz = z - step * (k - 1)
+                have = (zz >= 0) & (zz < nz) & (bp == kind)
+                onward = (z + step >= 0) & (z + step < nz)
+                index = jnp.clip(zz, 0, nz - 1)
+                block = buf.at[index, c, w]
+                if k > 1:
+
+                    @pl.when(have)
+                    def _(block=block, index=index):
+                        await_copy(block, r.wzr.at[index])
+
+                if k < nz:
+                    dev = (b, 2 * jnp.clip(z + step, 0, nz - 1) + c, w)
+                    copy = remote(block, block, r.wzs.at[way, k], r.wzr.at[index], dev)
+                    sends.start_if(have & onward, copy)
+                if k > 1 or way == 0:
+                    copy = remote(block, block, r.wxs.at[way, k - 1], r.wxr.at[index], x_dev)
+                    sends.start_if(have, copy)
+                if k > 1:
+                    copy = remote(block, block, r.wys.at[way, k - 1], r.wyr.at[index, w], y_dev)
+                    sends.start_if(have, copy)
+
+    weight_hop(1)
     gates = ((r.wg1, r.g1f), (r.wg2, r.g2f), (r.wo, r.wof))
     for i, (src, dst) in enumerate(gates):
         piece = at(c, src.shape[0] // 2)
         sends.start(remote(src.at[piece], dst.at[w, piece], r.gxs.at[i], r.gxr.at[i], x_dev))
         dst[w] = src[...]
-    r.wup[z, c, w] = r.wu[...]
-    r.wdn[z, c, w] = r.wd[...]
+    ccopy = remote(r.cot.at[theirs], r.cotr.at[:, own], r.xs.at[3], r.xr.at[3], x_dev)
     r.vecf[:, own] = r.vsrc[...]
     r.tokf[:, own] = r.tok[...]
     r.cotr[:, own] = r.cot[mine, :]
@@ -180,6 +201,7 @@
             qkv = nt(r.wt[t], n).astype(BF16)
             r.qsrc[t, :, part] = qkv[:HD]
             r.kvsrc[t, :, part] = qkv[HD:]
+        weight_hop(2 + k)
         for step in range(heads - 1, -1, -1):
             t = lax.rem(group + step, heads)
             span = pl.ds(k * half, half)
@@ -203,35 +225,19 @@
                     def _(src=src, dst=dst):
                         pltpu.make_async_copy(src, dst, r.qr.at[h]).start()
 
-    sends.start(remote(r.npair.at[c], r.npair.at[c], r.cs.at[0], r.cr.at[0], c_dev))
-
-    def weights_over_x():
+    for k in range(4, nz + 1):
+        weight_hop(k)
+
+    def weights_over_y():
         for kind, buf in enumerate((r.wup, r.wdn)):
 
             @pl.when(bp == kind)
             def _(buf=buf):
                 for k in range(nz):
                     zz, _ = z_dev(k)
-                    if k:
-                        await_copy(buf.at[zz, c, w], r.wzr.at[zz])
-                    block = buf.at[zz, c, w]
-                    remote(block, block, r.wxs.at[zz], r.wxr.at[zz], x_dev).start()
-
-    def weights_over_y():
-        for kind, buf in enumerate((r.wup, r.wdn)):
-
-            @pl.when(bp == kind)
-            def _(buf=buf):
-                for k in range(nz):
-                    zz, _ = z_dev(k)
-                    if k:
-                        block = buf.at[zz, c, w]
-                        remote(block, block, r.wys.at[zz, w], r.wyr.at[zz, w], y_dev).start()
-                for k in range(nz):
-                    zz, _ = z_dev(k)
                     block = buf.at[zz, c, 1 - w]
                     await_copy(block, r.wxr.at[zz])
-                    remote(block, block, r.wys.at[zz, 1 - w], r.wyr.at[zz, 1 - w], y_dev).start()
+                    remote(block, block, r.wyd.at[zz], r.wyr.at[zz, 1 - w], y_dev).start()
 
     def weights_over_core():
         for kind, buf in enumerate((r.wup, r.wdn)):
@@ -246,6 +252,8 @@
 
             block = buf.at[:, c]
             sends.start(remote(block, block, r.wcs.at[kind], r.wcr.at[kind], c_dev))
+
+    def gates_over_core():
         for i, (src, dst) in enumerate(gates):
             piece = dst.at[1 - w, at(c, src.shape[0] // 2)]
             await_copy(piece, r.gxr.at[i])
@@ -257,11 +265,7 @@
             @pl.when(bp == kind)
             def _(buf=buf):
                 for k in range(nz):
-                    zz, _ = z_dev(k)
-                    if k:
-                        await_copy(buf.at[zz, c, w], r.wys.at[zz, w])
-                    await_copy(buf.at[zz, c, w], r.wxs.at[zz])
-                    await_copy(buf.at[zz, c, w], r.wys.at[zz, 1 - w])
+                    await_copy(buf.at[z, c, w], r.wyd.at[k])
 
     def pass_on(s):
         @pl.when(lax.rem(s, dph) == sub)
@@ -336,14 +340,13 @@
 
         @pl.when(s == nh // 4)
         def _():
-            weights_over_x()
-
-        @pl.when(s == nh // 2)
-        def _():
             weights_over_y()
 
         return 0
 
+    sends.start(remote(r.npair.at[c], r.npair.at[c], r.cs.at[0], r.cr.at[0], c_dev))
+    gates_over_core()
+    sends.start(ccopy)
     pass_on(0)
     lax.fori_loop(0, nh, query_forward, 0)
     weights_over_core()
@@ -483,7 +486,6 @@
             block = nn(r.apair[m, v], r.bpair[m]).astype(BF16)
             for y in range(2):
                 r.gb[v, y, m * eighth : (m + 1) * eighth, :] = block[y * eighth : (y + 1) * eighth]
-    sends.start(remote(r.gb.at[:, 1 - bp], r.ybin, r.ys.at[0], r.yr.at[0], y_dev))
     await_copy(r.npt.at[:, lanes], r.cr.at[1])
     await_copy(r.gbt.at[:, lanes], r.cr.at[2])
 
@@ -497,6 +499,7 @@
     lax.fori_loop(0, nz, weight_grads, 0)
     sends.start(remote(r.ga.at[0, :, 1 - w], r.xin0, r.xs.at[5], r.xr.at[5], x_dev))
     sends.start(remote(r.ga.at[1, :, :, 1 - bp], r.yin1, r.ys.at[1], r.yr.at[1], y_dev))
+
 
     def ffn_second():
         await_copy(r.xin0, r.xr.at[5])
@@ -505,6 +508,7 @@
         await_copy(r.yin1, r.yr.at[1])
         r.ga[1, :, :, bp] = (r.ga[1, :, :, bp].astype(F32) + r.yin1[...].astype(F32)).astype(BF16)
         remote(r.ga.at[1, :, 1 - w, bp], r.xin1, r.xs.at[6], r.xr.at[6], x_dev).start()
+        remote(r.gb.at[:, 1 - bp], r.ybin, r.ys.at[0], r.yr.at[0], y_dev).start()
 
     def ffn_third():
         await_copy(r.yin0, r.yr.at[2])
@@ -701,22 +705,17 @@
 
         @pl.when(step == 2 * unit)
         def _():
-            square_x()
             ffn_second()
 
         @pl.when(step == 4 * unit)
         def _():
-            square_z(0)
             ffn_third()
-
-        @pl.when(step == 6 * unit)
-        def _():
-            square_spread(0)
 
         return 0
 
     lax.fori_loop(0, nh, query_backward, 0)
     finish(0)
+    square_x()
 
     for t in range(heads):
         await_copy(r.dqkv.at[t, pl.ds(HD, 2 * HD), :], r.dkr.at[t])
@@ -730,6 +729,7 @@
     def grad_normed(span):
         return nn(flip(r.dqkv[:, :, span].reshape(heads * 3 * HD, half)), wts)
 
+    square_z(0)
     r.psend[...] = grad_normed(theirs).astype(BF16)
     pcopy = remote(r.psend, r.precv, r.xs.at[8], r.xr.at[8], x_dev)
     sends.start(pcopy)
@@ -745,8 +745,7 @@
     centre = x - jnp.mean(x, -1, keepdims=True)
     rstd = lax.rsqrt(jnp.mean(centre * centre, -1, keepdims=True) + EPSILON)
     n = centre * rstd
-    square_y(0)
-    ffn_fourth()
+    square_spread(0)
     square_z(1)
     pcopy.wait_recv()
     gnorm = gnorm + r.precv[...].astype(F32)
@@ -770,8 +769,7 @@
                 sends.start(remote(r.vin4.at[me4], r.vin4.at[me4], r.v4s.at[k], r.v4r.at[me4], dev))
                 k += 1
     r.gtok[mine, :] = jnp.where(w == 0, result[:, :cw], result[:, cw:])
-    square_core(0)
-    square_spread(1)
+    square_y(0)
     for dc in range(2):
         for dw in range(2):
             if dc or dw:
@@ -781,6 +779,9 @@
     for k in range(1, nz):
         _, dev = z_dev(k)
         sends.start(remote(r.vinz.at[z], r.vinz.at[z], r.vzs.at[k], r.vzr.at[z], dev))
+    square_spread(1)
+    ffn_fourth()
+    square_core(0)
     tcopy.wait_recv()
     r.gtok[theirs, :] = r.trecv[...].astype(F32)
     ocopy.wait_recv()
@@ -838,6 +839,7 @@
         await_copy(r.acts.at[i2], r.as_.at[i2])
         await_copy(r.gpres.at[i2], r.ps_.at[i2])
     ffn_sent()
+    await_copy(r.ybin, r.ys.at[0])
     await_copy(r.xbin, r.xs.at[7])
     sends.finish()
     square_end(0)
@@ -933,9 +935,9 @@
         vin4=((4, 8, wide), F32), vinz=((nz, 8, wide), F32), vinb=((nb, 8, wide), F32),
     )
     sems = dict(
-        xs=(10,), xr=(10,), wzs=(nz,), wzr=(nz,), gxs=(3,), gxr=(3,), gcs=(3,), gcr=(3,),
+        xs=(10,), xr=(10,), wzs=(2, nz), wzr=(nz,), gxs=(3,), gxr=(3,), gcs=(3,), gcr=(3,),
         ks=(heads, 2), kr=(nh, 2), qs=(heads, dph), qr=(nh,), cs=(12,), cr=(12,),
-        wxs=(nz,), wxr=(nz,), wys=(nz, 2), wyr=(nz, 2), wcs=(2,), wcr=(2,),
+        wxs=(2, nz), wxr=(nz,), wys=(2, nz), wyr=(nz, 2), wyd=(nz,), wcs=(2,), wcr=(2,),
         fs=(nh, dph), fr=(nh,), osd=(nh,), orc=(2 * heads, per),
         as_=(nz,), ar=(nz,), ps_=(nz,), pr=(nz,), ds=(2, heads, per), dr=(nh,),
         ys=(5,), yr=(5,), zss=(nz,), zsr=(nz,), pas=(pairs,), par=(pairs,),
@@ -969,7 +971,7 @@
         out_shape=[jax.ShapeDtypeStruct(shape, kind) for shape, kind in grads],
         in_specs=[vmem] * len(outs),
         out_specs=[vmem] * len(grads),
-        compiler_params=pltpu.CompilerParams(vmem_limit_bytes=32 * 1024 * 1024),
+        compiler_params=pltpu.CompilerParams(vmem_limit_bytes=VMEM_LIMIT),
     )(*results)
     return tuple(a[0] if a.shape[0] == 1 else a for a in done)
 

time: 188 us -> 154 us (0.82)
  Pallas kernels: 182 us -> 152 us
  local copies, waits for them, and re-layouts: 5.04 us -> 0 us
    pallas_call x1, Pallas kernels: 179 us -> 147 us  [local(): pl.pallas_call(functools.partial(layer_kernel, names, sizes), out_shape=[...]
    unnamed x10 -> x0, local copies, waits for them, and re-layouts: 5.04 us -> none
where the time goes in v3:
time: 154 us; the launch traced here: 152 us
  Pallas kernels  152 us (99%)
    pallas_call x1, Pallas kernels, local(): pl.pallas_call(functools.partial(layer_kernel, names, sizes), out_shape=[...  147 us
    pallas_call x1, Pallas kernels, local(): pl.pallas_call(functools.partial(final_kernel, heads), out_shape=[jax.Sha...  4.16 us

profile of v3, /device:TPU:0, one launch (start us, length us, event | category | flops | bytes accessed | tf_op | source)
XLA Modules:
  0.0 152.4 jit_solution(3842299002952512181)
XLA Ops:
  0.7 147.5 %shard_map.288 = (bf16[512,256]{1,0:T(8,128)(2,1)}, f32[512,256]{1,0:T(8,128)}, bf16[2,2,128,256]{3,2,1,0:T(8,128)(2,1)}, bf16[2,2,2,192,512]{4,3,2,1,0:T(8,128)(2,1)}, f32[8,256]{1,0:T(8,128)}) custom-call(s32[1,3]{1,0:T(1,128)} %refs_0_.1, bf16[512,256]{1,0:T(8,128)(2,1)} %refs_1_.1, bf16[512,256]{1,0:T(8,128)(2,1)} %refs_2_.1, f32[1,256]{1,0:T(1,128)} %bitcast.12, ...), custom_call_target="tpu_custom_call" | custom-call | flops 10000000000 | bytes 10000000 | tf_op jit(solution)/shard_map/pallas_call | solution.py:951
  148.2 4.2 %shard_map.289 = (bf16[512,256]{1,0:T(8,128)(2,1)}, f32[512,256]{1,0:T(8,128)}, f32[1,256]{1,0:T(1,128)}, f32[1,256]{1,0:T(1,128)}, f32[512,256]{1,0:T(8,128)}, ...) custom-call(bf16[512,256]{1,0:T(8,128)(2,1)} %get-tuple-element.37.r, ...), custom_call_target="tpu_custom_call" | custom-call | tf_op jit(solution)/shard_map/pallas_call | solution.py:969

commit v4 on v3

--- a/solution.py
+++ b/solution.py
@@ -98,6 +98,7 @@
     half, wide, nz = rows // 2, 2 * cw, nh // 2
     per = half // tq
     pairs = nb // 2
+    hops = nz.bit_length() - 1
     b, h, w = lax.axis_index("batch"), lax.axis_index("hidden"), lax.axis_index("width")
     group, sub = lax.div(h, dph), lax.rem(h, dph)
     z, c, bp = lax.div(h, 2), lax.rem(h, 2), lax.rem(b, 2)
@@ -146,31 +147,34 @@
     r.wup[z, c, w] = r.wu[...]
     r.wdn[z, c, w] = r.wd[...]
 
-    def weight_hop(k):
+    def weight_hop(k, ending=False):
         for kind, buf in enumerate((r.wup, r.wdn)):
             for way, step in enumerate((1, -1)):
                 zz = z - step * (k - 1)
-                have = (zz >= 0) & (zz < nz) & (bp == kind)
                 onward = (z + step >= 0) & (z + step < nz)
+                here = (zz >= 0) & (zz < nz) & (bp == kind)
+                here = here & (jnp.logical_not(onward) if ending else onward)
                 index = jnp.clip(zz, 0, nz - 1)
                 block = buf.at[index, c, w]
                 if k > 1:
 
-                    @pl.when(have)
+                    @pl.when(here)
                     def _(block=block, index=index):
                         await_copy(block, r.wzr.at[index])
 
-                if k < nz:
+                if not ending:
                     dev = (b, 2 * jnp.clip(z + step, 0, nz - 1) + c, w)
                     copy = remote(block, block, r.wzs.at[way, k], r.wzr.at[index], dev)
-                    sends.start_if(have & onward, copy)
-                if k > 1 or way == 0:
+                    sends.start_if(here, copy)
+                if k > 1:
                     copy = remote(block, block, r.wxs.at[way, k - 1], r.wxr.at[index], x_dev)
-                    sends.start_if(have, copy)
-                if k > 1:
+                    sends.start_if(here, copy)
                     copy = remote(block, block, r.wys.at[way, k - 1], r.wyr.at[index, w], y_dev)
-                    sends.start_if(have, copy)
-
+                    sends.start_if(here, copy)
+
+    for kind, buf in enumerate((r.wup, r.wdn)):
+        block = buf.at[z, c, w]
+        sends.start_if(bp == kind, remote(block, block, r.wxs.at[0, 0], r.wxr.at[z], x_dev))
     weight_hop(1)
     gates = ((r.wg1, r.g1f), (r.wg2, r.g2f), (r.wo, r.wof))
     for i, (src, dst) in enumerate(gates):
@@ -189,7 +193,8 @@
 
     vcopy.wait_recv()
     gain, shift = r.vecf[0:1, :], r.vecf[1:2, :]
-    for k in range(2):
+
+    def project(k):
         part = slice(k * half, (k + 1) * half)
         tcopies[k].wait_recv()
         x = r.tokf[part, :].astype(F32)
@@ -201,32 +206,40 @@
             qkv = nt(r.wt[t], n).astype(BF16)
             r.qsrc[t, :, part] = qkv[:HD]
             r.kvsrc[t, :, part] = qkv[HD:]
-        weight_hop(2 + k)
-        for step in range(heads - 1, -1, -1):
-            t = lax.rem(group + step, heads)
-            span = pl.ds(k * half, half)
-            src, dst = r.kvsrc.at[t, :, span], r.kvt.at[h, :, span]
+
+    def send_heads(step, k):
+        t = lax.rem(group + step, heads)
+        span = pl.ds(k * half, half)
+        src, dst = r.kvsrc.at[t, :, span], r.kvt.at[h, :, span]
+        if step:
+            dev = (b, t * dph + sub, w)
+            sends.start(remote(src, dst, r.ks.at[step, k], r.kr.at[h, k], dev))
+        else:
+            pltpu.make_async_copy(src, dst, r.kr.at[h, k]).start()
+        for i in range(per):
+            row = k * per + i
+            target = sub_row(h, row, dph)
+            src, dst = r.qsrc.at[t, :, pl.ds(row * tq, tq)], r.qt.at[h]
+            copy = remote(src, dst, r.qs.at[step, row], r.qr.at[h], (b, t * dph + target, w))
             if step:
-                dev = (b, t * dph + sub, w)
-                sends.start(remote(src, dst, r.ks.at[step, k], r.kr.at[h, k], dev))
+                sends.start(copy)
             else:
-                pltpu.make_async_copy(src, dst, r.kr.at[h, k]).start()
-            for i in range(per):
-                row = k * per + i
-                target = sub_row(h, row, dph)
-                src, dst = r.qsrc.at[t, :, pl.ds(row * tq, tq)], r.qt.at[h]
-                copy = remote(src, dst, r.qs.at[step, row], r.qr.at[h], (b, t * dph + target, w))
-                if step:
-                    sends.start(copy)
-                else:
-                    sends.start_if(target != sub, copy)
-
-                    @pl.when(target == sub)
-                    def _(src=src, dst=dst):
-                        pltpu.make_async_copy(src, dst, r.qr.at[h]).start()
-
-    for k in range(4, nz + 1):
-        weight_hop(k)
+                sends.start_if(target != sub, copy)
+
+                @pl.when(target == sub)
+                def _(src=src, dst=dst):
+                    pltpu.make_async_copy(src, dst, r.qr.at[h]).start()
+
+    weight_hop(2)
+    project(0)
+    send_heads(heads - 1, 0)
+    weight_hop(3)
+    project(1)
+    send_heads(heads - 1, 1)
+    for step in range(heads - 2, -1, -1):
+        for k in range(2):
+            send_heads(step, k)
+
 
     def weights_over_y():
         for kind, buf in enumerate((r.wup, r.wdn)):
@@ -257,7 +270,7 @@
         for i, (src, dst) in enumerate(gates):
             piece = dst.at[1 - w, at(c, src.shape[0] // 2)]
             await_copy(piece, r.gxr.at[i])
-            sends.start(remote(piece, piece, r.gcs.at[i], r.gcr.at[i], c_dev))
+            remote(piece, piece, r.gcs.at[i], r.gcr.at[i], c_dev).start()
 
     def weights_sent():
         for kind, buf in enumerate((r.wup, r.wdn)):
@@ -266,6 +279,9 @@
             def _(buf=buf):
                 for k in range(nz):
                     await_copy(buf.at[z, c, w], r.wyd.at[k])
+
+        for i, (src, dst) in enumerate(gates):
+            await_copy(dst.at[1 - w, at(c, src.shape[0] // 2)], r.gcs.at[i])
 
     def pass_on(s):
         @pl.when(lax.rem(s, dph) == sub)
@@ -276,53 +292,43 @@
                 dev = (b, group * dph + lax.rem(sub + k, dph), w)
                 remote(r.kvt.at[s], r.kvt.at[s], r.fs.at[s, k], r.fr.at[s], dev).start()
 
-    def query_forward(s, _):
-        @pl.when(s + 1 < nh)
-        def _():
-            pass_on(s + 1)
-
+    def arrive(s):
         @pl.when(lax.rem(s, dph) != sub)
         def _():
             await_copy(r.kvt.at[s], r.fr.at[s])
 
         r.kvn[s] = flip(r.kvt[s])
         await_copy(r.qt.at[s], r.qr.at[s])
+        q = r.qt[s].astype(F32) * SCALE
+        r.qlow[s] = jnp.concatenate([q, jnp.zeros_like(q)], 0).astype(BF16)
+
+    def masked(scores, i, j):
+        query_base = i * rows + sub_row(i, sub, dph) * tq
+        return jnp.where(allowed_mask(j * rows, query_base, rows, tq, ends), scores, NEG)
+
+    def bias(scores, j):
+        key_pos = j * rows + lax.broadcasted_iota(jnp.int32, (rows, 1), 0)
+        return scores + jnp.where(key_pos < ends[0], NEG, 0.0)
+
+    def absorb(i, blocks):
+        top = r.top[i]
+        new_top = top
+        for scores, _ in blocks:
+            new_top = jnp.maximum(new_top, jnp.max(scores, 0, keepdims=True))
+        fade = jnp.exp(top - new_top)
+        total, mixed = r.total[i] * fade, r.ot[i] * fade
+        for scores, j in blocks:
+            weights = jnp.exp(scores - new_top)
+            total = total + jnp.sum(weights, 0, keepdims=True)
+            mixed = mixed + nn(r.kvt[j, HD:, :], weights.astype(BF16))
+        r.top[i], r.total[i], r.ot[i] = new_top, total, mixed
+
+    def send_attended(s):
         row = sub_row(s, sub, dph)
-        query_base = s * rows + row * tq
-        q = r.qt[s].astype(F32) * SCALE
-        q = jnp.concatenate([q, jnp.zeros_like(q)], 0).astype(BF16)
-
-        def masked(j, scores):
-            return jnp.where(allowed_mask(j * rows, query_base, rows, tq, ends), scores, NEG)
-
-        def absorb(j, scores, carry):
-            top, total, mixed = carry
-            new_top = jnp.maximum(top, jnp.max(scores, 0, keepdims=True))
-            fade = jnp.exp(top - new_top)
-            weights = jnp.exp(scores - new_top)
-            total = total * fade + jnp.sum(weights, 0, keepdims=True)
-            mixed = mixed * fade + nn(r.kvt[j, HD:, :], weights.astype(BF16))
-            return new_top, total, mixed
-
-        def plain_step(j, carry):
-            scores = r.sbuf[lax.rem(j, 2)]
-            r.sbuf[lax.rem(j + 1, 2)] = nn(r.kvn[j + 1], q)
-            return absorb(j, scores, carry)
-
-        def masked_step(j, carry):
-            scores = masked(j, r.sbuf[lax.rem(j, 2)])
-            r.sbuf[lax.rem(j + 1, 2)] = nn(r.kvn[j + 1], q)
-            return absorb(j, scores, carry)
-
-        r.sbuf[0] = masked(0, nn(r.kvn[0], q))
-        plain = jnp.where(s == nh - 1, 0, s)
-        carry = (jnp.full((1, tq), NEG, F32), jnp.zeros((1, tq), F32), jnp.zeros((HD, tq), F32))
-        carry = lax.fori_loop(0, plain, plain_step, carry)
-        carry = lax.fori_loop(plain, s, masked_step, carry)
-        top, total, mixed = absorb(s, masked(s, r.sbuf[lax.rem(s, 2)]), carry)
-        mixed = mixed / total
+        total = r.total[s]
+        mixed = r.ot[s] / total
         r.ot[s] = mixed
-        r.lse[s] = top + jnp.log(total)
+        r.lse[s] = r.top[s] + jnp.log(total)
         r.osend[s] = mixed.astype(BF16)
         row_w = lax.div(row * tq, half)
         lane = lax.rem(row * tq, half)
@@ -338,17 +344,80 @@
         def _():
             remote(r.osend.at[s], dst, r.osd.at[s], slot, (b, s, row_w)).start()
 
-        @pl.when(s == nh // 4)
+    def own_chip(n):
+        i = 2 * n
+        first = masked(nn(r.kvn[i], r.qlow[i]), i, i)
+        low = masked(nn(r.kvn[i], r.qlow[i + 1]), i + 1, i)
+        high = masked(nn(r.kvn[i + 1], r.qlow[i + 1]), i + 1, i + 1)
+        absorb(i, [(first, i)])
+        absorb(i + 1, [(low, i), (high, i + 1)])
+
+    def two_chips(hi, lo, last):
+        queries, keys = (2 * hi, 2 * hi + 1), (2 * lo, 2 * lo + 1)
+        scores = [[nn(r.kvn[j], r.qlow[i]) for j in keys] for i in queries]
+        for a, i in enumerate(queries):
+            if last and a:
+                blocks = [(masked(x, i, j), j) for x, j in zip(scores[a], keys)]
+            else:
+                blocks = [(bias(scores[a][0], keys[0]), keys[0]), (scores[a][1], keys[1])]
+            absorb(i, blocks)
+
+    def completes(chip):
+        return jnp.where(z == 0, chip, nz - z + jnp.minimum(chip, z - 1))
+
+    def forward_stage(d, _):
+        n = lax.rem(z + d, nz)
+
+        @pl.when(d == nz // 2)
         def _():
             weights_over_y()
+            gates_over_core()
+
+        pass_on(2 * n)
+        pass_on(2 * n + 1)
+        arrive(2 * n)
+        arrive(2 * n + 1)
+        own_chip(n)
+
+        def with_earlier(e, _):
+            m = lax.rem(z + e, nz)
+            hi, lo = jnp.maximum(n, m), jnp.minimum(n, m)
+
+            @pl.when(hi == nz - 1)
+            def _():
+                two_chips(hi, lo, True)
+
+            @pl.when(hi != nz - 1)
+            def _():
+                two_chips(hi, lo, False)
+
+            @pl.when((m > n) & (completes(m) == d))
+            def _():
+                send_attended(2 * m)
+                send_attended(2 * m + 1)
+
+            return 0
+
+        lax.fori_loop(0, d, with_earlier, 0)
+
+        @pl.when(completes(n) == d)
+        def _():
+            send_attended(2 * n)
+            send_attended(2 * n + 1)
 
         return 0
 
+    r.top[...] = jnp.full_like(r.top, NEG)
+    r.total[...] = jnp.zeros_like(r.total)
+    r.ot[...] = jnp.zeros_like(r.ot)
+    forward_stage(0, 0)
     sends.start(remote(r.npair.at[c], r.npair.at[c], r.cs.at[0], r.cr.at[0], c_dev))
-    gates_over_core()
+    for k in range(4, nz):
+        weight_hop(k)
+    for k in range(2, nz + 1):
+        weight_hop(k, ending=True)
     sends.start(ccopy)
-    pass_on(0)
-    lax.fori_loop(0, nh, query_forward, 0)
+    lax.fori_loop(1, nz, forward_stage, 0)
     weights_over_core()
 
     for i, (src, dst) in enumerate(gates):
@@ -485,7 +554,9 @@
             await_copy(r.apair.at[m, v, :, lanes], r.cr.at[6 + 2 * m + v])
             block = nn(r.apair[m, v], r.bpair[m]).astype(BF16)
             for y in range(2):
-                r.gb[v, y, m * eighth : (m + 1) * eighth, :] = block[y * eighth : (y + 1) * eighth]
+                r.gb[v, y, m] = block[y * eighth : (y + 1) * eighth]
+    for m in range(3):
+        sends.start(remote(r.gb.at[1 - w, :, m], r.xbin.at[:, m], r.sxs.at[m], r.sxr.at[m], x_dev))
     await_copy(r.npt.at[:, lanes], r.cr.at[1])
     await_copy(r.gbt.at[:, lanes], r.cr.at[2])
 
@@ -508,25 +579,38 @@
         await_copy(r.yin1, r.yr.at[1])
         r.ga[1, :, :, bp] = (r.ga[1, :, :, bp].astype(F32) + r.yin1[...].astype(F32)).astype(BF16)
         remote(r.ga.at[1, :, 1 - w, bp], r.xin1, r.xs.at[6], r.xr.at[6], x_dev).start()
-        remote(r.gb.at[:, 1 - bp], r.ybin, r.ys.at[0], r.yr.at[0], y_dev).start()
 
     def ffn_third():
         await_copy(r.yin0, r.yr.at[2])
         await_copy(r.xin1, r.xr.at[6])
         r.zs[:, 0] = (r.ga[0, :, w, bp].astype(F32) + r.yin0[...].astype(F32)).astype(BF16)
         r.zs[:, 1] = (r.ga[1, :, w, bp].astype(F32) + r.xin1[...].astype(F32)).astype(BF16)
-        for k in range(nz - 1, 0, -1):
-            zz, dev = z_dev(k)
-            remote(r.zs.at[zz], r.zin.at[z], r.zss.at[k], r.zsr.at[z], dev).start()
-        r.zin[z] = r.zs[z]
+        ffn_hop(0)
+
+    def z_block(q, flip_bit, v):
+        bit = lax.rem(lax.div(z, 1 << q), 2)
+        bit = 1 - bit if flip_bit else bit
+        return lax.rem(z, 1 << q) + bit * (1 << q) + v * (2 << q)
+
+    def ffn_hop(q):
+        if q:
+            ffn_add(q - 1)
+        bit = lax.rem(lax.div(z, 1 << q), 2)
+        dev = (b, 2 * (z + (1 << q) * (1 - 2 * bit)) + c, w)
+        for v in range(nz >> (q + 1)):
+            slot = nz - (nz >> q) + v
+            remote(r.zs.at[z_block(q, True, v)], r.zin.at[slot], r.zss.at[slot], r.zsr.at[slot], dev).start()
+
+    def ffn_add(q):
+        for v in range(nz >> (q + 1)):
+            slot = nz - (nz >> q) + v
+            await_copy(r.zin.at[slot], r.zsr.at[slot])
+            kept = z_block(q, False, v)
+            r.zs[kept] = (r.zs[kept].astype(F32) + r.zin[slot].astype(F32)).astype(BF16)
 
     def ffn_fourth():
-        for k in range(1, nz):
-            zz, _ = z_dev(k)
-            await_copy(r.zin.at[zz], r.zsr.at[zz])
-        total = r.zin[0].astype(F32)
-        for k in range(1, nz):
-            total = total + r.zin[k].astype(F32)
+        ffn_add(hops - 1)
+        total = r.zs[z].astype(F32)
         if pairs > 1:
             mypair = lax.div(b, 2)
             r.pin[mypair] = total.astype(BF16)
@@ -547,82 +631,88 @@
     def ffn_sent():
         await_copy(r.yin0, r.ys.at[2])
         await_copy(r.xin1, r.xs.at[6])
-        for k in range(1, nz):
-            await_copy(r.zin.at[z], r.zss.at[k])
-
-    deep = (heads // 2) * 3 * HD // 2
-    zr = deep * 4 // nz
+        for k in range(nz - 1):
+            await_copy(r.zin.at[k], r.zss.at[k])
+
+    zr = HD * 4 // nz
 
     def z_part(zz):
         return pl.ds(pl.multiple_of(lax.div(zz, 4) * zr, zr), zr), at(lax.rem(zz, 4), 128)
 
-    def square_x():
-        await_copy(r.ybin, r.yr.at[0])
-        r.gb[:, bp] = (r.gb[:, bp].astype(F32) + r.ybin[...].astype(F32)).astype(BF16)
-        remote(r.gb.at[1 - w, bp], r.xbin, r.xs.at[7], r.xr.at[7], x_dev).start()
+    def square_y(which):
+        for p in range(3):
+            if which == 0:
+                await_copy(r.xbin.at[:, p], r.sxr.at[p])
+                r.gb[w, :, p] = (r.gb[w, :, p].astype(F32) + r.xbin[:, p].astype(F32)).astype(BF16)
+                src = r.gb.at[w, 1 - bp, p]
+            else:
+                src = r.gc.at[1 - bp, p]
+            remote(src, r.yin.at[which, p], r.sys.at[which, p], r.syr.at[which, p], y_dev).start()
 
     def square_z(which):
-        if which == 0:
-            await_copy(r.xbin, r.xr.at[7])
-            total = r.gb[w, bp].astype(F32) + r.xbin[...].astype(F32)
-        else:
-            await_copy(r.ycin, r.yr.at[4])
-            total = r.gc[bp].astype(F32) + r.ycin[...].astype(F32)
-        r.sq[which] = total.astype(BF16)
-        for k in range(nz - 1, 0, -1):
-            zz, dev = z_dev(k)
-            src = r.sq.at[(which,) + z_part(zz)]
-            remote(src, r.sqin.at[which, z], r.sqs.at[which, k], r.sqr.at[which, z], dev).start()
+        for p in range(3):
+            await_copy(r.yin.at[which, p], r.syr.at[which, p])
+            mine_part = r.gb[w, bp, p] if which == 0 else r.gc[bp, p]
+            r.sq[which, p] = (mine_part.astype(F32) + r.yin[which, p].astype(F32)).astype(BF16)
+            for k in range(nz - 1, 0, -1):
+                zz, dev = z_dev(k)
+                src = r.sq.at[(which, p) + z_part(zz)]
+                slot = r.sqin.at[which, p, z]
+                remote(src, slot, r.sqs.at[which, p, k], r.sqr.at[which, p, z], dev).start()
 
     def square_spread(which):
-        total = r.sq[(which,) + z_part(z)].astype(F32)
-        r.sqin[which, z] = total.astype(BF16)
-        for k in range(1, nz):
-            zz, _ = z_dev(k)
-            await_copy(r.sqin.at[which, zz], r.sqr.at[which, zz])
-        total = r.sqin[which, 0].astype(F32)
-        for k in range(1, nz):
-            total = total + r.sqin[which, k].astype(F32)
-        if pairs > 1:
-            mypair = lax.div(b, 2)
-            r.sqpair[which, mypair] = total.astype(BF16)
-            for k in range(1, pairs):
-                dev = (lax.rem(b + 2 * k, nb), h, w)
-                block = r.sqpair.at[which, mypair]
-                remote(block, block, r.sqps.at[which, k], r.sqpr.at[which, mypair], dev).start()
-            for k in range(1, pairs):
-                pp = lax.rem(mypair + k, pairs)
-                await_copy(r.sqpair.at[which, pp], r.sqpr.at[which, pp])
-            total = r.sqpair[which, 0].astype(F32)
-            for k in range(1, pairs):
-                total = total + r.sqpair[which, k].astype(F32)
-        r.red_s[(which, c, bp) + z_part(z)] = total.astype(BF16)
-        for k in range(nz - 1, 0, -1):
-            _, dev = z_dev(k)
-            block = r.red_s.at[(which, c, bp) + z_part(z)]
-            remote(block, block, r.sgs.at[which, k], r.sgr.at[which, z], dev).start()
-
-    def square_y(which):
-        for k in range(1, nz):
-            zz, _ = z_dev(k)
-            await_copy(r.red_s.at[(which, c, bp) + z_part(zz)], r.sgr.at[which, zz])
-        block = r.red_s.at[which, c, bp]
-        remote(block, block, r.sys.at[which], r.syr.at[which], y_dev).start()
+        for p in range(3):
+            r.sqin[which, p, z] = r.sq[(which, p) + z_part(z)]
+            for k in range(1, nz):
+                zz, _ = z_dev(k)
+                await_copy(r.sqin.at[which, p, zz], r.sqr.at[which, p, zz])
+            total = r.sqin[which, p, 0].astype(F32)
+            for k in range(1, nz):
+                total = total + r.sqin[which, p, k].astype(F32)
+            if pairs > 1:
+                mypair = lax.div(b, 2)
+                r.sqpair[which, p, mypair] = total.astype(BF16)
+                for k in range(1, pairs):
+                    dev = (lax.rem(b + 2 * k, nb), h, w)
+                    block = r.sqpair.at[which, p, mypair]
+                    remote(block, block, r.sqps.at[which, p, k], r.sqpr.at[which, p, mypair], dev).start()
+                for k in range(1, pairs):
+                    pp = lax.rem(mypair + k, pairs)
+                    await_copy(r.sqpair.at[which, p, pp], r.sqpr.at[which, p, pp])
+                total = r.sqpair[which, p, 0].astype(F32)
+                for k in range(1, pairs):
+                    total = total + r.sqpair[which, p, k].astype(F32)
+            r.red_s[(which, c, bp, p) + z_part(z)] = total.astype(BF16)
+            for k in range(nz - 1, 0, -1):
+                _, dev = z_dev(k)
+                block = r.red_s.at[(which, c, bp, p) + z_part(z)]
+                remote(block, block, r.sgs.at[which, p, k], r.sgr.at[which, p, z], dev).start()
+
+    def square_back(which):
+        for p in range(3):
+            for k in range(1, nz):
+                zz, _ = z_dev(k)
+                await_copy(r.red_s.at[(which, c, bp, p) + z_part(zz)], r.sgr.at[which, p, zz])
+            block = r.red_s.at[which, c, bp, p]
+            remote(block, block, r.sbs.at[which, p], r.sbr.at[which, p], y_dev).start()
 
     def square_core(which):
-        await_copy(r.red_s.at[which, c, 1 - bp], r.syr.at[which])
-        block = r.red_s.at[which, c]
-        remote(block, block, r.scs.at[which], r.scr.at[which], c_dev).start()
+        for p in range(3):
+            await_copy(r.red_s.at[which, c, 1 - bp, p], r.sbr.at[which, p])
+            block = r.red_s.at[which, c, :, p]
+            remote(block, block, r.scs.at[which, p], r.scr.at[which, p], c_dev).start()
 
     def square_end(which):
-        await_copy(r.red_s.at[which, 1 - c], r.scr.at[which])
-        await_copy(r.red_s.at[which, c], r.scs.at[which])
-        await_copy(r.red_s.at[which, c, bp], r.sys.at[which])
-        for k in range(1, nz):
-            await_copy(r.sqin.at[which, z], r.sqs.at[which, k])
-            await_copy(r.sqin.at[which, z], r.sgs.at[which, k])
-            if k < pairs:
-                await_copy(r.sqpair.at[which, 0], r.sqps.at[which, k])
+        for p in range(3):
+            await_copy(r.red_s.at[which, 1 - c, :, p], r.scr.at[which, p])
+            await_copy(r.red_s.at[which, c, :, p], r.scs.at[which, p])
+            await_copy(r.yin.at[which, p], r.sys.at[which, p])
+            await_copy(r.yin.at[which, p], r.sbs.at[which, p])
+            for k in range(1, nz):
+                await_copy(r.sqin.at[which, p, z], r.sqs.at[which, p, k])
+                await_copy(r.sqin.at[which, p, z], r.sgs.at[which, p, k])
+                if k < pairs:
+                    await_copy(r.sqpair.at[which, p, 0], r.sqps.at[which, p, k])
 
     r.acc[...] = jnp.zeros_like(r.acc)
 
@@ -634,7 +724,8 @@
                 slot = r.pin_kv.at[lax.div(s, dph), k - 1]
                 await_copy(slot, r.pkr.at[lax.div(s, dph), k - 1])
                 total = total + r.pin_kv[lax.div(s, dph), k - 1]
-            r.dkvsend[s] = total.astype(BF16)
+            r.dkvsend[s, :HD] = (total[:HD] * SCALE).astype(BF16)
+            r.dkvsend[s, HD:] = total[HD:].astype(BF16)
             dst = r.dqkv.at[group, pl.ds(HD, 2 * HD), :]
 
             @pl.when(s == h)
@@ -645,39 +736,41 @@
             def _():
                 remote(r.dkvsend.at[s], dst, r.dks.at[s], r.dkr.at[group], (b, s, w)).start()
 
-    def query_backward(step, _):
-        s = nh - 1 - step
+    def pairs_backward(where, full):
+        scores = [nn(r.kvn[j], r.qlow[i]) for i, j in where]
+        gprobs = [nn(r.kvn[j], r.dhigh[i]) for i, j in where]
+        for x, gp, (i, j), whole in zip(scores, gprobs, where, full):
+            x = masked(x, i, j) if whole else bias(x, j)
+            probs = jnp.exp(x - r.lse[i])
+            gscores = (probs * (gp - r.centre[i])).astype(BF16)
+            r.acc[j, HD:, :] += nt(r.dhigh[i, HD:, :], probs.astype(BF16))
+            r.acc[j, :HD, :] += nt(r.qt[i], gscores)
+            r.dqa[i] += nn(r.kvt[j, :HD, :], gscores)
+
+    def choose(kinds, where):
+        taken = False
+        for cond, full in kinds:
+
+            @pl.when(jnp.logical_and(cond, jnp.logical_not(taken)))
+            def _(full=full):
+                pairs_backward(where, full)
+
+            taken = jnp.logical_or(taken, cond)
+
+    def pair_at(t, u):
+        lo, hi = t, nh - 1 - t
+        n = hi - lo + 1
+        return jnp.where(u < n, hi, lo + u - n), jnp.where(u < n, lo + u, lo)
+
+    def out_arrives(s):
+        await_copy(r.dot.at[s], r.dr.at[s])
+        dout = r.dot[s]
+        r.dhigh[s] = jnp.concatenate([jnp.zeros((HD, tq), BF16), dout], 0)
+        r.centre[s] = jnp.sum(r.ot[s] * dout.astype(F32), 0, keepdims=True)
+
+    def send_block(s):
         row = sub_row(s, sub, dph)
-        query_base = s * rows + row * tq
-        await_copy(r.dot.at[s], r.dr.at[s])
-        q = r.qt[s]
-        dout = r.dot[s]
-        q_low = jnp.concatenate([q.astype(F32) * SCALE, jnp.zeros((HD, tq), F32)], 0).astype(BF16)
-        d_high = jnp.concatenate([jnp.zeros((HD, tq), BF16), dout], 0)
-        log_sum = r.lse[s]
-        centre = jnp.sum(r.ot[s] * dout.astype(F32), 0, keepdims=True)
-
-        def block(j, dq, masked):
-            scores = nn(r.kvn[j], q_low)
-            if masked:
-                scores = jnp.where(allowed_mask(j * rows, query_base, rows, tq, ends), scores, NEG)
-            probs = jnp.exp(scores - log_sum)
-            gprobs = nn(r.kvn[j], d_high)
-            gscores = (probs * (gprobs - centre)).astype(BF16)
-            r.acc[j, HD:, :] += nt(dout, probs.astype(BF16))
-            r.acc[j, :HD, :] += nt(q, gscores) * SCALE
-            return dq + nn(r.kvt[j, :HD, :], gscores)
-
-        plain_end = jnp.where(s == nh - 1, 1, jnp.maximum(s, 1))
-        dq = jnp.zeros((HD, tq), F32)
-        dq = lax.fori_loop(1, plain_end, lambda j, d: block(j, d, False), dq)
-        count = 1 + jnp.where(s > 0, s + 1 - plain_end, 0)
-
-        def with_mask(t, d):
-            return block(jnp.where(t == 0, 0, plain_end + t - 1), d, True)
-
-        dq = lax.fori_loop(0, count, with_mask, dq)
-        r.dqsend[s] = (dq * SCALE).astype(BF16)
+        r.dqsend[s] = (r.dqa[s] * SCALE).astype(BF16)
         dst = r.dqkv.at[group, pl.ds(0, HD), pl.ds(pl.multiple_of(row * tq, tq), tq)]
 
         @pl.when(s == h)
@@ -697,25 +790,57 @@
             slot = lax.div(s, dph)
             remote(r.acc.at[s], r.pin_kv.at[slot, k - 1], r.pks.at[s], r.pkr.at[slot, k - 1], dev).start()
 
-        @pl.when(step > 0)
-        def _():
-            finish(s + 1)
-
-        unit = nh // 8
-
-        @pl.when(step == 2 * unit)
+    def round_backward(t, _):
+        lo, hi = t, nh - 1 - t
+        n = hi - lo + 1
+
+        def row_step(v, _):
+            where = [pair_at(t, 2 * v), pair_at(t, 2 * v + 1)]
+            diagonal = v == lax.div(n, 2) - 1
+            choose([(t == 0, (True, True)), (diagonal, (False, True)), (True, (False, False))], where)
+            return 0
+
+        lax.fori_loop(0, lax.div(n, 2), row_step, 0)
+        send_block(hi)
+
+        @pl.when(t == 0)
+        def _():
+            lax.fori_loop(0, nh - 1, lambda s, z: (out_arrives(s), z)[1], 0)
+
+        @pl.when(t > 0)
+        def _():
+            finish(lo - 1)
+
+        def column_step(v, _):
+            where = [pair_at(t, n + 2 * v), pair_at(t, n + 2 * v + 1)]
+            choose([(v == 0, (True, False)), (True, (False, False))], where)
+            return 0
+
+        lax.fori_loop(0, lax.div(n, 2) - 1, column_step, 0)
+        pairs_backward([pair_at(t, 2 * n - 2)], (True,))
+        send_block(lo)
+        finish(hi)
+
+        @pl.when(t == 0)
+        def _():
+            square_y(0)
+
+        @pl.when(t == nh // 8)
+        def _():
+            square_z(0)
+
+        @pl.when(t == nh // 4)
         def _():
             ffn_second()
 
-        @pl.when(step == 4 * unit)
-        def _():
-            ffn_third()
-
         return 0
 
-    lax.fori_loop(0, nh, query_backward, 0)
-    finish(0)
-    square_x()
+    r.dqa[...] = jnp.zeros_like(r.dqa)
+    out_arrives(nh - 1)
+    lax.fori_loop(0, nh // 2, round_backward, 0)
+    finish(nh // 2 - 1)
+    ffn_third()
+    square_spread(0)
 
     for t in range(heads):
         await_copy(r.dqkv.at[t, pl.ds(HD, 2 * HD), :], r.dkr.at[t])
@@ -729,7 +854,6 @@
     def grad_normed(span):
         return nn(flip(r.dqkv[:, :, span].reshape(heads * 3 * HD, half)), wts)
 
-    square_z(0)
     r.psend[...] = grad_normed(theirs).astype(BF16)
     pcopy = remote(r.psend, r.precv, r.xs.at[8], r.xr.at[8], x_dev)
     sends.start(pcopy)
@@ -737,15 +861,16 @@
     for j in range(heads // 2):
         await_copy(r.dsib.at[j], r.tr.at[j])
         part = nn(r.dqkv[2 * j + c], r.npair[c]) + nn(r.dsib[j], r.npair[1 - c])
-        span = slice((j % (heads // 4)) * 3 * HD, (j % (heads // 4) + 1) * 3 * HD)
-        r.gc[j // (heads // 4), span, :] = part.astype(BF16)
-    sends.start(remote(r.gc.at[1 - bp], r.ycin, r.ys.at[4], r.yr.at[4], y_dev))
+        for p in range(3):
+            r.gc[j, p] = part[p * HD : (p + 1) * HD].astype(BF16)
+    square_y(1)
+    for q in range(1, hops):
+        ffn_hop(q)
     gnorm = grad_normed(mine) + r.gterm[...]
     x = r.tokf[mine, :].astype(F32)
     centre = x - jnp.mean(x, -1, keepdims=True)
     rstd = lax.rsqrt(jnp.mean(centre * centre, -1, keepdims=True) + EPSILON)
     n = centre * rstd
-    square_spread(0)
     square_z(1)
     pcopy.wait_recv()
     gnorm = gnorm + r.precv[...].astype(F32)
@@ -769,7 +894,7 @@
                 sends.start(remote(r.vin4.at[me4], r.vin4.at[me4], r.v4s.at[k], r.v4r.at[me4], dev))
                 k += 1
     r.gtok[mine, :] = jnp.where(w == 0, result[:, :cw], result[:, cw:])
-    square_y(0)
+    square_back(0)
     for dc in range(2):
         for dw in range(2):
             if dc or dw:
@@ -781,7 +906,6 @@
         sends.start(remote(r.vinz.at[z], r.vinz.at[z], r.vzs.at[k], r.vzr.at[z], dev))
     square_spread(1)
     ffn_fourth()
-    square_core(0)
     tcopy.wait_recv()
     r.gtok[theirs, :] = r.trecv[...].astype(F32)
     ocopy.wait_recv()
@@ -795,7 +919,8 @@
     for k in range(1, nb):
         dev = (lax.rem(b + k, nb), h, w)
         sends.start(remote(r.vinb.at[b], r.vinb.at[b], r.vbs.at[k], r.vbr.at[b], dev))
-    square_y(1)
+    square_core(0)
+    square_back(1)
     for k in range(1, nb):
         bb = lax.rem(b + k, nb)
         await_copy(r.vinb.at[bb], r.vbr.at[bb])
@@ -839,8 +964,6 @@
         await_copy(r.acts.at[i2], r.as_.at[i2])
         await_copy(r.gpres.at[i2], r.ps_.at[i2])
     ffn_sent()
-    await_copy(r.ybin, r.ys.at[0])
-    await_copy(r.xbin, r.xs.at[7])
     sends.finish()
     square_end(0)
     square_end(1)
@@ -864,16 +987,14 @@
     for core in range(2):
         for y in range(2):
             base = (2 * core + y) * eighth
-            o_wo[base : base + eighth, :] = red_s[0, core, y, :eighth, :].astype(F32)
+            o_wo[base : base + eighth, :] = red_s[0, core, y, 0].astype(F32)
     for m, ref in ((1, o_gw1), (2, o_gw2)):
-        full = [red_s[0, core, y, m * eighth : (m + 1) * eighth, :] for core in range(2) for y in range(2)]
+        full = [red_s[0, core, y, m] for core in range(2) for y in range(2)]
         ref[...] = jnp.concatenate(full, 0).astype(F32).T
     for i, ref in enumerate((o_wq, o_wk, o_wv)):
         full = []
         for t in range(heads):
-            j, core = t // 2, t % 2
-            base = (j % (heads // 4)) * 3 * HD + i * HD
-            full.append(red_s[1, core, j // (heads // 4), base : base + HD, :])
+            full.append(red_s[1, t % 2, t // 2, i])
         ref[...] = jnp.concatenate(full, 0).astype(F32).T
 
 
@@ -888,8 +1009,7 @@
     dph = nh // heads
     tq, half, wide, nz, pairs = rows // dph, rows // 2, 2 * cw, nh // 2, nb // 2
     quarter = half // 2
-    deep = (heads // 2) * 3 * HD // 2
-    zr = deep * 4 // nz
+    zr = HD * 4 // nz
     per = half // tq
     sizes = (nb, nh, rows, cw, units, heads, dph, tq)
 
@@ -902,7 +1022,7 @@
         out_c=((rows, cw), BF16),
         gtok=((rows, cw), F32),
         red_a=((2, 2, quarter, units), BF16),
-        red_s=((2, 2, 2, deep, wide), BF16),
+        red_s=((2, 2, 2, 3, HD, wide), BF16),
         red_v=((8, cw), F32),
     )
     bufs = dict(
@@ -912,7 +1032,8 @@
         wt=((heads, 3 * HD, wide), BF16), npair=((2, rows, wide), BF16),
         qsrc=((heads, HD, rows), BF16), kvsrc=((heads, 2 * HD, rows), BF16),
         kvt=((nh, 2 * HD, rows), BF16), kvn=((nh, rows, 2 * HD), BF16), qt=((nh, HD, tq), BF16),
-        sbuf=((2, rows, tq), F32), ot=((nh, HD, tq), F32), lse=((nh, 1, tq), F32), osend=((nh, HD, tq), BF16),
+        qlow=((nh, 2 * HD, tq), BF16), dhigh=((nh, 2 * HD, tq), BF16), top=((nh, 1, tq), F32), total=((nh, 1, tq), F32),
+        centre=((nh, 1, tq), F32), dqa=((nh, HD, tq), F32), ot=((nh, HD, tq), F32), lse=((nh, 1, tq), F32), osend=((nh, HD, tq), BF16),
         att=((2 * heads * HD, half), BF16),
         pre=((nz, 2, half, units), F32), acts=((nz, half, units), BF16), actp=((nz, rows, units), BF16),
         gpres=((nz, half, units), BF16), gprep=((nz, rows, units), BF16),
@@ -920,13 +1041,13 @@
         ginp=((half, wide), F32), gterm=((half, wide), F32), npt=((wide, rows), BF16), gbt=((wide, rows), BF16),
         lsrc=((3, wide, half), BF16), bpair=((3, rows, wide), BF16), apair=((3, 2, quarter, rows), BF16),
         vsum=((8, wide), F32),
-        gb=((2, 2, deep, wide), BF16), ybin=((2, deep, wide), BF16), xbin=((deep, wide), BF16),
+        gb=((2, 2, 3, HD, wide), BF16), xbin=((2, 3, HD, wide), BF16), yin=((2, 3, HD, wide), BF16),
         ga=((2, nz, 2, 2, quarter, units), BF16), xin0=((nz, 2, quarter, units), BF16),
         yin1=((nz, 2, quarter, units), BF16), yin0=((nz, quarter, units), BF16), xin1=((nz, quarter, units), BF16),
         zs=((nz, 2, quarter, units), BF16), zin=((nz, 2, quarter, units), BF16),
         pin=((pairs, 2, quarter, units), BF16),
-        gc=((2, deep, wide), BF16), ycin=((deep, wide), BF16), sq=((2, deep, wide), BF16),
-        sqin=((2, nz, zr, 128), BF16), sqpair=((2, pairs, zr, 128), BF16),
+        gc=((2, 3, HD, wide), BF16), sq=((2, 3, HD, wide), BF16),
+        sqin=((2, 3, nz, zr, 128), BF16), sqpair=((2, 3, pairs, zr, 128), BF16),
         acc=((nh, 2 * HD, rows), F32), pin_kv=((nh // dph, max(dph - 1, 1), 2 * HD, rows), F32),
         dkvsend=((nh, 2 * HD, rows), BF16), dqsend=((nh, HD, tq), BF16),
         dqkv=((heads, 3 * HD, rows), BF16), dsib=((heads // 2, 3 * HD, rows), BF16),
@@ -941,8 +1062,8 @@
         fs=(nh, dph), fr=(nh,), osd=(nh,), orc=(2 * heads, per),
         as_=(nz,), ar=(nz,), ps_=(nz,), pr=(nz,), ds=(2, heads, per), dr=(nh,),
         ys=(5,), yr=(5,), zss=(nz,), zsr=(nz,), pas=(pairs,), par=(pairs,),
-        sqs=(2, nz), sqr=(2, nz), sqps=(2, pairs), sqpr=(2, pairs), sgs=(2, nz), sgr=(2, nz),
-        sys=(2,), syr=(2,), scs=(2,), scr=(2,),
+        sqs=(2, 3, nz), sqr=(2, 3, nz), sqps=(2, 3, pairs), sqpr=(2, 3, pairs), sgs=(2, 3, nz), sgr=(2, 3, nz),
+        sxs=(3,), sxr=(3,), sys=(2, 3), syr=(2, 3), sbs=(2, 3), sbr=(2, 3), scs=(2, 3), scr=(2, 3),
         pks=(nh,), pkr=(nh // dph, max(dph - 1, 1)), dqs=(nh,), dqr=(heads, dph), dks=(nh,), dkr=(heads,),
         ts=(heads,), tr=(heads // 2,), v4s=(3,), v4r=(4,), vzs=(nz,), vzr=(nz,), vbs=(nb,), vbr=(nb,),
     )

time: 154 us -> 139 us (0.903)
  Pallas kernels: 152 us -> 138 us
    pallas_call x1, Pallas kernels: 147 us -> 134 us  [local(): pl.pallas_call(functools.partial(layer_kernel, names, sizes), out_shape=[...]
where the time goes in v4:
time: 139 us
  Pallas kernels  138 us (99%)
    pallas_call x1, Pallas kernels, local(): pl.pallas_call(functools.partial(layer_kernel, names, sizes), out_shape=[...  134 us
    pallas_call x1, Pallas kernels, local(): pl.pallas_call(functools.partial(final_kernel, heads), out_shape=[jax.Sha...  4.16 us

profile of v4, /device:TPU:0, one launch (start us, length us, event | category | flops | bytes accessed | tf_op | source)
XLA Modules:
  0.0 138.9 jit_solution(13319366893830294945)
XLA Ops:
  0.7 134.0 %shard_map.288 = (bf16[512,256]{1,0:T(8,128)(2,1)}, f32[512,256]{1,0:T(8,128)}, bf16[2,2,128,256]{3,2,1,0:T(8,128)(2,1)}, bf16[2,2,2,3,64,512]{5,4,3,2,1,0:T(8,128)(2,1)}, f32[8,256]{1,0:T(8,128)}) custom-call(s32[1,3]{1,0:T(1,128)} %refs_0_.1, bf16[512,256]{1,0:T(8,128)(2,1)} %refs_1_.1, bf16[512,256]{1,0:T(8,128)(2,1)} %refs_2_.1, f32[1,256]{1,0:T(1,128)} %bitcast.12, ...), custom_call_target="tpu_custom_call" | custom-call | flops 10000000000 | bytes 10000000 | tf_op jit(solution)/shard_map/pallas_call | solution.py:1072
  134.7 4.2 %shard_map.289 = (bf16[512,256]{1,0:T(8,128)(2,1)}, f32[512,256]{1,0:T(8,128)}, f32[1,256]{1,0:T(1,128)}, f32[1,256]{1,0:T(1,128)}, f32[512,256]{1,0:T(8,128)}, ...) custom-call(bf16[512,256]{1,0:T(8,128)(2,1)} %get-tuple-element.37.r, ...), custom_call_target="tpu_custom_call" | custom-call | tf_op jit(solution)/shard_map/pallas_call | solution.py:1090

commit v5 on v4

--- a/solution.py
+++ b/solution.py
@@ -15,6 +15,12 @@
 BF16 = jnp.bfloat16
 NEG = -1e30
 VMEM_LIMIT = 62 * 1024 * 1024
+HALVING = False
+PLAN = {
+    "begin": ("a1",), "row0": (), "col0": ("bx",), "row1": (), "col1": ("bz",), "row2": ("a2",), "col2": (),
+    "loop": ("a3", "bg"), "whole": (), "sent": (), "proj": ("cy", "a4", "a5"), "half": ("cz",),
+    "norm": ("bb",), "vec": ("cg", "a6"), "rows": (), "last": ("bc", "cb"), "end": ("cc",),
+}
 SCALE = HD**-0.5
 
 
@@ -147,39 +153,52 @@
     r.wup[z, c, w] = r.wu[...]
     r.wdn[z, c, w] = r.wd[...]
 
+    def weight_blocks(distance):
+        for kind, buf in enumerate((r.wup, r.wdn)):
+            for step in (1, -1) if distance else (1,):
+                zz = z - step * distance
+                index = jnp.clip(zz, 0, nz - 1)
+                yield (zz >= 0) & (zz < nz) & (bp == kind), index, buf, step
+
     def weight_hop(k, ending=False):
-        for kind, buf in enumerate((r.wup, r.wdn)):
-            for way, step in enumerate((1, -1)):
-                zz = z - step * (k - 1)
-                onward = (z + step >= 0) & (z + step < nz)
-                here = (zz >= 0) & (zz < nz) & (bp == kind)
-                here = here & (jnp.logical_not(onward) if ending else onward)
-                index = jnp.clip(zz, 0, nz - 1)
+        for here, index, buf, step in weight_blocks(k - 1):
+            for way in (1, -1) if k == 1 else (step,):
+                onward = (z + way >= 0) & (z + way < nz)
+                going = here & (jnp.logical_not(onward) if ending else onward)
                 block = buf.at[index, c, w]
                 if k > 1:
 
-                    @pl.when(here)
+                    @pl.when(going)
                     def _(block=block, index=index):
                         await_copy(block, r.wzr.at[index])
+                        remote(block, block, r.wxs.at[index], r.wxr.at[index], x_dev).start()
+                        remote(block, block, r.wys.at[index, w], r.wyr.at[index, w], y_dev).start()
 
                 if not ending:
-                    dev = (b, 2 * jnp.clip(z + step, 0, nz - 1) + c, w)
-                    copy = remote(block, block, r.wzs.at[way, k], r.wzr.at[index], dev)
-                    sends.start_if(here, copy)
-                if k > 1:
-                    copy = remote(block, block, r.wxs.at[way, k - 1], r.wxr.at[index], x_dev)
-                    sends.start_if(here, copy)
-                    copy = remote(block, block, r.wys.at[way, k - 1], r.wyr.at[index, w], y_dev)
-                    sends.start_if(here, copy)
-
-    for kind, buf in enumerate((r.wup, r.wdn)):
-        block = buf.at[z, c, w]
-        sends.start_if(bp == kind, remote(block, block, r.wxs.at[0, 0], r.wxr.at[z], x_dev))
+                    dev = (b, 2 * jnp.clip(z + way, 0, nz - 1) + c, w)
+                    copy = remote(block, block, r.wzs.at[(1 - way) // 2, k], r.wzr.at[index], dev)
+                    sends.start_if(going, copy)
+
+    def weight_cross(distance):
+        for here, index, buf, _ in weight_blocks(distance):
+
+            @pl.when(here)
+            def _(index=index, buf=buf):
+                block = buf.at[index, c, 1 - w]
+                await_copy(block, r.wxr.at[index])
+                remote(block, block, r.wys.at[index, 1 - w], r.wyr.at[index, 1 - w], y_dev).start()
+
+    for here, index, buf, _ in weight_blocks(0):
+        block = buf.at[index, c, w]
+        copy = remote(block, block, r.wxs.at[index], r.wxr.at[index], x_dev)
+
+        @pl.when(here)
+        def _(copy=copy):
+            copy.start()
+
     weight_hop(1)
     gates = ((r.wg1, r.g1f), (r.wg2, r.g2f), (r.wo, r.wof))
-    for i, (src, dst) in enumerate(gates):
-        piece = at(c, src.shape[0] // 2)
-        sends.start(remote(src.at[piece], dst.at[w, piece], r.gxs.at[i], r.gxr.at[i], x_dev))
+    for src, dst in gates:
         dst[w] = src[...]
     ccopy = remote(r.cot.at[theirs], r.cotr.at[:, own], r.xs.at[3], r.xr.at[3], x_dev)
     r.vecf[:, own] = r.vsrc[...]
@@ -207,50 +226,55 @@
             r.qsrc[t, :, part] = qkv[:HD]
             r.kvsrc[t, :, part] = qkv[HD:]
 
-    def send_heads(step, k):
+    def head_copies(step, k):
         t = lax.rem(group + step, heads)
         span = pl.ds(k * half, half)
         src, dst = r.kvsrc.at[t, :, span], r.kvt.at[h, :, span]
         if step:
-            dev = (b, t * dph + sub, w)
-            sends.start(remote(src, dst, r.ks.at[step, k], r.kr.at[h, k], dev))
+            yield None, remote(src, dst, r.ks.at[step, k], r.kr.at[h, k], (b, t * dph + sub, w))
         else:
-            pltpu.make_async_copy(src, dst, r.kr.at[h, k]).start()
+            yield None, pltpu.make_async_copy(src, dst, r.kr.at[h, k])
         for i in range(per):
             row = k * per + i
             target = sub_row(h, row, dph)
             src, dst = r.qsrc.at[t, :, pl.ds(row * tq, tq)], r.qt.at[h]
             copy = remote(src, dst, r.qs.at[step, row], r.qr.at[h], (b, t * dph + target, w))
             if step:
-                sends.start(copy)
+                yield None, copy
             else:
-                sends.start_if(target != sub, copy)
-
-                @pl.when(target == sub)
-                def _(src=src, dst=dst):
-                    pltpu.make_async_copy(src, dst, r.qr.at[h]).start()
-
+                yield target != sub, copy
+                yield target == sub, pltpu.make_async_copy(src, dst, r.qr.at[h])
+
+    def send_heads(step, k):
+        for cond, copy in head_copies(step, k):
+            if cond is None:
+                copy.start()
+            else:
+
+                @pl.when(cond)
+                def _(copy=copy):
+                    copy.start()
+
+    def heads_sent():
+        for k in range(2):
+            for step in range(1, heads):
+                for _, copy in head_copies(step, k):
+                    copy.wait_send()
+            for i in range(per):
+                row = k * per + i
+
+                @pl.when(sub_row(h, row, dph) != sub)
+                def _(row=row):
+                    await_copy(r.qt.at[h], r.qs.at[0, row])
+
+    project(0)
     weight_hop(2)
-    project(0)
+    weight_hop(2, ending=True)
     send_heads(heads - 1, 0)
-    weight_hop(3)
     project(1)
     send_heads(heads - 1, 1)
-    for step in range(heads - 2, -1, -1):
-        for k in range(2):
-            send_heads(step, k)
-
-
-    def weights_over_y():
-        for kind, buf in enumerate((r.wup, r.wdn)):
-
-            @pl.when(bp == kind)
-            def _(buf=buf):
-                for k in range(nz):
-                    zz, _ = z_dev(k)
-                    block = buf.at[zz, c, 1 - w]
-                    await_copy(block, r.wxr.at[zz])
-                    remote(block, block, r.wyd.at[zz], r.wyr.at[zz, 1 - w], y_dev).start()
+    for k in range(2):
+        send_heads(0, k)
 
     def weights_over_core():
         for kind, buf in enumerate((r.wup, r.wdn)):
@@ -277,8 +301,13 @@
 
             @pl.when(bp == kind)
             def _(buf=buf):
+                block = buf.at[z, c, w]
                 for k in range(nz):
-                    await_copy(buf.at[z, c, w], r.wyd.at[k])
+                    zz, _ = z_dev(k)
+                    await_copy(block, r.wxs.at[zz])
+                    await_copy(block, r.wys.at[zz, 1 - w])
+                    if k:
+                        await_copy(block, r.wys.at[zz, w])
 
         for i, (src, dst) in enumerate(gates):
             await_copy(dst.at[1 - w, at(c, src.shape[0] // 2)], r.gcs.at[i])
@@ -365,16 +394,15 @@
     def completes(chip):
         return jnp.where(z == 0, chip, nz - z + jnp.minimum(chip, z - 1))
 
-    def forward_stage(d, _):
-        n = lax.rem(z + d, nz)
-
-        @pl.when(d == nz // 2)
-        def _():
-            weights_over_y()
-            gates_over_core()
-
-        pass_on(2 * n)
-        pass_on(2 * n + 1)
+    def chip_at(d):
+        return lax.rem(z + d, nz)
+
+    def stage_passes(d):
+        pass_on(2 * chip_at(d))
+        pass_on(2 * chip_at(d) + 1)
+
+    def stage_computes(d):
+        n = chip_at(d)
         arrive(2 * n)
         arrive(2 * n + 1)
         own_chip(n)
@@ -405,19 +433,46 @@
             send_attended(2 * n)
             send_attended(2 * n + 1)
 
+    def late_stage(d, _):
+        stage_passes(d)
+
+        @pl.when(d == 2)
+        def _():
+            for distance in range(2):
+                weight_cross(distance)
+
+        @pl.when(d == nz - 1)
+        def _():
+            weight_hop(nz, ending=True)
+            for distance in range(2, nz - 1):
+                weight_cross(distance)
+
+        stage_computes(d)
         return 0
 
     r.top[...] = jnp.full_like(r.top, NEG)
     r.total[...] = jnp.zeros_like(r.total)
     r.ot[...] = jnp.zeros_like(r.ot)
-    forward_stage(0, 0)
+    stage_passes(0)
+    stage_computes(0)
+    for k in range(2):
+        send_heads(2, k)
+    for i, (src, dst) in enumerate(gates):
+        piece = at(c, src.shape[0] // 2)
+        sends.start(remote(src.at[piece], dst.at[w, piece], r.gxs.at[i], r.gxr.at[i], x_dev))
     sends.start(remote(r.npair.at[c], r.npair.at[c], r.cs.at[0], r.cr.at[0], c_dev))
-    for k in range(4, nz):
+    stage_passes(1)
+    for k in range(3, nz):
         weight_hop(k)
-    for k in range(2, nz + 1):
+    for k in range(3, nz):
         weight_hop(k, ending=True)
+    for k in range(2):
+        send_heads(1, k)
+    stage_computes(1)
     sends.start(ccopy)
-    lax.fori_loop(1, nz, forward_stage, 0)
+    lax.fori_loop(2, nz, late_stage, 0)
+    weight_cross(nz - 1)
+    gates_over_core()
     weights_over_core()
 
     for i, (src, dst) in enumerate(gates):
@@ -556,7 +611,7 @@
             for y in range(2):
                 r.gb[v, y, m] = block[y * eighth : (y + 1) * eighth]
     for m in range(3):
-        sends.start(remote(r.gb.at[1 - w, :, m], r.xbin.at[:, m], r.sxs.at[m], r.sxr.at[m], x_dev))
+        sends.start(remote(r.gb.at[:, 1 - bp, m], r.ybin.at[:, m], r.sys.at[m], r.syr.at[m], y_dev))
     await_copy(r.npt.at[:, lanes], r.cr.at[1])
     await_copy(r.gbt.at[:, lanes], r.cr.at[2])
 
@@ -569,8 +624,15 @@
 
     lax.fori_loop(0, nz, weight_grads, 0)
     sends.start(remote(r.ga.at[0, :, 1 - w], r.xin0, r.xs.at[5], r.xr.at[5], x_dev))
-    sends.start(remote(r.ga.at[1, :, :, 1 - bp], r.yin1, r.ys.at[1], r.yr.at[1], y_dev))
-
+
+
+    def z_block(q, flip_bit, v):
+        bit = lax.rem(lax.div(z, 1 << q), 2)
+        bit = 1 - bit if flip_bit else bit
+        return lax.rem(z, 1 << q) + bit * (1 << q) + v * (2 << q)
+
+    def ffn_first():
+        remote(r.ga.at[1, :, :, 1 - bp], r.yin1, r.ys.at[1], r.yr.at[1], y_dev).start()
 
     def ffn_second():
         await_copy(r.xin0, r.xr.at[5])
@@ -586,11 +648,6 @@
         r.zs[:, 0] = (r.ga[0, :, w, bp].astype(F32) + r.yin0[...].astype(F32)).astype(BF16)
         r.zs[:, 1] = (r.ga[1, :, w, bp].astype(F32) + r.xin1[...].astype(F32)).astype(BF16)
         ffn_hop(0)
-
-    def z_block(q, flip_bit, v):
-        bit = lax.rem(lax.div(z, 1 << q), 2)
-        bit = 1 - bit if flip_bit else bit
-        return lax.rem(z, 1 << q) + bit * (1 << q) + v * (2 << q)
 
     def ffn_hop(q):
         if q:
@@ -617,7 +674,7 @@
             for k in range(1, pairs):
                 dev = (lax.rem(b + 2 * k, nb), h, w)
                 block = r.pin.at[mypair]
-                sends.start(remote(block, block, r.pas.at[k], r.par.at[mypair], dev))
+                remote(block, block, r.pas.at[k], r.par.at[mypair], dev).start()
             for k in range(1, pairs):
                 pp = lax.rem(mypair + k, pairs)
                 await_copy(r.pin.at[pp], r.par.at[pp])
@@ -626,9 +683,13 @@
                 total = total + r.pin[k].astype(F32)
         r.red_a[bp] = total.astype(BF16)
         block = r.red_a.at[bp]
-        sends.start(remote(block, block, r.ys.at[3], r.yr.at[3], y_dev))
+        remote(block, block, r.ys.at[3], r.yr.at[3], y_dev).start()
 
     def ffn_sent():
+        await_copy(r.red_a.at[bp], r.ys.at[3])
+        for k in range(1, pairs):
+            await_copy(r.pin.at[0], r.pas.at[k])
+        await_copy(r.yin1, r.ys.at[1])
         await_copy(r.yin0, r.ys.at[2])
         await_copy(r.xin1, r.xs.at[6])
         for k in range(nz - 1):
@@ -639,60 +700,78 @@
     def z_part(zz):
         return pl.ds(pl.multiple_of(lax.div(zz, 4) * zr, zr), zr), at(lax.rem(zz, 4), 128)
 
-    def square_y(which):
+    def square_x():
         for p in range(3):
-            if which == 0:
-                await_copy(r.xbin.at[:, p], r.sxr.at[p])
-                r.gb[w, :, p] = (r.gb[w, :, p].astype(F32) + r.xbin[:, p].astype(F32)).astype(BF16)
-                src = r.gb.at[w, 1 - bp, p]
+            await_copy(r.ybin.at[:, p], r.syr.at[p])
+            r.gb[:, bp, p] = (r.gb[:, bp, p].astype(F32) + r.ybin[:, p].astype(F32)).astype(BF16)
+            remote(r.gb.at[1 - w, bp, p], r.xbin.at[p], r.sxs.at[p], r.sxr.at[p], x_dev).start()
+
+    def z_peer(q):
+        return (b, 2 * (z + (1 << q) * (1 - 2 * lax.rem(lax.div(z, 1 << q), 2))) + c, w)
+
+    def z_slots(q):
+        return [(nz - (nz >> q) + v, v) for v in range(nz >> (q + 1))]
+
+    def square_add(which, p, q):
+        for slot, v in z_slots(q):
+            await_copy(r.sqin.at[which, p, slot], r.sqr.at[which, p, slot])
+            kept = (which, p) + z_part(z_block(q, False, v))
+            r.sq[kept] = (r.sq[kept].astype(F32) + r.sqin[which, p, slot].astype(F32)).astype(BF16)
+
+    def square_hop(which, q):
+        for p in range(3):
+            if q == 0:
+                await_copy(r.xbin.at[p], r.sxr.at[p])
+                r.sq[which, p] = (r.gb[w, bp, p].astype(F32) + r.xbin[p].astype(F32)).astype(BF16)
             else:
-                src = r.gc.at[1 - bp, p]
-            remote(src, r.yin.at[which, p], r.sys.at[which, p], r.syr.at[which, p], y_dev).start()
-
-    def square_z(which):
+                square_add(which, p, q - 1)
+            for slot, v in z_slots(q):
+                src = r.sq.at[(which, p) + z_part(z_block(q, True, v))]
+                dst = r.sqin.at[which, p, slot]
+                remote(src, dst, r.sqs.at[which, p, slot], r.sqr.at[which, p, slot], z_peer(q)).start()
+
+    def spread_part(which, p, q):
+        for slot, v in z_slots(q):
+            block = r.red_s.at[(which, c, bp, p) + z_part(z_block(q, False, v))]
+            remote(block, block, r.sgs.at[which, p, slot], r.sgr.at[which, p, slot], z_peer(q)).start()
+
+    def spread_await(which, p, q):
+        for slot, v in z_slots(q):
+            block = r.red_s.at[(which, c, bp, p) + z_part(z_block(q, True, v))]
+            await_copy(block, r.sgr.at[which, p, slot])
+
+    def over_pairs(which, p, total):
+        if pairs == 1:
+            return total
+        mypair = lax.div(b, 2)
+        r.sqpair[which, p, mypair] = total
+        for k in range(1, pairs):
+            dev = (lax.rem(b + 2 * k, nb), h, w)
+            block = r.sqpair.at[which, p, mypair]
+            remote(block, block, r.sqps.at[which, p, k], r.sqpr.at[which, p, mypair], dev).start()
+        for k in range(1, pairs):
+            pp = lax.rem(mypair + k, pairs)
+            await_copy(r.sqpair.at[which, p, pp], r.sqpr.at[which, p, pp])
+        total = r.sqpair[which, p, 0].astype(F32)
+        for k in range(1, pairs):
+            total = total + r.sqpair[which, p, k].astype(F32)
+        return total.astype(BF16)
+
+    def square_turn(which):
         for p in range(3):
-            await_copy(r.yin.at[which, p], r.syr.at[which, p])
-            mine_part = r.gb[w, bp, p] if which == 0 else r.gc[bp, p]
-            r.sq[which, p] = (mine_part.astype(F32) + r.yin[which, p].astype(F32)).astype(BF16)
-            for k in range(nz - 1, 0, -1):
-                zz, dev = z_dev(k)
-                src = r.sq.at[(which, p) + z_part(zz)]
-                slot = r.sqin.at[which, p, z]
-                remote(src, slot, r.sqs.at[which, p, k], r.sqr.at[which, p, z], dev).start()
-
-    def square_spread(which):
+            square_add(which, p, hops - 1)
+            total = over_pairs(which, p, r.sq[(which, p) + z_part(z)])
+            r.red_s[(which, c, bp, p) + z_part(z)] = total
+            spread_part(which, p, hops - 1)
+
+    def square_spread(which, q):
         for p in range(3):
-            r.sqin[which, p, z] = r.sq[(which, p) + z_part(z)]
-            for k in range(1, nz):
-                zz, _ = z_dev(k)
-                await_copy(r.sqin.at[which, p, zz], r.sqr.at[which, p, zz])
-            total = r.sqin[which, p, 0].astype(F32)
-            for k in range(1, nz):
-                total = total + r.sqin[which, p, k].astype(F32)
-            if pairs > 1:
-                mypair = lax.div(b, 2)
-                r.sqpair[which, p, mypair] = total.astype(BF16)
-                for k in range(1, pairs):
-                    dev = (lax.rem(b + 2 * k, nb), h, w)
-                    block = r.sqpair.at[which, p, mypair]
-                    remote(block, block, r.sqps.at[which, p, k], r.sqpr.at[which, p, mypair], dev).start()
-                for k in range(1, pairs):
-                    pp = lax.rem(mypair + k, pairs)
-                    await_copy(r.sqpair.at[which, p, pp], r.sqpr.at[which, p, pp])
-                total = r.sqpair[which, p, 0].astype(F32)
-                for k in range(1, pairs):
-                    total = total + r.sqpair[which, p, k].astype(F32)
-            r.red_s[(which, c, bp, p) + z_part(z)] = total.astype(BF16)
-            for k in range(nz - 1, 0, -1):
-                _, dev = z_dev(k)
-                block = r.red_s.at[(which, c, bp, p) + z_part(z)]
-                remote(block, block, r.sgs.at[which, p, k], r.sgr.at[which, p, z], dev).start()
+            spread_await(which, p, q + 1)
+            spread_part(which, p, q)
 
     def square_back(which):
         for p in range(3):
-            for k in range(1, nz):
-                zz, _ = z_dev(k)
-                await_copy(r.red_s.at[(which, c, bp, p) + z_part(zz)], r.sgr.at[which, p, zz])
+            spread_await(which, p, 0)
             block = r.red_s.at[which, c, bp, p]
             remote(block, block, r.sbs.at[which, p], r.sbr.at[which, p], y_dev).start()
 
@@ -702,17 +781,87 @@
             block = r.red_s.at[which, c, :, p]
             remote(block, block, r.scs.at[which, p], r.scr.at[which, p], c_dev).start()
 
+    def scatter(which):
+        for p in range(3):
+            if which:
+                await_copy(r.ycin.at[p], r.pyr.at[p])
+                r.sq[1, p] = (r.gc[bp, p].astype(F32) + r.ycin[p].astype(F32)).astype(BF16)
+            else:
+                await_copy(r.xbin.at[p], r.sxr.at[p])
+                r.sq[0, p] = (r.gb[w, bp, p].astype(F32) + r.xbin[p].astype(F32)).astype(BF16)
+            for k in range(nz - 1, 0, -1):
+                zz, dev = z_dev(k)
+                src, dst = r.sq.at[(which, p) + z_part(zz)], r.pzin.at[which, p, z]
+                remote(src, dst, r.pzs.at[which, p, k], r.pzr.at[which, p, z], dev).start()
+
+    def gather(which):
+        for p in range(3):
+            total = r.sq[(which, p) + z_part(z)].astype(F32)
+            for k in range(1, nz):
+                zz, _ = z_dev(k)
+                await_copy(r.pzin.at[which, p, zz], r.pzr.at[which, p, zz])
+                total = total + r.pzin[which, p, zz].astype(F32)
+            block = (which, c, bp, p) + z_part(z)
+            r.red_s[block] = over_pairs(which, p, total.astype(BF16))
+            for k in range(nz - 1, 0, -1):
+                _, dev = z_dev(k)
+                ref = r.red_s.at[block]
+                remote(ref, ref, r.pgs.at[which, p, k], r.pgr.at[which, p, z], dev).start()
+
+    def back(which):
+        for p in range(3):
+            for k in range(1, nz):
+                zz, _ = z_dev(k)
+                await_copy(r.red_s.at[(which, c, bp, p) + z_part(zz)], r.pgr.at[which, p, zz])
+            block = r.red_s.at[which, c, bp, p]
+            remote(block, block, r.sbs.at[which, p], r.sbr.at[which, p], y_dev).start()
+
+    def proj_y():
+        for p in range(3):
+            remote(r.gc.at[1 - bp, p], r.ycin.at[p], r.pys.at[p], r.pyr.at[p], y_dev).start()
+
     def square_end(which):
         for p in range(3):
             await_copy(r.red_s.at[which, 1 - c, :, p], r.scr.at[which, p])
             await_copy(r.red_s.at[which, c, :, p], r.scs.at[which, p])
-            await_copy(r.yin.at[which, p], r.sys.at[which, p])
-            await_copy(r.yin.at[which, p], r.sbs.at[which, p])
-            for k in range(1, nz):
-                await_copy(r.sqin.at[which, p, z], r.sqs.at[which, p, k])
-                await_copy(r.sqin.at[which, p, z], r.sgs.at[which, p, k])
-                if k < pairs:
-                    await_copy(r.sqpair.at[which, p, 0], r.sqps.at[which, p, k])
+            await_copy(r.xbin.at[p], r.sbs.at[which, p])
+            if which == 0:
+                await_copy(r.xbin.at[p], r.sxs.at[p])
+            else:
+                await_copy(r.ycin.at[p], r.pys.at[p])
+            if which == 0 and HALVING:
+                for slot in range(nz - 1):
+                    await_copy(r.sqin.at[which, p, slot], r.sqs.at[which, p, slot])
+                    await_copy(r.sqin.at[which, p, slot], r.sgs.at[which, p, slot])
+            else:
+                for k in range(1, nz):
+                    await_copy(r.pzin.at[which, p, z], r.pzs.at[which, p, k])
+                    await_copy(r.pzin.at[which, p, z], r.pgs.at[which, p, k])
+            for k in range(1, pairs):
+                await_copy(r.sqpair.at[which, p, 0], r.sqps.at[which, p, k])
+
+    def each(step, *args):
+        return lambda: [step(*(a if isinstance(a, tuple) else (a,))) for a in args]
+
+    later = list(range(2, hops))
+    down_again = list(range(hops - 2, -1, -1))
+    steps = dict(
+        a1=ffn_first, a2=ffn_second, a3=ffn_third, a4=lambda: ffn_hop(1), a5=each(ffn_hop, *later), a6=ffn_fourth,
+        bx=square_x, cy=proj_y, cz=lambda: scatter(1), cg=lambda: gather(1), cb=lambda: back(1),
+        cc=lambda: square_core(1), bc=lambda: square_core(0),
+    )
+    if HALVING:
+        steps.update(
+            bz0=lambda: square_hop(0, 0), bz1=lambda: square_hop(0, 1), bz2=each(square_hop, *[(0, q) for q in later]),
+            bt=lambda: square_turn(0), bs=each(square_spread, *[(0, q) for q in down_again]),
+            bb=lambda: square_back(0),
+        )
+    else:
+        steps.update(bz=lambda: scatter(0), bg=lambda: gather(0), bb=lambda: back(0))
+
+    def take(point):
+        for name in PLAN[point]:
+            steps[name]()
 
     r.acc[...] = jnp.zeros_like(r.acc)
 
@@ -794,53 +943,66 @@
         lo, hi = t, nh - 1 - t
         n = hi - lo + 1
 
+        rowed = lax.div(n, 2)
+        columned = rowed - 1
+
         def row_step(v, _):
             where = [pair_at(t, 2 * v), pair_at(t, 2 * v + 1)]
-            diagonal = v == lax.div(n, 2) - 1
-            choose([(t == 0, (True, True)), (diagonal, (False, True)), (True, (False, False))], where)
+            choose([(t == 0, (True, True)), (v == rowed - 1, (False, True)), (True, (False, False))], where)
+
+            @pl.when((t > 0) & (v == jnp.minimum(1, rowed - 1)))
+            def _():
+                finish(lo - 1)
+
             return 0
 
-        lax.fori_loop(0, lax.div(n, 2), row_step, 0)
+        lax.fori_loop(0, rowed, row_step, 0)
         send_block(hi)
 
         @pl.when(t == 0)
         def _():
             lax.fori_loop(0, nh - 1, lambda s, z: (out_arrives(s), z)[1], 0)
 
-        @pl.when(t > 0)
-        def _():
-            finish(lo - 1)
+        for at_round, point in ((0, "row0"), (nh // 8, "row1"), (nh // 4, "row2")):
+            if PLAN[point]:
+
+                @pl.when(t == at_round)
+                def _(point=point):
+                    take(point)
 
         def column_step(v, _):
             where = [pair_at(t, n + 2 * v), pair_at(t, n + 2 * v + 1)]
             choose([(v == 0, (True, False)), (True, (False, False))], where)
+
+            @pl.when(v == jnp.minimum(1, columned - 1))
+            def _():
+                finish(hi)
+
             return 0
 
-        lax.fori_loop(0, lax.div(n, 2) - 1, column_step, 0)
+        lax.fori_loop(0, columned, column_step, 0)
         pairs_backward([pair_at(t, 2 * n - 2)], (True,))
         send_block(lo)
-        finish(hi)
-
-        @pl.when(t == 0)
-        def _():
-            square_y(0)
-
-        @pl.when(t == nh // 8)
-        def _():
-            square_z(0)
-
-        @pl.when(t == nh // 4)
-        def _():
-            ffn_second()
+
+        @pl.when(columned == 0)
+        def _():
+            finish(hi)
+
+        for at_round, point in ((0, "col0"), (nh // 8, "col1"), (nh // 4, "col2")):
+            if PLAN[point]:
+
+                @pl.when(t == at_round)
+                def _(point=point):
+                    take(point)
 
         return 0
 
     r.dqa[...] = jnp.zeros_like(r.dqa)
     out_arrives(nh - 1)
+    take("begin")
     lax.fori_loop(0, nh // 2, round_backward, 0)
     finish(nh // 2 - 1)
-    ffn_third()
-    square_spread(0)
+    take("loop")
 
     for t in range(heads):
         await_copy(r.dqkv.at[t, pl.ds(HD, 2 * HD), :], r.dkr.at[t])
@@ -849,6 +1011,7 @@
         sends.start_if(
             t % 2 != c, remote(r.dqkv.at[t], r.dsib.at[t // 2], r.ts.at[t], r.tr.at[t // 2], c_dev)
         )
+    take("whole")
     wts = r.wt[...].reshape(heads * 3 * HD, wide)
 
     def grad_normed(span):
@@ -857,21 +1020,20 @@
     r.psend[...] = grad_normed(theirs).astype(BF16)
     pcopy = remote(r.psend, r.precv, r.xs.at[8], r.xr.at[8], x_dev)
     sends.start(pcopy)
+    take("sent")
     await_copy(r.npair.at[1 - c], r.cr.at[0])
     for j in range(heads // 2):
         await_copy(r.dsib.at[j], r.tr.at[j])
         part = nn(r.dqkv[2 * j + c], r.npair[c]) + nn(r.dsib[j], r.npair[1 - c])
         for p in range(3):
             r.gc[j, p] = part[p * HD : (p + 1) * HD].astype(BF16)
-    square_y(1)
-    for q in range(1, hops):
-        ffn_hop(q)
+    take("proj")
     gnorm = grad_normed(mine) + r.gterm[...]
     x = r.tokf[mine, :].astype(F32)
     centre = x - jnp.mean(x, -1, keepdims=True)
     rstd = lax.rsqrt(jnp.mean(centre * centre, -1, keepdims=True) + EPSILON)
     n = centre * rstd
-    square_z(1)
+    take("half")
     pcopy.wait_recv()
     gnorm = gnorm + r.precv[...].astype(F32)
     e = gnorm * r.vecf[0:1, :]
@@ -894,7 +1056,7 @@
                 sends.start(remote(r.vin4.at[me4], r.vin4.at[me4], r.v4s.at[k], r.v4r.at[me4], dev))
                 k += 1
     r.gtok[mine, :] = jnp.where(w == 0, result[:, :cw], result[:, cw:])
-    square_back(0)
+    take("norm")
     for dc in range(2):
         for dw in range(2):
             if dc or dw:
@@ -904,11 +1066,11 @@
     for k in range(1, nz):
         _, dev = z_dev(k)
         sends.start(remote(r.vinz.at[z], r.vinz.at[z], r.vzs.at[k], r.vzr.at[z], dev))
-    square_spread(1)
-    ffn_fourth()
+    take("vec")
     tcopy.wait_recv()
     r.gtok[theirs, :] = r.trecv[...].astype(F32)
     ocopy.wait_recv()
+    take("rows")
     for k in range(1, nz):
         zz, _ = z_dev(k)
         await_copy(r.vinz.at[zz], r.vzr.at[zz])
@@ -919,8 +1081,7 @@
     for k in range(1, nb):
         dev = (lax.rem(b + k, nb), h, w)
         sends.start(remote(r.vinb.at[b], r.vinb.at[b], r.vbs.at[k], r.vbr.at[b], dev))
-    square_core(0)
-    square_back(1)
+    take("last")
     for k in range(1, nb):
         bb = lax.rem(b + k, nb)
         await_copy(r.vinb.at[bb], r.vbr.at[bb])
@@ -928,8 +1089,8 @@
     for k in range(1, nb):
         total = total + r.vinb[k]
     r.red_v[...] = jnp.where(w == 0, total[:, :cw], total[:, cw:])
+    take("end")
     await_copy(r.red_a.at[1 - bp], r.yr.at[3])
-    square_core(1)
 
     def sent(s, _):
         row = sub_row(s, sub, dph)
@@ -960,6 +1121,7 @@
 
     lax.fori_loop(0, nh, sent, 0)
     weights_sent()
+    heads_sent()
     for i2 in range(nz):
         await_copy(r.acts.at[i2], r.as_.at[i2])
         await_copy(r.gpres.at[i2], r.ps_.at[i2])
@@ -1041,13 +1203,13 @@
         ginp=((half, wide), F32), gterm=((half, wide), F32), npt=((wide, rows), BF16), gbt=((wide, rows), BF16),
         lsrc=((3, wide, half), BF16), bpair=((3, rows, wide), BF16), apair=((3, 2, quarter, rows), BF16),
         vsum=((8, wide), F32),
-        gb=((2, 2, 3, HD, wide), BF16), xbin=((2, 3, HD, wide), BF16), yin=((2, 3, HD, wide), BF16),
+        gb=((2, 2, 3, HD, wide), BF16), ybin=((2, 3, HD, wide), BF16), xbin=((3, HD, wide), BF16),
         ga=((2, nz, 2, 2, quarter, units), BF16), xin0=((nz, 2, quarter, units), BF16),
         yin1=((nz, 2, quarter, units), BF16), yin0=((nz, quarter, units), BF16), xin1=((nz, quarter, units), BF16),
         zs=((nz, 2, quarter, units), BF16), zin=((nz, 2, quarter, units), BF16),
         pin=((pairs, 2, quarter, units), BF16),
-        gc=((2, 3, HD, wide), BF16), sq=((2, 3, HD, wide), BF16),
-        sqin=((2, 3, nz, zr, 128), BF16), sqpair=((2, 3, pairs, zr, 128), BF16),
+        gc=((2, 3, HD, wide), BF16), ycin=((3, HD, wide), BF16), sq=((2, 3, HD, wide), BF16),
+        sqin=((1, 3, nz - 1, zr, 128), BF16), pzin=((2, 3, nz, zr, 128), BF16), sqpair=((2, 3, pairs, zr, 128), BF16),
         acc=((nh, 2 * HD, rows), F32), pin_kv=((nh // dph, max(dph - 1, 1), 2 * HD, rows), F32),
         dkvsend=((nh, 2 * HD, rows), BF16), dqsend=((nh, HD, tq), BF16),
         dqkv=((heads, 3 * HD, rows), BF16), dsib=((heads // 2, 3 * HD, rows), BF16),
@@ -1058,12 +1220,13 @@
     sems = dict(
         xs=(10,), xr=(10,), wzs=(2, nz), wzr=(nz,), gxs=(3,), gxr=(3,), gcs=(3,), gcr=(3,),
         ks=(heads, 2), kr=(nh, 2), qs=(heads, dph), qr=(nh,), cs=(12,), cr=(12,),
-        wxs=(2, nz), wxr=(nz,), wys=(2, nz), wyr=(nz, 2), wyd=(nz,), wcs=(2,), wcr=(2,),
+        wxs=(nz,), wxr=(nz,), wys=(nz, 2), wyr=(nz, 2), wcs=(2,), wcr=(2,),
         fs=(nh, dph), fr=(nh,), osd=(nh,), orc=(2 * heads, per),
         as_=(nz,), ar=(nz,), ps_=(nz,), pr=(nz,), ds=(2, heads, per), dr=(nh,),
         ys=(5,), yr=(5,), zss=(nz,), zsr=(nz,), pas=(pairs,), par=(pairs,),
-        sqs=(2, 3, nz), sqr=(2, 3, nz), sqps=(2, 3, pairs), sqpr=(2, 3, pairs), sgs=(2, 3, nz), sgr=(2, 3, nz),
-        sxs=(3,), sxr=(3,), sys=(2, 3), syr=(2, 3), sbs=(2, 3), sbr=(2, 3), scs=(2, 3), scr=(2, 3),
+        sqs=(1, 3, nz), sqr=(1, 3, nz), sqps=(2, 3, pairs), sqpr=(2, 3, pairs), sgs=(1, 3, nz), sgr=(1, 3, nz),
+        pys=(3,), pyr=(3,), pzs=(2, 3, nz), pzr=(2, 3, nz), pgs=(2, 3, nz), pgr=(2, 3, nz),
+        sxs=(3,), sxr=(3,), sys=(3,), syr=(3,), sbs=(2, 3), sbr=(2, 3), scs=(2, 3), scr=(2, 3),
         pks=(nh,), pkr=(nh // dph, max(dph - 1, 1)), dqs=(nh,), dqr=(heads, dph), dks=(nh,), dkr=(heads,),
         ts=(heads,), tr=(heads // 2,), v4s=(3,), v4r=(4,), vzs=(nz,), vzr=(nz,), vbs=(nb,), vbr=(nb,),
     )

time: 139 us -> 137 us (0.986)
  Pallas kernels: 138 us -> 136 us
    pallas_call x1, Pallas kernels: 134 us -> 132 us  [local(): pl.pallas_call(functools.partial(layer_kernel, names, sizes), out_shape=[...]
where the time goes in v5:
time: 137 us
  Pallas kernels  136 us (99%)
    pallas_call x1, Pallas kernels, local(): pl.pallas_call(functools.partial(layer_kernel, names, sizes), out_shape=[...  132 us
    pallas_call x1, Pallas kernels, local(): pl.pallas_call(functools.partial(final_kernel, heads), out_shape=[jax.Sha...  4.16 us

profile of v5, /device:TPU:0, one launch (start us, length us, event | category | flops | bytes accessed | tf_op | source)
XLA Modules:
  0.0 136.8 jit_solution(12740550267038292466)
XLA Ops:
  0.7 131.8 %shard_map.288 = (bf16[512,256]{1,0:T(8,128)(2,1)}, f32[512,256]{1,0:T(8,128)}, bf16[2,2,128,256]{3,2,1,0:T(8,128)(2,1)}, bf16[2,2,2,3,64,512]{5,4,3,2,1,0:T(8,128)(2,1)}, f32[8,256]{1,0:T(8,128)}) custom-call(s32[1,3]{1,0:T(1,128)} %refs_0_.1, bf16[512,256]{1,0:T(8,128)(2,1)} %refs_1_.1, bf16[512,256]{1,0:T(8,128)(2,1)} %refs_2_.1, f32[1,256]{1,0:T(1,128)} %bitcast.12, ...), custom_call_target="tpu_custom_call" | custom-call | flops 10000000000 | bytes 10000000 | tf_op jit(solution)/shard_map/pallas_call | solution.py:1235
  132.5 4.2 %shard_map.289 = (bf16[512,256]{1,0:T(8,128)(2,1)}, f32[512,256]{1,0:T(8,128)}, f32[1,256]{1,0:T(1,128)}, f32[1,256]{1,0:T(1,128)}, f32[512,256]{1,0:T(8,128)}, ...) custom-call(bf16[512,256]{1,0:T(8,128)(2,1)} %get-tuple-element.37.r, ...), custom_call_target="tpu_custom_call" | custom-call | tf_op jit(solution)/shard_map/pallas_call | solution.py:1253

commit v6 on v5

--- a/solution.py
+++ b/solution.py
@@ -1,4 +1,5 @@
 import functools
+import math
 import types
 
 import jax
@@ -15,11 +16,10 @@
 BF16 = jnp.bfloat16
 NEG = -1e30
 VMEM_LIMIT = 62 * 1024 * 1024
-HALVING = False
 PLAN = {
     "begin": ("a1",), "row0": (), "col0": ("bx",), "row1": (), "col1": ("bz",), "row2": ("a2",), "col2": (),
-    "loop": ("a3", "bg"), "whole": (), "sent": (), "proj": ("cy", "a4", "a5"), "half": ("cz",),
-    "norm": ("bb",), "vec": ("cg", "a6"), "rows": (), "last": ("bc", "cb"), "end": ("cc",),
+    "loop": ("a3", "bg"), "whole": (), "sent": (), "proj": ("cy", "a4"), "half": ("cz",),
+    "norm": ("bb",), "vec": ("cg", "a5"), "rows": (), "last": ("bc", "cb"), "end": ("cc",),
 }
 SCALE = HD**-0.5
 
@@ -72,13 +72,27 @@
     return 1.0 / (1.0 + jnp.exp(-x))
 
 
+def nbytes(ref):
+    return math.prod(ref.shape) * ref.dtype.itemsize
+
+
 class Sends:
-    def __init__(self):
+    def __init__(self, sems, tally):
+        self.sems, self.tally = sems, tally
+        self.bytes = {}
         self.items = []
 
-    def start(self, copy):
+    def sem(self, group):
+        return self.sems.at[group]
+
+    def count(self, group, *sizes):
+        self.bytes[group] = self.bytes.get(group, 0) + sum(sizes)
+
+    def go(self, src, dst, recv, dev, group=0):
+        copy = remote(src, dst, self.sem(group), recv, dev)
         copy.start()
-        self.items.append((None, copy))
+        self.count(group, nbytes(src))
+        return copy
 
     def start_if(self, cond, copy):
         @pl.when(cond)
@@ -87,15 +101,17 @@
 
         self.items.append((cond, copy))
 
+    def wait(self, group, size):
+        await_copy(self.tally.at[pl.ds(0, size // 512)], self.sem(group))
+
     def finish(self):
+        for group, size in self.bytes.items():
+            self.wait(group, size)
         for cond, copy in self.items:
-            if cond is None:
+
+            @pl.when(cond)
+            def _(copy=copy):
                 copy.wait_send()
-            else:
-
-                @pl.when(cond)
-                def _(copy=copy):
-                    copy.wait_send()
 
 
 def layer_kernel(names, sizes, *refs):
@@ -124,7 +140,8 @@
         r.lens[0, 0] + r.lens[0, 1],
         r.lens[0, 0] + r.lens[0, 1] + r.lens[0, 2],
     ]
-    sends = Sends()
+    sends = Sends(r.snd, r.tally)
+    SUMS, LOOPS, ROWS, WEIGHTS, BACK = 3, 4, 5, 6, 7
 
     barrier = pltpu.get_barrier_semaphore()
     count = 0
@@ -138,20 +155,28 @@
         dev = (lax.rem(b + db, nb), h, w)
         pl.semaphore_signal(barrier, inc=1, device_id=dev, device_id_type=MESH)
         count += 1
-    pl.semaphore_wait(barrier, count)
-
+    loads = dict(
+        tok0=(r.tok.at[pl.ds(0, half)], r.tokf.at[pl.ds(0, half), own]),
+        tok1=(r.tok.at[pl.ds(half, half)], r.tokf.at[pl.ds(half, half), own]),
+        wu=(r.wu, r.wup.at[z, c, w]), wd=(r.wd, r.wdn.at[z, c, w]),
+        wq=(r.wq, r.wqkv.at[0]), wk=(r.wk, r.wqkv.at[1]), wv=(r.wv, r.wqkv.at[2]),
+        wg1=(r.wg1, r.g1f.at[w]), wg2=(r.wg2, r.g2f.at[w]), wo=(r.wo, r.wof.at[w]),
+        cot=(r.cot.at[mine], r.cotr.at[:, own]),
+    )
+    shared = dict(tok0=0, tok1=1, wu=2, wd=2, wq=3, wk=3, wv=3, wg1=4, wg2=4, wo=4, cot=5)
+    for name, (src, dst) in loads.items():
+        pltpu.make_async_copy(src, dst, r.ls.at[shared[name]]).start()
     for i, vec in enumerate((r.v0, r.v1, r.v2, r.v3, r.v4, r.v5)):
         r.vsrc[i : i + 1, :] = vec[...]
-    vcopy = remote(r.vsrc, r.vecf.at[:, own], r.xs.at[0], r.xr.at[0], x_dev)
-    sends.start(vcopy)
+    pl.semaphore_wait(barrier, count)
+
+    vcopy = sends.go(r.vsrc, r.vecf.at[:, own], r.xr.at[0], x_dev)
     tcopies = []
     for k in range(2):
-        part = pl.ds(k * half, half)
-        copy = remote(r.tok.at[part], r.tokf.at[part, own], r.xs.at[1 + k], r.xr.at[1 + k], x_dev)
-        sends.start(copy)
-        tcopies.append(copy)
-    r.wup[z, c, w] = r.wu[...]
-    r.wdn[z, c, w] = r.wd[...]
+        block = r.tokf.at[pl.ds(k * half, half), own]
+        await_copy(block, r.ls.at[k])
+        tcopies.append(sends.go(block, block, r.xr.at[1 + k], x_dev))
+    await_copy(r.wup.at[z, c], r.ls.at[2])
 
     def weight_blocks(distance):
         for kind, buf in enumerate((r.wup, r.wdn)):
@@ -171,8 +196,8 @@
                     @pl.when(going)
                     def _(block=block, index=index):
                         await_copy(block, r.wzr.at[index])
-                        remote(block, block, r.wxs.at[index], r.wxr.at[index], x_dev).start()
-                        remote(block, block, r.wys.at[index, w], r.wyr.at[index, w], y_dev).start()
+                        remote(block, block, sends.sem(WEIGHTS), r.wxr.at[index], x_dev).start()
+                        remote(block, block, sends.sem(WEIGHTS), r.wyr.at[0], y_dev).start()
 
                 if not ending:
                     dev = (b, 2 * jnp.clip(z + way, 0, nz - 1) + c, w)
@@ -186,11 +211,11 @@
             def _(index=index, buf=buf):
                 block = buf.at[index, c, 1 - w]
                 await_copy(block, r.wxr.at[index])
-                remote(block, block, r.wys.at[index, 1 - w], r.wyr.at[index, 1 - w], y_dev).start()
+                remote(block, block, sends.sem(WEIGHTS), r.wyr.at[0], y_dev).start()
 
     for here, index, buf, _ in weight_blocks(0):
         block = buf.at[index, c, w]
-        copy = remote(block, block, r.wxs.at[index], r.wxr.at[index], x_dev)
+        copy = remote(block, block, sends.sem(WEIGHTS), r.wxr.at[index], x_dev)
 
         @pl.when(here)
         def _(copy=copy):
@@ -198,15 +223,11 @@
 
     weight_hop(1)
     gates = ((r.wg1, r.g1f), (r.wg2, r.g2f), (r.wo, r.wof))
-    for src, dst in gates:
-        dst[w] = src[...]
-    ccopy = remote(r.cot.at[theirs], r.cotr.at[:, own], r.xs.at[3], r.xr.at[3], x_dev)
     r.vecf[:, own] = r.vsrc[...]
-    r.tokf[:, own] = r.tok[...]
-    r.cotr[:, own] = r.cot[mine, :]
-
-    for i, weight in enumerate((r.wq, r.wk, r.wv)):
-        turned = flip(weight[...])
+
+    await_copy(r.wqkv, r.ls.at[3])
+    for i in range(3):
+        turned = flip(r.wqkv[i])
         for t in range(heads):
             r.wt[t, i * HD : (i + 1) * HD, :] = turned[t * HD : (t + 1) * HD]
 
@@ -231,14 +252,14 @@
         span = pl.ds(k * half, half)
         src, dst = r.kvsrc.at[t, :, span], r.kvt.at[h, :, span]
         if step:
-            yield None, remote(src, dst, r.ks.at[step, k], r.kr.at[h, k], (b, t * dph + sub, w))
+            yield None, remote(src, dst, sends.sem(LOOPS), r.kr.at[h], (b, t * dph + sub, w))
         else:
-            yield None, pltpu.make_async_copy(src, dst, r.kr.at[h, k])
+            yield None, pltpu.make_async_copy(src, dst, r.kr.at[h])
         for i in range(per):
             row = k * per + i
             target = sub_row(h, row, dph)
             src, dst = r.qsrc.at[t, :, pl.ds(row * tq, tq)], r.qt.at[h]
-            copy = remote(src, dst, r.qs.at[step, row], r.qr.at[h], (b, t * dph + target, w))
+            copy = remote(src, dst, sends.sem(LOOPS), r.qr.at[h], (b, t * dph + target, w))
             if step:
                 yield None, copy
             else:
@@ -254,18 +275,6 @@
                 @pl.when(cond)
                 def _(copy=copy):
                     copy.start()
-
-    def heads_sent():
-        for k in range(2):
-            for step in range(1, heads):
-                for _, copy in head_copies(step, k):
-                    copy.wait_send()
-            for i in range(per):
-                row = k * per + i
-
-                @pl.when(sub_row(h, row, dph) != sub)
-                def _(row=row):
-                    await_copy(r.qt.at[h], r.qs.at[0, row])
 
     project(0)
     weight_hop(2)
@@ -276,50 +285,36 @@
     for k in range(2):
         send_heads(0, k)
 
+    def sends_of(count, buf, sem):
+        await_copy(r.tally.at[pl.ds(0, count * nbytes(buf.at[0, 0, 0]) // 512)], sem)
+
     def weights_over_core():
         for kind, buf in enumerate((r.wup, r.wdn)):
 
             @pl.when(bp != kind)
             def _(buf=buf):
-                for k in range(nz):
-                    zz, _ = z_dev(k)
-                    if k:
-                        await_copy(buf.at[zz, c, w], r.wyr.at[zz, w])
-                    await_copy(buf.at[zz, c, 1 - w], r.wyr.at[zz, 1 - w])
+                sends_of(2 * nz - 1, buf, r.wyr.at[0])
 
             block = buf.at[:, c]
-            sends.start(remote(block, block, r.wcs.at[kind], r.wcr.at[kind], c_dev))
+            sends.go(block, block, r.wcr.at[kind], c_dev, 1)
 
     def gates_over_core():
         for i, (src, dst) in enumerate(gates):
             piece = dst.at[1 - w, at(c, src.shape[0] // 2)]
-            await_copy(piece, r.gxr.at[i])
-            remote(piece, piece, r.gcs.at[i], r.gcr.at[i], c_dev).start()
+            if i == 0:
+                await_copy(r.tally.at[pl.ds(0, 3 * nbytes(piece) // 512)], r.gxr.at[0])
+            sends.go(piece, piece, r.gcr.at[0], c_dev)
 
     def weights_sent():
-        for kind, buf in enumerate((r.wup, r.wdn)):
-
-            @pl.when(bp == kind)
-            def _(buf=buf):
-                block = buf.at[z, c, w]
-                for k in range(nz):
-                    zz, _ = z_dev(k)
-                    await_copy(block, r.wxs.at[zz])
-                    await_copy(block, r.wys.at[zz, 1 - w])
-                    if k:
-                        await_copy(block, r.wys.at[zz, w])
-
-        for i, (src, dst) in enumerate(gates):
-            await_copy(dst.at[1 - w, at(c, src.shape[0] // 2)], r.gcs.at[i])
+        sends.wait(WEIGHTS, (3 * nz - 1) * nbytes(r.wu))
 
     def pass_on(s):
         @pl.when(lax.rem(s, dph) == sub)
         def _():
-            for k in range(2):
-                await_copy(r.kvt.at[s, :, pl.ds(k * half, half)], r.kr.at[s, k])
+            await_copy(r.kvt.at[s], r.kr.at[s])
             for k in range(1, dph):
                 dev = (b, group * dph + lax.rem(sub + k, dph), w)
-                remote(r.kvt.at[s], r.kvt.at[s], r.fs.at[s, k], r.fr.at[s], dev).start()
+                remote(r.kvt.at[s], r.kvt.at[s], sends.sem(LOOPS), r.fr.at[s], dev).start()
 
     def arrive(s):
         @pl.when(lax.rem(s, dph) != sub)
@@ -362,7 +357,7 @@
         row_w = lax.div(row * tq, half)
         lane = lax.rem(row * tq, half)
         dst = r.att.at[at(w * heads + group, HD), pl.ds(pl.multiple_of(lane, tq), tq)]
-        slot = r.orc.at[w * heads + group, lax.div(lane, tq)]
+        slot = r.orc.at[0]
         here = (s == h) & (row_w == w)
 
         @pl.when(here)
@@ -371,7 +366,7 @@
 
         @pl.when(jnp.logical_not(here))
         def _():
-            remote(r.osend.at[s], dst, r.osd.at[s], slot, (b, s, row_w)).start()
+            remote(r.osend.at[s], dst, sends.sem(ROWS), slot, (b, s, row_w)).start()
 
     def own_chip(n):
         i = 2 * n
@@ -408,6 +403,10 @@
         own_chip(n)
 
         def with_earlier(e, _):
+            @pl.when((d == nz - 1) & (e == 1))
+            def _():
+                weight_cross(nz - 1)
+
             m = lax.rem(z + e, nz)
             hi, lo = jnp.maximum(n, m), jnp.minimum(n, m)
 
@@ -457,10 +456,11 @@
     stage_computes(0)
     for k in range(2):
         send_heads(2, k)
-    for i, (src, dst) in enumerate(gates):
-        piece = at(c, src.shape[0] // 2)
-        sends.start(remote(src.at[piece], dst.at[w, piece], r.gxs.at[i], r.gxr.at[i], x_dev))
-    sends.start(remote(r.npair.at[c], r.npair.at[c], r.cs.at[0], r.cr.at[0], c_dev))
+    await_copy(r.wqkv, r.ls.at[4])
+    for src, dst in gates:
+        block = dst.at[w, at(c, src.shape[0] // 2)]
+        sends.go(block, block, r.gxr.at[0], x_dev)
+    sends.go(r.npair.at[c], r.npair.at[c], r.cr.at[0], c_dev)
     stage_passes(1)
     for k in range(3, nz):
         weight_hop(k)
@@ -469,14 +469,13 @@
     for k in range(2):
         send_heads(1, k)
     stage_computes(1)
-    sends.start(ccopy)
+    await_copy(r.cotr.at[:, own], r.ls.at[5])
+    sends.go(r.cot.at[theirs], r.cotr.at[:, own], r.xr.at[3], x_dev)
     lax.fori_loop(2, nz, late_stage, 0)
-    weight_cross(nz - 1)
     gates_over_core()
     weights_over_core()
 
-    for i, (src, dst) in enumerate(gates):
-        await_copy(dst.at[1 - w, at(1 - c, src.shape[0] // 2)], r.gcr.at[i])
+    await_copy(r.tally.at[pl.ds(0, 3 * nbytes(r.wg1) // 1024)], r.gcr.at[0])
 
     def two(a, weight):
         return jnp.concatenate([nn(a, weight[0]), nn(a, weight[1])], 1)
@@ -487,9 +486,7 @@
     tok = r.tokf[mine, :].astype(F32)
     n1 = r.npair[c, mine, :]
     gate_one = sigmoid(two(n1, r.g1f) + r.vecf[2:3, :])
-    for g in range(2 * heads):
-        for i in range(per):
-            await_copy(r.att.at[pl.ds(g * HD, HD), pl.ds(i * tq, tq)], r.orc.at[g, i])
+    await_copy(r.att, r.orc.at[0])
     wof = r.wof[...].reshape(wide, wide)
     branch_one = nn(flip(r.att[...]), wof)
     middle = tok + gate_one * (branch_one - tok)
@@ -511,21 +508,22 @@
             pre = nn(normed_two, r.wup[i, q].reshape(wide, units))
             r.pre[i2, p] = pre
             act = jax.nn.gelu(pre).astype(BF16)
-            branch = branch + jnp.concatenate([nn(act, r.wdn[i, q, 0]), nn(act, r.wdn[i, q, 1])], 1)
+            r.actall[:, pl.ds(pl.multiple_of((2 * i + q) * units, units), units)] = act
             if p:
                 r.acts[i2] = act
                 dst = r.actp.at[i2, lanes, :]
-                remote(r.acts.at[i2], dst, r.as_.at[i2], r.ar.at[i2], c_dev).start()
+                remote(r.acts.at[i2], dst, sends.sem(LOOPS), r.ar.at[0], c_dev).start()
             else:
                 r.actp[i2, lanes, :] = act
         return branch
 
-    branch_two = lax.fori_loop(0, nz, up, jnp.zeros(middle.shape, F32))
+    lax.fori_loop(0, nz, up, 0)
+    deep = nh * units
+    branch_two = jnp.concatenate([nn(r.actall[...], r.wdn[:, :, v].reshape(deep, cw)) for v in range(2)], 1)
     delta = branch_two - middle
     r.outr[...] = (middle + gate_two * delta).astype(BF16)
-    ocopy = remote(r.outr.at[:, other], r.out_c.at[mine, :], r.xs.at[4], r.xr.at[4], x_dev)
-    sends.start(ocopy)
-    ccopy.wait_recv()
+    ocopy = sends.go(r.outr.at[:, other], r.out_c.at[mine, :], r.xr.at[4], x_dev)
+    await_copy(r.cotr.at[:, own], r.xr.at[3])
     grad = r.cotr[...].astype(F32)
     gb2 = (grad * gate_two).astype(BF16)
     gl2 = (grad * delta * gate_two * (1.0 - gate_two)).astype(BF16)
@@ -544,7 +542,7 @@
             if p:
                 r.gpres[i2] = gpre
                 dst = r.gprep.at[i2, lanes, :]
-                remote(r.gpres.at[i2], dst, r.ps_.at[i2], r.pr.at[i2], c_dev).start()
+                remote(r.gpres.at[i2], dst, sends.sem(LOOPS), r.pr.at[0], c_dev).start()
             else:
                 r.gprep[i2, lanes, :] = gpre
         return total
@@ -565,22 +563,26 @@
                 src = r.gatt.at[at(wt * heads + t, HD), pl.ds(i * tq, tq)]
                 dst = r.dot.at[h]
                 dev = (b, t * dph + target, wt)
-                copy = remote(src, dst, r.ds.at[dw, step, i], r.dr.at[h], dev)
+                slot = r.dr.at[jnp.where(h == nh - 1, 1, 0)]
+                copy = remote(src, dst, sends.sem(ROWS), slot, dev)
                 if step or dw:
-                    sends.start(copy)
+                    copy.start()
                 else:
-                    sends.start_if(target != sub, copy)
+
+                    @pl.when(target != sub)
+                    def _(copy=copy):
+                        copy.start()
 
                     @pl.when(target == sub)
-                    def _(src=src, dst=dst):
-                        pltpu.make_async_copy(src, dst, r.dr.at[h]).start()
+                    def _(src=src, dst=dst, slot=slot):
+                        pltpu.make_async_copy(src, dst, slot).start()
 
     gl1 = (gmid * (branch_one - tok) * gate_one * (1.0 - gate_one)).astype(BF16)
     r.ginp[...] = gmid * (1.0 - gate_one)
     r.npt[:, lanes] = flip(normed_two)
-    sends.start(remote(r.npt.at[:, lanes], r.npt.at[:, lanes], r.cs.at[1], r.cr.at[1], c_dev))
+    sends.go(r.npt.at[:, lanes], r.npt.at[:, lanes], r.cr.at[1], c_dev)
     r.gbt[:, lanes] = flip(gb2)
-    sends.start(remote(r.gbt.at[:, lanes], r.gbt.at[:, lanes], r.cs.at[2], r.cr.at[2], c_dev))
+    sends.go(r.gbt.at[:, lanes], r.gbt.at[:, lanes], r.cr.at[1], c_dev)
     quarter = half // 2
     r.lsrc[0] = r.att[...]
     r.lsrc[1] = flip(gl1)
@@ -588,11 +590,11 @@
     for m, right in enumerate((gb1, n1, normed_two)):
         r.bpair[m, lanes, :] = right
         block = r.bpair.at[m, lanes, :]
-        sends.start(remote(block, block, r.cs.at[3 + m], r.cr.at[3 + m], c_dev))
+        sends.go(block, block, r.cr.at[2], c_dev, 2)
         for v in range(2):
             src = r.lsrc.at[m, at(2 * v + 1 - c, quarter), :]
             dst = r.apair.at[m, v, :, lanes]
-            sends.start(remote(src, dst, r.cs.at[6 + 2 * m + v], r.cr.at[6 + 2 * m + v], c_dev))
+            sends.go(src, dst, r.cr.at[2], c_dev, 2)
             r.apair[m, v, :, lanes] = r.lsrc[m, at(2 * v + c, quarter), :]
     r.gterm[...] = two_back(gl1, r.g1f)
     r.vsum[...] = jnp.zeros_like(r.vsum)
@@ -603,27 +605,26 @@
     r.out_c[mine, :] = r.outr[:, own]
 
     eighth = quarter // 2
+    await_copy(r.npt, r.cr.at[1])
+    await_copy(r.gpres, r.pr.at[0])
+    await_copy(r.acts, r.ar.at[0])
+
+    def weight_grads(i2, _):
+        r.ga[0, i2] = nn(r.npt[...], r.gprep[i2]).astype(BF16).reshape(2, 2, quarter, units)
+        r.ga[1, i2] = nn(r.gbt[...], r.actp[i2]).astype(BF16).reshape(2, 2, quarter, units)
+        return 0
+
+    lax.fori_loop(0, nz, weight_grads, 0)
+    sends.go(r.ga.at[0, :, 1 - w], r.xin0, r.xr.at[5], x_dev, 2)
+    pair_bytes = 3 * (nbytes(r.bpair.at[0, lanes, :]) + 2 * nbytes(r.apair.at[0, 0, :, lanes]))
+    await_copy(r.tally.at[pl.ds(0, pair_bytes // 512)], r.cr.at[2])
     for m in range(3):
-        await_copy(r.bpair.at[m, lanes, :], r.cr.at[3 + m])
         for v in range(2):
-            await_copy(r.apair.at[m, v, :, lanes], r.cr.at[6 + 2 * m + v])
             block = nn(r.apair[m, v], r.bpair[m]).astype(BF16)
             for y in range(2):
                 r.gb[v, y, m] = block[y * eighth : (y + 1) * eighth]
     for m in range(3):
-        sends.start(remote(r.gb.at[:, 1 - bp, m], r.ybin.at[:, m], r.sys.at[m], r.syr.at[m], y_dev))
-    await_copy(r.npt.at[:, lanes], r.cr.at[1])
-    await_copy(r.gbt.at[:, lanes], r.cr.at[2])
-
-    def weight_grads(i2, _):
-        await_copy(r.gprep.at[i2, lanes, :], r.pr.at[i2])
-        await_copy(r.actp.at[i2, lanes, :], r.ar.at[i2])
-        r.ga[0, i2] = nn(r.npt[...], r.gprep[i2]).astype(BF16).reshape(2, 2, quarter, units)
-        r.ga[1, i2] = nn(r.gbt[...], r.actp[i2]).astype(BF16).reshape(2, 2, quarter, units)
-        return 0
-
-    lax.fori_loop(0, nz, weight_grads, 0)
-    sends.start(remote(r.ga.at[0, :, 1 - w], r.xin0, r.xs.at[5], r.xr.at[5], x_dev))
+        sends.go(r.gb.at[:, 1 - bp, m], r.ybin.at[:, m], r.syr.at[0], y_dev, 2)
 
 
     def z_block(q, flip_bit, v):
@@ -632,15 +633,15 @@
         return lax.rem(z, 1 << q) + bit * (1 << q) + v * (2 << q)
 
     def ffn_first():
-        remote(r.ga.at[1, :, :, 1 - bp], r.yin1, r.ys.at[1], r.yr.at[1], y_dev).start()
+        remote(r.ga.at[1, :, :, 1 - bp], r.yin1, sends.sem(SUMS), r.yr.at[1], y_dev).start()
 
     def ffn_second():
         await_copy(r.xin0, r.xr.at[5])
         r.ga[0, :, w] = (r.ga[0, :, w].astype(F32) + r.xin0[...].astype(F32)).astype(BF16)
-        remote(r.ga.at[0, :, w, 1 - bp], r.yin0, r.ys.at[2], r.yr.at[2], y_dev).start()
+        remote(r.ga.at[0, :, w, 1 - bp], r.yin0, sends.sem(SUMS), r.yr.at[2], y_dev).start()
         await_copy(r.yin1, r.yr.at[1])
         r.ga[1, :, :, bp] = (r.ga[1, :, :, bp].astype(F32) + r.yin1[...].astype(F32)).astype(BF16)
-        remote(r.ga.at[1, :, 1 - w, bp], r.xin1, r.xs.at[6], r.xr.at[6], x_dev).start()
+        remote(r.ga.at[1, :, 1 - w, bp], r.xin1, sends.sem(SUMS), r.xr.at[6], x_dev).start()
 
     def ffn_third():
         await_copy(r.yin0, r.yr.at[2])
@@ -656,7 +657,7 @@
         dev = (b, 2 * (z + (1 << q) * (1 - 2 * bit)) + c, w)
         for v in range(nz >> (q + 1)):
             slot = nz - (nz >> q) + v
-            remote(r.zs.at[z_block(q, True, v)], r.zin.at[slot], r.zss.at[slot], r.zsr.at[slot], dev).start()
+            remote(r.zs.at[z_block(q, True, v)], r.zin.at[slot], sends.sem(SUMS), r.zsr.at[slot], dev).start()
 
     def ffn_add(q):
         for v in range(nz >> (q + 1)):
@@ -674,7 +675,7 @@
             for k in range(1, pairs):
                 dev = (lax.rem(b + 2 * k, nb), h, w)
                 block = r.pin.at[mypair]
-                remote(block, block, r.pas.at[k], r.par.at[mypair], dev).start()
+                remote(block, block, sends.sem(SUMS), r.par.at[mypair], dev).start()
             for k in range(1, pairs):
                 pp = lax.rem(mypair + k, pairs)
                 await_copy(r.pin.at[pp], r.par.at[pp])
@@ -683,17 +684,13 @@
                 total = total + r.pin[k].astype(F32)
         r.red_a[bp] = total.astype(BF16)
         block = r.red_a.at[bp]
-        remote(block, block, r.ys.at[3], r.yr.at[3], y_dev).start()
-
-    def ffn_sent():
-        await_copy(r.red_a.at[bp], r.ys.at[3])
-        for k in range(1, pairs):
-            await_copy(r.pin.at[0], r.pas.at[k])
-        await_copy(r.yin1, r.ys.at[1])
-        await_copy(r.yin0, r.ys.at[2])
-        await_copy(r.xin1, r.xs.at[6])
-        for k in range(nz - 1):
-            await_copy(r.zin.at[k], r.zss.at[k])
+        remote(block, block, sends.sem(SUMS), r.yr.at[3], y_dev).start()
+
+    def sums_sent():
+        sends.count(SUMS, nbytes(r.yin1), nbytes(r.yin0), nbytes(r.xin1), nbytes(r.red_a.at[0]))
+        sends.count(SUMS, (nz - 1) * nbytes(r.zin.at[0]), (pairs - 1) * nbytes(r.pin.at[0]))
+        sends.count(SUMS, nbytes(r.xbin), nbytes(r.ycin), 2 * nbytes(r.ycin), nbytes(r.red_s) // 2)
+        sends.count(SUMS, 6 * (2 * (nz - 1) + pairs - 1) * nbytes(r.pzin.at[0, 0, 0]))
 
     zr = HD * 4 // nz
 
@@ -701,44 +698,10 @@
         return pl.ds(pl.multiple_of(lax.div(zz, 4) * zr, zr), zr), at(lax.rem(zz, 4), 128)
 
     def square_x():
+        await_copy(r.ybin, r.syr.at[0])
         for p in range(3):
-            await_copy(r.ybin.at[:, p], r.syr.at[p])
             r.gb[:, bp, p] = (r.gb[:, bp, p].astype(F32) + r.ybin[:, p].astype(F32)).astype(BF16)
-            remote(r.gb.at[1 - w, bp, p], r.xbin.at[p], r.sxs.at[p], r.sxr.at[p], x_dev).start()
-
-    def z_peer(q):
-        return (b, 2 * (z + (1 << q) * (1 - 2 * lax.rem(lax.div(z, 1 << q), 2))) + c, w)
-
-    def z_slots(q):
-        return [(nz - (nz >> q) + v, v) for v in range(nz >> (q + 1))]
-
-    def square_add(which, p, q):
-        for slot, v in z_slots(q):
-            await_copy(r.sqin.at[which, p, slot], r.sqr.at[which, p, slot])
-            kept = (which, p) + z_part(z_block(q, False, v))
-            r.sq[kept] = (r.sq[kept].astype(F32) + r.sqin[which, p, slot].astype(F32)).astype(BF16)
-
-    def square_hop(which, q):
-        for p in range(3):
-            if q == 0:
-                await_copy(r.xbin.at[p], r.sxr.at[p])
-                r.sq[which, p] = (r.gb[w, bp, p].astype(F32) + r.xbin[p].astype(F32)).astype(BF16)
-            else:
-                square_add(which, p, q - 1)
-            for slot, v in z_slots(q):
-                src = r.sq.at[(which, p) + z_part(z_block(q, True, v))]
-                dst = r.sqin.at[which, p, slot]
-                remote(src, dst, r.sqs.at[which, p, slot], r.sqr.at[which, p, slot], z_peer(q)).start()
-
-    def spread_part(which, p, q):
-        for slot, v in z_slots(q):
-            block = r.red_s.at[(which, c, bp, p) + z_part(z_block(q, False, v))]
-            remote(block, block, r.sgs.at[which, p, slot], r.sgr.at[which, p, slot], z_peer(q)).start()
-
-    def spread_await(which, p, q):
-        for slot, v in z_slots(q):
-            block = r.red_s.at[(which, c, bp, p) + z_part(z_block(q, True, v))]
-            await_copy(block, r.sgr.at[which, p, slot])
+            remote(r.gb.at[1 - w, bp, p], r.xbin.at[p], sends.sem(SUMS), r.sxr.at[0], x_dev).start()
 
     def over_pairs(which, p, total):
         if pairs == 1:
@@ -748,7 +711,7 @@
         for k in range(1, pairs):
             dev = (lax.rem(b + 2 * k, nb), h, w)
             block = r.sqpair.at[which, p, mypair]
-            remote(block, block, r.sqps.at[which, p, k], r.sqpr.at[which, p, mypair], dev).start()
+            remote(block, block, sends.sem(SUMS), r.sqpr.at[which, p, mypair], dev).start()
         for k in range(1, pairs):
             pp = lax.rem(mypair + k, pairs)
             await_copy(r.sqpair.at[which, p, pp], r.sqpr.at[which, p, pp])
@@ -757,107 +720,55 @@
             total = total + r.sqpair[which, p, k].astype(F32)
         return total.astype(BF16)
 
-    def square_turn(which):
-        for p in range(3):
-            square_add(which, p, hops - 1)
-            total = over_pairs(which, p, r.sq[(which, p) + z_part(z)])
-            r.red_s[(which, c, bp, p) + z_part(z)] = total
-            spread_part(which, p, hops - 1)
-
-    def square_spread(which, q):
-        for p in range(3):
-            spread_await(which, p, q + 1)
-            spread_part(which, p, q)
-
-    def square_back(which):
-        for p in range(3):
-            spread_await(which, p, 0)
-            block = r.red_s.at[which, c, bp, p]
-            remote(block, block, r.sbs.at[which, p], r.sbr.at[which, p], y_dev).start()
-
-    def square_core(which):
-        for p in range(3):
-            await_copy(r.red_s.at[which, c, 1 - bp, p], r.sbr.at[which, p])
-            block = r.red_s.at[which, c, :, p]
-            remote(block, block, r.scs.at[which, p], r.scr.at[which, p], c_dev).start()
-
     def scatter(which):
         for p in range(3):
             if which:
                 await_copy(r.ycin.at[p], r.pyr.at[p])
                 r.sq[1, p] = (r.gc[bp, p].astype(F32) + r.ycin[p].astype(F32)).astype(BF16)
             else:
-                await_copy(r.xbin.at[p], r.sxr.at[p])
+                if p == 0:
+                    await_copy(r.xbin, r.sxr.at[0])
                 r.sq[0, p] = (r.gb[w, bp, p].astype(F32) + r.xbin[p].astype(F32)).astype(BF16)
             for k in range(nz - 1, 0, -1):
                 zz, dev = z_dev(k)
                 src, dst = r.sq.at[(which, p) + z_part(zz)], r.pzin.at[which, p, z]
-                remote(src, dst, r.pzs.at[which, p, k], r.pzr.at[which, p, z], dev).start()
+                remote(src, dst, sends.sem(SUMS), r.pzr.at[which, p], dev).start()
 
     def gather(which):
         for p in range(3):
             total = r.sq[(which, p) + z_part(z)].astype(F32)
+            await_copy(r.pzin.at[which, p, pl.ds(0, nz - 1)], r.pzr.at[which, p])
             for k in range(1, nz):
                 zz, _ = z_dev(k)
-                await_copy(r.pzin.at[which, p, zz], r.pzr.at[which, p, zz])
                 total = total + r.pzin[which, p, zz].astype(F32)
             block = (which, c, bp, p) + z_part(z)
             r.red_s[block] = over_pairs(which, p, total.astype(BF16))
             for k in range(nz - 1, 0, -1):
                 _, dev = z_dev(k)
                 ref = r.red_s.at[block]
-                remote(ref, ref, r.pgs.at[which, p, k], r.pgr.at[which, p, z], dev).start()
+                remote(ref, ref, sends.sem(SUMS), r.pgr.at[which, p], dev).start()
 
     def back(which):
         for p in range(3):
-            for k in range(1, nz):
-                zz, _ = z_dev(k)
-                await_copy(r.red_s.at[(which, c, bp, p) + z_part(zz)], r.pgr.at[which, p, zz])
+            await_copy(r.pzin.at[which, p, pl.ds(0, nz - 1)], r.pgr.at[which, p])
             block = r.red_s.at[which, c, bp, p]
-            remote(block, block, r.sbs.at[which, p], r.sbr.at[which, p], y_dev).start()
+            remote(block, block, sends.sem(SUMS), r.sbr.at[which, p], y_dev).start()
+
+    def square_core(which):
+        for p in range(3):
+            await_copy(r.red_s.at[which, c, 1 - bp, p], r.sbr.at[which, p])
+            block = r.red_s.at[which, c, :, p]
+            remote(block, block, sends.sem(SUMS), r.scr.at[which], c_dev).start()
 
     def proj_y():
         for p in range(3):
-            remote(r.gc.at[1 - bp, p], r.ycin.at[p], r.pys.at[p], r.pyr.at[p], y_dev).start()
-
-    def square_end(which):
-        for p in range(3):
-            await_copy(r.red_s.at[which, 1 - c, :, p], r.scr.at[which, p])
-            await_copy(r.red_s.at[which, c, :, p], r.scs.at[which, p])
-            await_copy(r.xbin.at[p], r.sbs.at[which, p])
-            if which == 0:
-                await_copy(r.xbin.at[p], r.sxs.at[p])
-            else:
-                await_copy(r.ycin.at[p], r.pys.at[p])
-            if which == 0 and HALVING:
-                for slot in range(nz - 1):
-                    await_copy(r.sqin.at[which, p, slot], r.sqs.at[which, p, slot])
-                    await_copy(r.sqin.at[which, p, slot], r.sgs.at[which, p, slot])
-            else:
-                for k in range(1, nz):
-                    await_copy(r.pzin.at[which, p, z], r.pzs.at[which, p, k])
-                    await_copy(r.pzin.at[which, p, z], r.pgs.at[which, p, k])
-            for k in range(1, pairs):
-                await_copy(r.sqpair.at[which, p, 0], r.sqps.at[which, p, k])
-
-    def each(step, *args):
-        return lambda: [step(*(a if isinstance(a, tuple) else (a,))) for a in args]
-
-    later = list(range(2, hops))
-    down_again = list(range(hops - 2, -1, -1))
+            remote(r.gc.at[1 - bp, p], r.ycin.at[p], sends.sem(SUMS), r.pyr.at[p], y_dev).start()
+
     steps = dict(
-        a1=ffn_first, a2=ffn_second, a3=ffn_third, a4=lambda: ffn_hop(1), a5=each(ffn_hop, *later), a6=ffn_fourth,
-        bx=square_x, cy=proj_y, cz=lambda: scatter(1), cg=lambda: gather(1), cb=lambda: back(1),
-        cc=lambda: square_core(1), bc=lambda: square_core(0),
+        a1=ffn_first, a2=ffn_second, a3=ffn_third, a4=lambda: [ffn_hop(q) for q in range(1, hops)], a5=ffn_fourth,
+        bx=square_x, bz=lambda: scatter(0), bg=lambda: gather(0), bb=lambda: back(0), bc=lambda: square_core(0),
+        cy=proj_y, cz=lambda: scatter(1), cg=lambda: gather(1), cb=lambda: back(1), cc=lambda: square_core(1),
     )
-    if HALVING:
-        steps.update(
-            bz0=lambda: square_hop(0, 0), bz1=lambda: square_hop(0, 1), bz2=each(square_hop, *[(0, q) for q in later]),
-            bt=lambda: square_turn(0), bs=each(square_spread, *[(0, q) for q in down_again]),
-            bb=lambda: square_back(0),
-        )
-    else:
-        steps.update(bz=lambda: scatter(0), bg=lambda: gather(0), bb=lambda: back(0))
 
     def take(point):
         for name in PLAN[point]:
@@ -883,7 +794,7 @@
 
             @pl.when(s != h)
             def _():
-                remote(r.dkvsend.at[s], dst, r.dks.at[s], r.dkr.at[group], (b, s, w)).start()
+                remote(r.dkvsend.at[s], dst, sends.sem(BACK), r.dkr.at[group], (b, s, w)).start()
 
     def pairs_backward(where, full):
         scores = [nn(r.kvn[j], r.qlow[i]) for i, j in where]
@@ -912,7 +823,6 @@
         return jnp.where(u < n, hi, lo + u - n), jnp.where(u < n, lo + u, lo)
 
     def out_arrives(s):
-        await_copy(r.dot.at[s], r.dr.at[s])
         dout = r.dot[s]
         r.dhigh[s] = jnp.concatenate([jnp.zeros((HD, tq), BF16), dout], 0)
         r.centre[s] = jnp.sum(r.ot[s] * dout.astype(F32), 0, keepdims=True)
@@ -924,11 +834,11 @@
 
         @pl.when(s == h)
         def _():
-            pltpu.make_async_copy(r.dqsend.at[s], dst, r.dqr.at[group, row]).start()
+            pltpu.make_async_copy(r.dqsend.at[s], dst, r.dkr.at[group]).start()
 
         @pl.when(s != h)
         def _():
-            remote(r.dqsend.at[s], dst, r.dqs.at[s], r.dqr.at[group, row], (b, s, w)).start()
+            remote(r.dqsend.at[s], dst, sends.sem(BACK), r.dkr.at[group], (b, s, w)).start()
 
         owner = lax.rem(s, dph)
 
@@ -937,7 +847,7 @@
             k = lax.rem(sub - owner + dph, dph)
             dev = (b, group * dph + owner, w)
             slot = lax.div(s, dph)
-            remote(r.acc.at[s], r.pin_kv.at[slot, k - 1], r.pks.at[s], r.pkr.at[slot, k - 1], dev).start()
+            remote(r.acc.at[s], r.pin_kv.at[slot, k - 1], sends.sem(BACK), r.pkr.at[slot, k - 1], dev).start()
 
     def round_backward(t, _):
         lo, hi = t, nh - 1 - t
@@ -961,6 +871,7 @@
 
         @pl.when(t == 0)
         def _():
+            await_copy(r.dot.at[pl.ds(0, nh - 1)], r.dr.at[0])
             lax.fori_loop(0, nh - 1, lambda s, z: (out_arrives(s), z)[1], 0)
 
         for at_round, point in ((0, "row0"), (nh // 8, "row1"), (nh // 4, "row2")):
@@ -998,19 +909,26 @@
         return 0
 
     r.dqa[...] = jnp.zeros_like(r.dqa)
+    await_copy(r.dot.at[nh - 1], r.dr.at[1])
     out_arrives(nh - 1)
     take("begin")
     lax.fori_loop(0, nh // 2, round_backward, 0)
     finish(nh // 2 - 1)
     take("loop")
 
+    def write(i, src, dst):
+        pltpu.make_async_copy(src, dst, r.os.at[i]).start()
+
+    ocopy.wait_recv()
+    write(0, r.out_c, r.h_out_c)
+
     for t in range(heads):
-        await_copy(r.dqkv.at[t, pl.ds(HD, 2 * HD), :], r.dkr.at[t])
-        for i in range(dph):
-            await_copy(r.dqkv.at[t, pl.ds(0, HD), pl.ds(i * tq, tq)], r.dqr.at[t, i])
-        sends.start_if(
-            t % 2 != c, remote(r.dqkv.at[t], r.dsib.at[t // 2], r.ts.at[t], r.tr.at[t // 2], c_dev)
-        )
+        await_copy(r.dqkv.at[t], r.dkr.at[t])
+
+        @pl.when(t % 2 != c)
+        def _(t=t):
+            remote(r.dqkv.at[t], r.dsib.at[t // 2], sends.sem(BACK), r.tr.at[0], c_dev).start()
+
     take("whole")
     wts = r.wt[...].reshape(heads * 3 * HD, wide)
 
@@ -1018,12 +936,11 @@
         return nn(flip(r.dqkv[:, :, span].reshape(heads * 3 * HD, half)), wts)
 
     r.psend[...] = grad_normed(theirs).astype(BF16)
-    pcopy = remote(r.psend, r.precv, r.xs.at[8], r.xr.at[8], x_dev)
-    sends.start(pcopy)
+    pcopy = sends.go(r.psend, r.precv, r.xr.at[8], x_dev)
     take("sent")
     await_copy(r.npair.at[1 - c], r.cr.at[0])
+    await_copy(r.dsib, r.tr.at[0])
     for j in range(heads // 2):
-        await_copy(r.dsib.at[j], r.tr.at[j])
         part = nn(r.dqkv[2 * j + c], r.npair[c]) + nn(r.dsib[j], r.npair[1 - c])
         for p in range(3):
             r.gc[j, p] = part[p * HD : (p + 1) * HD].astype(BF16)
@@ -1041,94 +958,75 @@
         e - jnp.mean(e, -1, keepdims=True) - n * jnp.mean(e * n, -1, keepdims=True)
     )
     r.tsend[...] = result.astype(BF16)
-    tcopy = remote(r.tsend.at[:, other], r.trecv, r.xs.at[9], r.xr.at[9], x_dev)
-    sends.start(tcopy)
+    tcopy = sends.go(r.tsend.at[:, other], r.trecv, r.xr.at[9], x_dev)
     r.vsum[0:1, :] = jnp.sum(gnorm * n, 0, keepdims=True)
     r.vsum[1:2, :] = jnp.sum(gnorm, 0, keepdims=True)
     me4 = 2 * c + w
     r.vin4[me4] = r.vsum[...]
-    k = 0
     for dc in range(2):
         for dw in range(2):
             if dc or dw:
                 cc, ww = lax.rem(c + dc, 2), lax.rem(w + dw, 2)
                 dev = (b, 2 * z + cc, ww)
-                sends.start(remote(r.vin4.at[me4], r.vin4.at[me4], r.v4s.at[k], r.v4r.at[me4], dev))
-                k += 1
+                sends.go(r.vin4.at[me4], r.vin4.at[me4], r.vr.at[0], dev)
     r.gtok[mine, :] = jnp.where(w == 0, result[:, :cw], result[:, cw:])
+    write(1, r.gtok.at[mine], r.h_gtok.at[mine])
     take("norm")
-    for dc in range(2):
-        for dw in range(2):
-            if dc or dw:
-                peer = 2 * lax.rem(c + dc, 2) + lax.rem(w + dw, 2)
-                await_copy(r.vin4.at[peer], r.v4r.at[peer])
+    await_copy(r.vin4.at[pl.ds(0, 3)], r.vr.at[0])
     r.vinz[z] = r.vin4[0] + r.vin4[1] + r.vin4[2] + r.vin4[3]
     for k in range(1, nz):
         _, dev = z_dev(k)
-        sends.start(remote(r.vinz.at[z], r.vinz.at[z], r.vzs.at[k], r.vzr.at[z], dev))
+        sends.go(r.vinz.at[z], r.vinz.at[z], r.vr.at[1], dev)
     take("vec")
     tcopy.wait_recv()
     r.gtok[theirs, :] = r.trecv[...].astype(F32)
-    ocopy.wait_recv()
+    write(1, r.gtok.at[theirs], r.h_gtok.at[theirs])
     take("rows")
-    for k in range(1, nz):
-        zz, _ = z_dev(k)
-        await_copy(r.vinz.at[zz], r.vzr.at[zz])
+    await_copy(r.vinz.at[pl.ds(0, nz - 1)], r.vr.at[1])
     total = r.vinz[0]
     for k in range(1, nz):
         total = total + r.vinz[k]
     r.vinb[b] = total
     for k in range(1, nb):
         dev = (lax.rem(b + k, nb), h, w)
-        sends.start(remote(r.vinb.at[b], r.vinb.at[b], r.vbs.at[k], r.vbr.at[b], dev))
+        sends.go(r.vinb.at[b], r.vinb.at[b], r.vr.at[2], dev)
     take("last")
-    for k in range(1, nb):
-        bb = lax.rem(b + k, nb)
-        await_copy(r.vinb.at[bb], r.vbr.at[bb])
+    await_copy(r.vinb.at[pl.ds(0, nb - 1)], r.vr.at[2])
     total = r.vinb[0]
     for k in range(1, nb):
         total = total + r.vinb[k]
     r.red_v[...] = jnp.where(w == 0, total[:, :cw], total[:, cw:])
+    write(2, r.red_v, r.h_red_v)
+    write(3, r.red_s.at[0, c], r.h_red_s.at[0, c])
     take("end")
+    write(3, r.red_s.at[1, c], r.h_red_s.at[1, c])
     await_copy(r.red_a.at[1 - bp], r.yr.at[3])
-
-    def sent(s, _):
-        row = sub_row(s, sub, dph)
-        here = (s == h) & (lax.div(row * tq, half) == w)
-
-        @pl.when(jnp.logical_not(here))
-        def _():
-            await_copy(r.osend.at[s], r.osd.at[s])
-
-        @pl.when(lax.rem(s, dph) == sub)
-        def _():
-            for k in range(1, dph):
-                await_copy(r.kvt.at[s], r.fs.at[s, k])
-
-        @pl.when(s != h)
-        def _():
-            await_copy(r.dqsend.at[s], r.dqs.at[s])
-
-        @pl.when((s != h) & (lax.rem(s, dph) == sub))
-        def _():
-            await_copy(r.dkvsend.at[s], r.dks.at[s])
-
-        @pl.when(lax.rem(s, dph) != sub)
-        def _():
-            await_copy(r.acc.at[s], r.pks.at[s])
-
-        return 0
-
-    lax.fori_loop(0, nh, sent, 0)
+    write(4, r.red_a, r.h_red_a)
+    for which in range(2):
+        await_copy(r.red_s.at[which, 1 - c], r.scr.at[which])
+        write(3, r.red_s.at[which, 1 - c], r.h_red_s.at[which, 1 - c])
+
+    own_blocks = nh // dph
+    loops = [(heads - 1) * nbytes(r.kvt.at[0]), (nh - 1) * nbytes(r.qt.at[0]), (dph - 1) * own_blocks * nbytes(r.kvt.at[0])]
+    sends.count(LOOPS, *loops, nbytes(r.acts), nbytes(r.gpres))
+    sends.count(BACK, (nh - 1) * nbytes(r.dqsend.at[0]), heads // 2 * nbytes(r.dqkv.at[0]))
+    sends.count(BACK, (own_blocks - 1) * nbytes(r.dkvsend.at[0]), (nh - own_blocks) * nbytes(r.acc.at[0]))
+    rowed = (nh + 2 * heads * per) * nbytes(r.osend.at[0])
+    local_row = lax.div(sub_row(h, sub, dph) * tq, half) == w
+
+    @pl.when(local_row)
+    def _():
+        sends.wait(ROWS, rowed - 2 * nbytes(r.osend.at[0]))
+
+    @pl.when(jnp.logical_not(local_row))
+    def _():
+        sends.wait(ROWS, rowed)
+
     weights_sent()
-    heads_sent()
-    for i2 in range(nz):
-        await_copy(r.acts.at[i2], r.as_.at[i2])
-        await_copy(r.gpres.at[i2], r.ps_.at[i2])
-    ffn_sent()
+    sums_sent()
     sends.finish()
-    square_end(0)
-    square_end(1)
+    for i, ref in enumerate((r.out_c, r.gtok, r.red_v, r.red_s, r.red_a)):
+        await_copy(ref, r.os.at[i])
 
 
 def final_kernel(heads, *refs):
@@ -1180,14 +1078,16 @@
         v3=ln2_gain[None], v4=ln2_bias[None], v5=gate2_bias[None], wq=w_query, wk=w_key, wv=w_value,
         wo=w_out, wg1=gate1_weight, wg2=gate2_weight, wu=w_up, wd=w_down,
     )
-    outs = dict(
+    results = dict(
         out_c=((rows, cw), BF16),
         gtok=((rows, cw), F32),
         red_a=((2, 2, quarter, units), BF16),
         red_s=((2, 2, 2, 3, HD, wide), BF16),
         red_v=((8, cw), F32),
     )
+    outs = {"h_" + name: spec for name, spec in results.items()}
     bufs = dict(
+        **results, tally=((8192, 128), F32), wqkv=((3, wide, cw), BF16),
         vsrc=((8, cw), F32), vecf=((8, wide), F32), tokf=((rows, wide), BF16), cotr=((half, wide), BF16),
         g1f=((2, wide, cw), BF16), g2f=((2, wide, cw), BF16), wof=((2, cw, wide), BF16),
         wup=((nz, 2, 2, cw, units), BF16), wdn=((nz, 2, 2, units, cw), BF16),
@@ -1197,7 +1097,7 @@
         qlow=((nh, 2 * HD, tq), BF16), dhigh=((nh, 2 * HD, tq), BF16), top=((nh, 1, tq), F32), total=((nh, 1, tq), F32),
         centre=((nh, 1, tq), F32), dqa=((nh, HD, tq), F32), ot=((nh, HD, tq), F32), lse=((nh, 1, tq), F32), osend=((nh, HD, tq), BF16),
         att=((2 * heads * HD, half), BF16),
-        pre=((nz, 2, half, units), F32), acts=((nz, half, units), BF16), actp=((nz, rows, units), BF16),
+        pre=((nz, 2, half, units), F32), actall=((half, nh * units), BF16), acts=((nz, half, units), BF16), actp=((nz, rows, units), BF16),
         gpres=((nz, half, units), BF16), gprep=((nz, rows, units), BF16),
         outr=((half, wide), BF16), gatt=((wide, half), BF16), dot=((nh, HD, tq), BF16),
         ginp=((half, wide), F32), gterm=((half, wide), F32), npt=((wide, rows), BF16), gbt=((wide, rows), BF16),
@@ -1209,7 +1109,7 @@
         zs=((nz, 2, quarter, units), BF16), zin=((nz, 2, quarter, units), BF16),
         pin=((pairs, 2, quarter, units), BF16),
         gc=((2, 3, HD, wide), BF16), ycin=((3, HD, wide), BF16), sq=((2, 3, HD, wide), BF16),
-        sqin=((1, 3, nz - 1, zr, 128), BF16), pzin=((2, 3, nz, zr, 128), BF16), sqpair=((2, 3, pairs, zr, 128), BF16),
+        pzin=((2, 3, nz, zr, 128), BF16), sqpair=((2, 3, pairs, zr, 128), BF16),
         acc=((nh, 2 * HD, rows), F32), pin_kv=((nh // dph, max(dph - 1, 1), 2 * HD, rows), F32),
         dkvsend=((nh, 2 * HD, rows), BF16), dqsend=((nh, HD, tq), BF16),
         dqkv=((heads, 3 * HD, rows), BF16), dsib=((heads // 2, 3 * HD, rows), BF16),
@@ -1218,25 +1118,20 @@
         vin4=((4, 8, wide), F32), vinz=((nz, 8, wide), F32), vinb=((nb, 8, wide), F32),
     )
     sems = dict(
-        xs=(10,), xr=(10,), wzs=(2, nz), wzr=(nz,), gxs=(3,), gxr=(3,), gcs=(3,), gcr=(3,),
-        ks=(heads, 2), kr=(nh, 2), qs=(heads, dph), qr=(nh,), cs=(12,), cr=(12,),
-        wxs=(nz,), wxr=(nz,), wys=(nz, 2), wyr=(nz, 2), wcs=(2,), wcr=(2,),
-        fs=(nh, dph), fr=(nh,), osd=(nh,), orc=(2 * heads, per),
-        as_=(nz,), ar=(nz,), ps_=(nz,), pr=(nz,), ds=(2, heads, per), dr=(nh,),
-        ys=(5,), yr=(5,), zss=(nz,), zsr=(nz,), pas=(pairs,), par=(pairs,),
-        sqs=(1, 3, nz), sqr=(1, 3, nz), sqps=(2, 3, pairs), sqpr=(2, 3, pairs), sgs=(1, 3, nz), sgr=(1, 3, nz),
-        pys=(3,), pyr=(3,), pzs=(2, 3, nz), pzr=(2, 3, nz), pgs=(2, 3, nz), pgr=(2, 3, nz),
-        sxs=(3,), sxr=(3,), sys=(3,), syr=(3,), sbs=(2, 3), sbr=(2, 3), scs=(2, 3), scr=(2, 3),
-        pks=(nh,), pkr=(nh // dph, max(dph - 1, 1)), dqs=(nh,), dqr=(heads, dph), dks=(nh,), dkr=(heads,),
-        ts=(heads,), tr=(heads // 2,), v4s=(3,), v4r=(4,), vzs=(nz,), vzr=(nz,), vbs=(nb,), vbr=(nb,),
+        ls=(6,), os=(5,), snd=(8,), xr=(10,), wzs=(2, nz), wzr=(nz,), gxr=(1,), gcr=(1,), kr=(nh,), qr=(nh,), cr=(3,),
+        wxr=(nz,), wyr=(1,), wcr=(2,), fr=(nh,), orc=(1,), ar=(1,), pr=(1,), dr=(2,), yr=(4,), zsr=(nz,), par=(pairs,),
+        sqpr=(2, 3, pairs) if pairs > 1 else (1,), pyr=(3,), pzr=(2, 3), pgr=(2, 3), sxr=(1,), syr=(1,), sbr=(2, 3),
+        scr=(2,), pkr=(nh // dph, max(dph - 1, 1)), dkr=(heads,), tr=(1,), vr=(3,),
     )
     names = list(ins) + list(outs) + list(bufs) + list(sems)
     vmem = pl.BlockSpec(memory_space=pltpu.VMEM)
-    results = pl.pallas_call(
+    any_space = pl.BlockSpec(memory_space=pl.ANY)
+    in_specs = [vmem if name[0] == "v" else any_space for name in list(ins)[1:]]
+    sums = pl.pallas_call(
         functools.partial(layer_kernel, names, sizes),
         out_shape=[jax.ShapeDtypeStruct(shape, kind) for shape, kind in outs.values()],
-        in_specs=[pl.BlockSpec(memory_space=pltpu.SMEM)] + [vmem] * (len(ins) - 1),
-        out_specs=[vmem] * len(outs),
+        in_specs=[pl.BlockSpec(memory_space=pltpu.SMEM)] + in_specs,
+        out_specs=[any_space] * len(outs),
         scratch_shapes=[pltpu.VMEM(shape, kind) for shape, kind in bufs.values()]
         + [pltpu.SemaphoreType.DMA(shape) for shape in sems.values()],
         compiler_params=pltpu.CompilerParams(
@@ -1256,7 +1151,7 @@
         in_specs=[vmem] * len(outs),
         out_specs=[vmem] * len(grads),
         compiler_params=pltpu.CompilerParams(vmem_limit_bytes=VMEM_LIMIT),
-    )(*results)
+    )(*sums)
     return tuple(a[0] if a.shape[0] == 1 else a for a in done)
 
 

time: 137 us -> 131 us (0.956)
  Pallas kernels: 136 us -> 129 us
    pallas_call x1, Pallas kernels: 132 us -> 125 us  [local(): pl.pallas_call(functools.partial(layer_kernel, names, sizes), out_shape=[...]
where the time goes in v6:
time: 131 us; the launch traced here: 130 us
  Pallas kernels  129 us (98%)
    pallas_call x1, Pallas kernels, local(): pl.pallas_call(functools.partial(layer_kernel, names, sizes), out_shape=[...  125 us
    pallas_call x1, Pallas kernels, local(): pl.pallas_call(functools.partial(final_kernel, heads), out_shape=[jax.Sha...  4.16 us

profile of v6, /device:TPU:0, one launch (start us, length us, event | category | flops | bytes accessed | tf_op | source)
XLA Modules:
  0.0 130.2 jit_solution(14481520339253024477)
XLA Ops:
  0.7 125.3 %shard_map.288 = (bf16[512,256]{1,0:T(8,128)(2,1)}, f32[512,256]{1,0:T(8,128)}, bf16[2,2,128,256]{3,2,1,0:T(8,128)(2,1)}, bf16[2,2,2,3,64,512]{5,4,3,2,1,0:T(8,128)(2,1)}, f32[8,256]{1,0:T(8,128)}) custom-call(s32[1,3]{1,0:T(1,128)} %refs_0_.1, bf16[512,256]{1,0:T(8,128)(2,1)} %refs_1_.1, bf16[512,256]{1,0:T(8,128)(2,1)} %refs_2_.1, f32[1,256]{1,0:T(1,128)} %bitcast.12, ...), custom_call_target="tpu_custom_call" | custom-call | flops 10000000000 | bytes 10000000 | tf_op jit(solution)/shard_map/pallas_call | solution.py:1130
  125.9 4.2 %shard_map.289 = (bf16[512,256]{1,0:T(8,128)(2,1)}, f32[512,256]{1,0:T(8,128)}, f32[1,256]{1,0:T(1,128)}, f32[1,256]{1,0:T(1,128)}, f32[512,256]{1,0:T(8,128)}, ...) custom-call(bf16[512,256]{1,0:T(8,128)(2,1)} %get-tuple-element.37.r, ...), custom_call_target="tpu_custom_call" | custom-call | tf_op jit(solution)/shard_map/pallas_call | solution.py:1148

commit v7 on v6

--- a/solution.py
+++ b/solution.py
@@ -18,8 +18,8 @@
 VMEM_LIMIT = 62 * 1024 * 1024
 PLAN = {
     "begin": ("a1",), "row0": (), "col0": ("bx",), "row1": (), "col1": ("bz",), "row2": ("a2",), "col2": (),
-    "loop": ("a3", "bg"), "whole": (), "sent": (), "proj": ("cy", "a4"), "half": ("cz",),
-    "norm": ("bb",), "vec": ("cg", "a5"), "rows": (), "last": ("bc", "cb"), "end": ("cc",),
+    "loop": ("a3",), "whole": (), "sent": ("bg",), "proj": ("cy", "a4"), "half": ("cz",),
+    "norm": ("bb",), "vec": ("cg",), "rows": ("a5",), "last": ("bc", "cb"), "end": ("cc",),
 }
 SCALE = HD**-0.5
 
@@ -437,6 +437,8 @@
 
         @pl.when(d == 2)
         def _():
+            for k in range(2):
+                send_heads(1, k)
             for distance in range(2):
                 weight_cross(distance)
 
@@ -454,8 +456,6 @@
     r.ot[...] = jnp.zeros_like(r.ot)
     stage_passes(0)
     stage_computes(0)
-    for k in range(2):
-        send_heads(2, k)
     await_copy(r.wqkv, r.ls.at[4])
     for src, dst in gates:
         block = dst.at[w, at(c, src.shape[0] // 2)]
@@ -464,10 +464,10 @@
     stage_passes(1)
     for k in range(3, nz):
         weight_hop(k)
+    for k in range(2):
+        send_heads(2, k)
     for k in range(3, nz):
         weight_hop(k, ending=True)
-    for k in range(2):
-        send_heads(1, k)
     stage_computes(1)
     await_copy(r.cotr.at[:, own], r.ls.at[5])
     sends.go(r.cot.at[theirs], r.cotr.at[:, own], r.xr.at[3], x_dev)

time: 131 us -> 127 us (0.969)
  Pallas kernels: 129 us -> 126 us
    pallas_call x1, Pallas kernels: 125 us -> 122 us  [local(): pl.pallas_call(functools.partial(layer_kernel, names, sizes), out_shape=[...]
where the time goes in v7:
time: 127 us
  Pallas kernels  126 us (99%)
    pallas_call x1, Pallas kernels, local(): pl.pallas_call(functools.partial(layer_kernel, names, sizes), out_shape=[...  122 us
    pallas_call x1, Pallas kernels, local(): pl.pallas_call(functools.partial(final_kernel, heads), out_shape=[jax.Sha...  4.16 us

profile of v7, /device:TPU:0, one launch (start us, length us, event | category | flops | bytes accessed | tf_op | source)
XLA Modules:
  0.0 126.8 jit_solution(18073365186541716039)
XLA Ops:
  0.7 121.8 %shard_map.288 = (bf16[512,256]{1,0:T(8,128)(2,1)}, f32[512,256]{1,0:T(8,128)}, bf16[2,2,128,256]{3,2,1,0:T(8,128)(2,1)}, bf16[2,2,2,3,64,512]{5,4,3,2,1,0:T(8,128)(2,1)}, f32[8,256]{1,0:T(8,128)}) custom-call(s32[1,3]{1,0:T(1,128)} %refs_0_.1, bf16[512,256]{1,0:T(8,128)(2,1)} %refs_1_.1, bf16[512,256]{1,0:T(8,128)(2,1)} %refs_2_.1, f32[1,256]{1,0:T(1,128)} %bitcast.12, ...), custom_call_target="tpu_custom_call" | custom-call | flops 10000000000 | bytes 10000000 | tf_op jit(solution)/shard_map/pallas_call | solution.py:1130
  122.5 4.2 %shard_map.289 = (bf16[512,256]{1,0:T(8,128)(2,1)}, f32[512,256]{1,0:T(8,128)}, f32[1,256]{1,0:T(1,128)}, f32[1,256]{1,0:T(1,128)}, f32[512,256]{1,0:T(8,128)}, ...) custom-call(bf16[512,256]{1,0:T(8,128)(2,1)} %get-tuple-element.37.r, ...), custom_call_target="tpu_custom_call" | custom-call | tf_op jit(solution)/shard_map/pallas_call | solution.py:1148

commit v8 on v7

--- a/solution.py
+++ b/solution.py
@@ -328,7 +328,7 @@
 
     def masked(scores, i, j):
         query_base = i * rows + sub_row(i, sub, dph) * tq
-        return jnp.where(allowed_mask(j * rows, query_base, rows, tq, ends), scores, NEG)
+        return jnp.where(allowed_mask(j * rows, query_base, scores.shape[0], tq, ends), scores, NEG)
 
     def bias(scores, j):
         key_pos = j * rows + lax.broadcasted_iota(jnp.int32, (rows, 1), 0)
@@ -344,7 +344,7 @@
         for scores, j in blocks:
             weights = jnp.exp(scores - new_top)
             total = total + jnp.sum(weights, 0, keepdims=True)
-            mixed = mixed + nn(r.kvt[j, HD:, :], weights.astype(BF16))
+            mixed = mixed + nn(r.kvt[j, HD:, : weights.shape[0]], weights.astype(BF16))
         r.top[i], r.total[i], r.ot[i] = new_top, total, mixed
 
     def send_attended(s):
@@ -368,13 +368,26 @@
         def _():
             remote(r.osend.at[s], dst, sends.sem(ROWS), slot, (b, s, row_w)).start()
 
+    def short(i):
+        return (sub_row(i, sub, dph) + 1) * tq <= half
+
     def own_chip(n):
         i = 2 * n
-        first = masked(nn(r.kvn[i], r.qlow[i]), i, i)
-        low = masked(nn(r.kvn[i], r.qlow[i + 1]), i + 1, i)
-        high = masked(nn(r.kvn[i + 1], r.qlow[i + 1]), i + 1, i + 1)
-        absorb(i, [(first, i)])
-        absorb(i + 1, [(low, i), (high, i + 1)])
+
+        def with_keys(first_keys, second_keys):
+            first = masked(nn(r.kvn[i, :first_keys], r.qlow[i]), i, i)
+            low = masked(nn(r.kvn[i], r.qlow[i + 1]), i + 1, i)
+            high = masked(nn(r.kvn[i + 1, :second_keys], r.qlow[i + 1]), i + 1, i + 1)
+            absorb(i, [(first, i)])
+            absorb(i + 1, [(low, i), (high, i + 1)])
+
+        @pl.when(short(i))
+        def _():
+            with_keys(half, rows)
+
+        @pl.when(jnp.logical_not(short(i)))
+        def _():
+            with_keys(rows, half)
 
     def two_chips(hi, lo, last):
         queries, keys = (2 * hi, 2 * hi + 1), (2 * lo, 2 * lo + 1)
@@ -442,9 +455,12 @@
             for distance in range(2):
                 weight_cross(distance)
 
+        @pl.when(d == nz // 2)
+        def _():
+            weight_hop(nz, ending=True)
+
         @pl.when(d == nz - 1)
         def _():
-            weight_hop(nz, ending=True)
             for distance in range(2, nz - 1):
                 weight_cross(distance)
 
@@ -797,15 +813,16 @@
                 remote(r.dkvsend.at[s], dst, sends.sem(BACK), r.dkr.at[group], (b, s, w)).start()
 
     def pairs_backward(where, full):
-        scores = [nn(r.kvn[j], r.qlow[i]) for i, j in where]
-        gprobs = [nn(r.kvn[j], r.dhigh[i]) for i, j in where]
-        for x, gp, (i, j), whole in zip(scores, gprobs, where, full):
+        spans = [slice(0, half if whole == "half" else rows) for whole in full]
+        scores = [nn(r.kvn[j, span], r.qlow[i]) for (i, j), span in zip(where, spans)]
+        gprobs = [nn(r.kvn[j, span], r.dhigh[i]) for (i, j), span in zip(where, spans)]
+        for x, gp, (i, j), whole, span in zip(scores, gprobs, where, full, spans):
             x = masked(x, i, j) if whole else bias(x, j)
             probs = jnp.exp(x - r.lse[i])
             gscores = (probs * (gp - r.centre[i])).astype(BF16)
-            r.acc[j, HD:, :] += nt(r.dhigh[i, HD:, :], probs.astype(BF16))
-            r.acc[j, :HD, :] += nt(r.qt[i], gscores)
-            r.dqa[i] += nn(r.kvt[j, :HD, :], gscores)
+            r.acc[j, HD:, span] += nt(r.dhigh[i, HD:, :], probs.astype(BF16))
+            r.acc[j, :HD, span] += nt(r.qt[i], gscores)
+            r.dqa[i] += nn(r.kvt[j, :HD, span], gscores)
 
     def choose(kinds, where):
         taken = False
@@ -858,7 +875,8 @@
 
         def row_step(v, _):
             where = [pair_at(t, 2 * v), pair_at(t, 2 * v + 1)]
-            choose([(t == 0, (True, True)), (v == rowed - 1, (False, True)), (True, (False, False))], where)
+            kinds = [(t == 0, (True, True)), ((v == rowed - 1) & short(hi), (False, "half"))]
+            choose(kinds + [(v == rowed - 1, (False, True)), (True, (False, False))], where)
 
             @pl.when((t > 0) & (v == jnp.minimum(1, rowed - 1)))
             def _():
@@ -883,7 +901,8 @@
 
         def column_step(v, _):
             where = [pair_at(t, n + 2 * v), pair_at(t, n + 2 * v + 1)]
-            choose([(v == 0, (True, False)), (True, (False, False))], where)
+            kinds = [((v == 0) & short(lo), ("half", False)), (v == 0, (True, False))]
+            choose(kinds + [(True, (False, False))], where)
 
             @pl.when(v == jnp.minimum(1, columned - 1))
             def _():

time: 127 us -> 127 us (level)
  no operation moved by 1% of the time
where the time goes in v8:
time: 127 us
  Pallas kernels  126 us (99%)
    pallas_call x1, Pallas kernels, local(): pl.pallas_call(functools.partial(layer_kernel, names, sizes), out_shape=[...  122 us
    pallas_call x1, Pallas kernels, local(): pl.pallas_call(functools.partial(final_kernel, heads), out_shape=[jax.Sha...  4.16 us

profile of v8, /device:TPU:0, one launch (start us, length us, event | category | flops | bytes accessed | tf_op | source)
XLA Modules:
  0.0 126.6 jit_solution(18099299460484964578)
XLA Ops:
  0.7 121.7 %shard_map.288 = (bf16[512,256]{1,0:T(8,128)(2,1)}, f32[512,256]{1,0:T(8,128)}, bf16[2,2,128,256]{3,2,1,0:T(8,128)(2,1)}, bf16[2,2,2,3,64,512]{5,4,3,2,1,0:T(8,128)(2,1)}, f32[8,256]{1,0:T(8,128)}) custom-call(s32[1,3]{1,0:T(1,128)} %refs_0_.1, bf16[512,256]{1,0:T(8,128)(2,1)} %refs_1_.1, bf16[512,256]{1,0:T(8,128)(2,1)} %refs_2_.1, f32[1,256]{1,0:T(1,128)} %bitcast.12, ...), custom_call_target="tpu_custom_call" | custom-call | flops 10000000000 | bytes 10000000 | tf_op jit(solution)/shard_map/pallas_call | solution.py:1149
  122.4 4.2 %shard_map.289 = (bf16[512,256]{1,0:T(8,128)(2,1)}, f32[512,256]{1,0:T(8,128)}, f32[1,256]{1,0:T(1,128)}, f32[1,256]{1,0:T(1,128)}, f32[512,256]{1,0:T(8,128)}, ...) custom-call(bf16[512,256]{1,0:T(8,128)(2,1)} %get-tuple-element.37.r, ...), custom_call_target="tpu_custom_call" | custom-call | tf_op jit(solution)/shard_map/pallas_call | solution.py:1167
